TPU v7x, 32 devices: a whole 2x2x4 slice. The times are simulated.
32 devices in a mesh: groups: 2 (over x), wide: 16 (over z, y, core).
Axes of the slice: x: 2, y: 2, z: 4, core: 2. Of those that a mesh axis runs over, the one named last changes fastest.
Arguments:
- tokens: bfloat16 [32, 16384], P('groups', 'wide'), parts along dimension 0, may hold values from -6 to 6
- norm_gain: bfloat16 [16384], P('wide'), may hold values from 0.099609375 to 1.8984375
- slot_of_row: int32 [32], P('groups'), parts along dimension 0, may hold values from 0 to 15, each once
- lengths: int32 [32], P('groups'), parts along dimension 0, may hold values from 512 to 4096, as said below
- w_query: bfloat16 [16384, 8192], P(None, 'wide'), may hold values from -1 to 1
- key_projection: bfloat16 [16384, 512], P('wide'), may hold values from -1 to 1
- value_projection: bfloat16 [16384, 512], P('wide'), may hold values from -0.046875 to 0.046875
- output_projection: bfloat16 [8192, 16384], P(None, 'wide'), may hold values from -0.25 to 0.25
- slot_key_cache: bfloat16 [128, 4096, 128], P(('groups', 'wide')), parts along dimension 0, may hold values from -1000 to 1000
- slot_value_cache: bfloat16 [128, 4096, 128], P(('groups', 'wide')), parts along dimension 0, may hold values from -12 to 12
Outputs:
- attn_out: bfloat16 [32, 16384], P('groups', 'wide'), parts along dimension 0
There are 2 independent parts, one for each index of `groups`. A program takes and returns all parts, laid end to end along the dimension named above; an argument that names none is the same for every part. Nothing has to cross between parts.
Inputs may be any that keep to these rules, and one draw needn't show every extreme that they name: `lengths`: at least 512, and 4096 for at least one slot.
All inputs are finite; a program needn't handle non-finite values.
Results may differ from a plain program's by a relative error of at most 0.01.
Values may be sent and summed in bfloat16 or wider, within the bound.
No kernel may reach another device: no remote copies, remote signals or barrier semaphores. Data moves between devices by JAX's collectives and lax.ppermute only.
A program may use at most 128 MiB of HBM per device.

v0:
```python
import math

import jax
import jax.numpy as jnp
from jax import lax
from jax.sharding import PartitionSpec as P

QUERY_HEADS = 64
KEY_VALUE_HEADS = 4
HEAD_SIZE = 128


EPS = 1e-05
ROPE_BASE = 500000.0


def rotate(mat, positions, start):
    rows, cols = mat.shape
    index = (start + jnp.arange(cols, dtype=jnp.int32)) % HEAD_SIZE
    rate = ROPE_BASE ** (-(index - index % 2).astype(jnp.float32) / HEAD_SIZE)
    angle = positions.astype(jnp.float32)[:, None] * rate[None, :]
    paired = mat.reshape(rows, cols // 2, 2)
    swapped = jnp.stack([-paired[..., 1], paired[..., 0]], axis=-1).reshape(rows, cols)
    return mat * jnp.cos(angle) + swapped * jnp.sin(angle)


def pick_head(matrix, chosen_head):
    return jnp.sum(jnp.where(chosen_head[:, :, None], matrix, 0.0), axis=1)


def body(
    tokens,
    norm_gain,
    slot_of_row,
    lengths,
    w_query,
    key_projection,
    value_projection,
    output_projection,
    slot_key_cache,
    slot_value_cache,
):
    place = lax.axis_index("wide")
    query_group = QUERY_HEADS // KEY_VALUE_HEADS
    score_scale = 1.0 / math.sqrt(HEAD_SIZE)
    whole, gain_all = (
        lax.all_gather(tokens, "wide", axis=1, tiled=True),
        lax.all_gather(norm_gain, "wide", axis=0, tiled=True),
    )
    wide_f = whole.astype(jnp.float32)
    normed = (
        wide_f
        * lax.rsqrt(jnp.mean(wide_f * wide_f, axis=1, keepdims=True) + EPS)
        * gain_all.astype(jnp.float32)
    ).astype(jnp.bfloat16)
    rows = whole.shape[0]
    slot_ids = jnp.arange(rows, dtype=jnp.int32)
    row_to_slot = slot_of_row[:, None] == slot_ids[None, :]
    positions = jnp.sum(jnp.where(row_to_slot, lengths[None, :], 0), axis=1)
    q_cols = w_query.shape[1]
    query_vector = rotate(
        jnp.dot(normed, w_query, preferred_element_type=jnp.float32), positions, place * q_cols
    ).astype(jnp.bfloat16)
    feat_rows = key_projection.shape[0]
    normed_local = lax.dynamic_slice_in_dim(normed, place * feat_rows, feat_rows, 1)
    key_share = jnp.dot(normed_local, key_projection, preferred_element_type=jnp.float32)
    value_share = jnp.dot(normed_local, value_projection, preferred_element_type=jnp.float32)
    key_total, value_total = lax.psum((key_share, value_share), "wide")
    fresh_key = rotate(key_total, positions, 0).astype(jnp.bfloat16)
    fresh_value = value_total.astype(jnp.bfloat16)
    head_pairs = slot_key_cache.shape[0]
    pair_ids = place * head_pairs + jnp.arange(head_pairs, dtype=jnp.int32)
    partner_head = pair_ids // rows
    pair_slot = pair_ids % rows
    chosen_slot = (pair_slot[:, None] == slot_of_row[None, :]).astype(jnp.bfloat16)
    chosen_head = partner_head[:, None] == jnp.arange(KEY_VALUE_HEADS, dtype=jnp.int32)[None, :]
    pair_key = pick_head(
        jnp.dot(chosen_slot, fresh_key, preferred_element_type=jnp.float32).reshape(
            head_pairs, KEY_VALUE_HEADS, HEAD_SIZE
        ),
        chosen_head,
    ).astype(jnp.bfloat16)
    pair_value = pick_head(
        jnp.dot(chosen_slot, fresh_value, preferred_element_type=jnp.float32).reshape(
            head_pairs, KEY_VALUE_HEADS, HEAD_SIZE
        ),
        chosen_head,
    ).astype(jnp.bfloat16)
    everything = lax.all_gather(query_vector, "wide", axis=1, tiled=True)
    selected = jnp.dot(chosen_slot, everything, preferred_element_type=jnp.float32).reshape(
        head_pairs, query_group, KEY_VALUE_HEADS, HEAD_SIZE
    )
    pair_query = jnp.sum(jnp.where(chosen_head[:, None, :, None], selected, 0.0), axis=2).astype(
        jnp.bfloat16
    )
    logit_scores = (
        jnp.einsum("pgd,pld->pgl", pair_query, slot_key_cache, preferred_element_type=jnp.float32)
        * score_scale
    )
    pair_len = jnp.sum(
        jnp.where(pair_slot[:, None] == slot_ids[None, :], lengths[None, :], 0), axis=1
    )
    valid = (
        jnp.arange(slot_key_cache.shape[1], dtype=jnp.int32)[None, None, :]
        < pair_len[:, None, None]
    )
    own = (
        jnp.sum(pair_query.astype(jnp.float32) * pair_key.astype(jnp.float32)[:, None, :], axis=-1)
        * score_scale
    )
    top = jnp.maximum(jnp.max(jnp.where(valid, logit_scores, -jnp.inf), axis=-1), own)
    weights = jnp.where(valid, jnp.exp(logit_scores - top[..., None]), 0.0)
    own_w = jnp.exp(own - top)
    denom = jnp.sum(weights, axis=-1) + own_w
    attention_probability = (weights / denom[..., None]).astype(jnp.bfloat16)
    own_p = (own_w / denom).astype(jnp.bfloat16)
    blended_values = jnp.einsum(
        "pgl,pld->pgd", attention_probability, slot_value_cache, preferred_element_type=jnp.float32
    )
    blended_values = (
        blended_values
        + own_p.astype(jnp.float32)[..., None] * pair_value.astype(jnp.float32)[:, None, :]
    )
    attended = blended_values.astype(jnp.bfloat16)
    output_columns = output_projection.shape[1]
    weight_per_head = (
        output_projection.reshape(query_group, KEY_VALUE_HEADS, HEAD_SIZE, output_columns)
        .transpose(1, 0, 2, 3)
        .reshape(KEY_VALUE_HEADS, query_group * HEAD_SIZE, output_columns)
    )
    head_numbers = jnp.arange(KEY_VALUE_HEADS, dtype=jnp.int32)
    piece = lax.all_gather(
        attended.reshape(head_pairs, query_group * HEAD_SIZE), "wide", axis=0, tiled=True
    )
    count = piece.shape[0]
    piece_ids = jnp.arange(count, dtype=jnp.int32)
    piece_head = piece_ids // rows
    piece_slot = piece_ids % rows
    per_head = jnp.einsum("ck,hko->cho", piece, weight_per_head, preferred_element_type=jnp.float32)
    chosen = pick_head(per_head, piece_head[:, None] == head_numbers[None, :])
    placing = (slot_of_row[:, None] == piece_slot[None, :]).astype(jnp.float32)
    summed = jnp.dot(
        placing, chosen, precision=lax.Precision.HIGHEST, preferred_element_type=jnp.float32
    )
    return summed.astype(jnp.bfloat16)


def solution(mesh):
    placed = (
        P("groups", "wide"),
        P("wide"),
        P("groups"),
        P("groups"),
        P(None, "wide"),
        P("wide", None),
        P("wide", None),
        P(None, "wide"),
        P(("groups", "wide"), None, None),
        P(("groups", "wide"), None, None),
    )
    return jax.shard_map(
        body, mesh=mesh, in_specs=placed, out_specs=P("groups", "wide"), check_vma=False
    )
```

profile of v0, /device:TPU:0, one launch (start us, length us, event | category | flops | bytes accessed | tf_op | source)
XLA Modules:
  0.0 174.6 jit_solution(5362743915272927086)
XLA Ops:
  0.0 0.0 copy-start
  0.0 0.0 copy-start.1
  0.0 24.9 %all_gather.12 = bf16[16,16384]{1,0:T(8,128)(2,1)S(1)} all-gather(bf16[16,1024]{1,0:T(8,128)(2,1)} %param.10), channel_id=1, replica_groups=mesh['groups'=2,'wide'=16] {'wide'}, dimensions={1}, use_global_device_ids=true | all-gather | bytes 557056 | tf_op jit(solution)/shard_map/all_gather | solution.py:47
  24.9 0.2 fusion.2
  25.2 0.0 copy-start.2
  25.2 17.8 %all_gather.13 = bf16[16384]{0:T(1024)(128)(2,1)S(1)} all-gather(bf16[1024]{0:T(1024)(128)(2,1)} %param.11), channel_id=1, replica_groups=mesh['groups'=2,'wide'=16] {'wide'}, dimensions={0}, use_global_device_ids=true | all-gather | bytes 34816 | tf_op jit(solution)/shard_map/all_gather | solution.py:48
  43.0 0.2 fusion.4
  43.1 0.0 copy-done
  43.2 0.2 fusion.18
  43.4 1.5 fusion.20
  44.9 59.2 %all-reduce = (bf16[16,512]{1,0:T(8,128)(2,1)S(1)}, f32[16,512]{1,0:T(8,128)S(1)}) all-reduce(f32[16,512]{1,0:T(8,128)S(1)} %fusion.18, f32[16,512]{1,0:T(8,128)S(1)} %fusion.20), channel_id=1, replica_groups=mesh['groups'=2,'wide'=16] {'wide'}, use_global_device_ids=true, to_apply=%region_9.10 | all-reduce | flops 16384 | bytes 114688 | tf_op jit(solution)/shard_map/psum | solution.py:68
  104.1 0.1 copy.33
  104.2 0.2 slice_negate_fusion
  104.4 0.3 pad_maximum_fusion.1
  104.7 0.1 copy.34
  104.8 0.9 select_reduce_fusion.4
  105.7 1.0 fusion.24
  106.7 0.8 fusion.22
  107.5 0.1 iota_compare_fusion.2
  107.6 0.1 select_reduce_fusion.2
  107.7 8.0 %fusion.61 = f32[16,512]{1,0:T(8,128)S(1)} fusion(bf16[16,16384]{1,0:T(8,128)(2,1)S(1)} %fusion.4, bf16[16384,512]{1,0:T(8,128)(2,1)} %param.14), kind=kOutput, calls=%fused_computation.116 | convolution fusion | flops 268435456 | bytes 17334272 | tf_op jit(solution)/shard_map/dot_general | solution.py:62
  115.7 0.1 copy.31
  115.9 0.2 slice_negate_fusion.1
  116.1 0.3 pad_maximum_fusion
  116.4 0.1 copy.32
  116.5 0.2 fusion.12
  116.8 17.8 %all_gather.14 = bf16[16,8192]{1,0:T(8,128)(2,1)S(1)} all-gather(bf16[16,512]{1,0:T(8,128)(2,1)S(1)} %fusion.12), channel_id=1, replica_groups=mesh['groups'=2,'wide'=16] {'wide'}, dimensions={1}, use_global_device_ids=true | all-gather | bytes 278528 | tf_op jit(solution)/shard_map/all_gather | solution.py:89
  134.6 0.0 copy-done.1
  134.6 0.2 fusion.32
  134.8 0.1 reshape.270
  135.0 0.2 select_reduce_fusion.1
  135.1 0.1 multiply_reduce_fusion
  135.2 0.0 copy-done.2
  135.2 0.2 select_reduce_fusion.5
  135.4 0.1 iota_compare_fusion
  135.5 3.5 %select_reduce_fusion = (f32[4,16]{1,0:T(4,128)S(1)}, f32[4,16,4096]{2,1,0:T(8,128)S(1)}) fusion(pred[4,4096]{1,0:T(4,128)(4,1)S(1)} %iota_compare_fusion, bf16[4,16,128]{2,1,0:T(8,128)(2,1)S(1)} %select_reduce_fusion.1, bf16[4,4096,128]{2,1,0:T(8,128)(2,1)} %param.18), kind=kOutput, calls=%fused_computation.13 | convolution fusion | flops 67895232 | bytes 5275904 | tf_op jit(solution)/shard_map/pgd,pld->pgl/dot_general | solution.py:97
  139.0 0.4 fusion.5
  139.4 3.0 %fusion.1 = bf16[4,16,128]{2,1,0:T(8,128)(2,1)S(1)} fusion(bf16[4,4096,128]{2,1,0:T(8,128)(2,1)} %param.19, f32[4,16,4096]{2,1,0:T(8,128)S(1)} %get-tuple-element.16, f32[4,16]{1,0:T(4,128)S(1)} %get-tuple-element.14, f32[4,16]{1,0:T(4,128)S(1)} %multiply_maximum_fusion, pred[4,4096]{1,0:T(4,128)(4,1)S(1)} %iota_compare_fusion, ...), kind=kOutput, calls=%fused_computation.7 | convolution fusion | flops 68182016 | bytes 5278464 | tf_op jit(solution)/shard_map/pgl,pld->pgd/dot_general | solution.py:117
  142.4 19.9 %all-gather = bf16[16,4,2048]{2,1,0:T(4,128)(2,1)S(1)} all-gather(bf16[1,4,2048]{2,1,0:T(4,128)(2,1)S(1)} %reshape.278), channel_id=1, replica_groups=mesh['groups'=2,'wide'=16] {'wide'}, dimensions={0}, use_global_device_ids=true | all-gather | bytes 278528 | tf_op jit(solution)/shard_map/all_gather | solution.py:132
  162.3 0.1 reshape.281
  162.4 8.2 %copy.35 = bf16[4,16,128,1024]{3,2,1,0:T(8,128)(2,1)S(1)} copy(bf16[4,16,128,1024]{3,2,0,1:T(8,128)(2,1)} %bitcast.21) | data formatting | bytes 33554432 | tf_op jit(solution)/shard_map/transpose | solution.py:128
  170.6 3.1 %fusion = f32[64,1024]{1,0:T(8,128)S(1)} fusion(bf16[64,2048,1]{1,0,2:T(8,128)(2,1)S(1)} %reshape.281, bf16[4,2048,1024]{2,1,0:T(8,128)(2,1)S(1)} %bitcast.20, pred[64,4]{0,1:T(4,128)(4,1)S(1)} %iota_compare_fusion.4), kind=kOutput, calls=%fused_computation.4 | convolution fusion | flops 1074200576 | bytes 17301760 | tf_op jit(solution)/shard_map/ck,hko->cho/dot_general | solution.py:139
  173.8 0.9 convolution_convert_fusion
  (16 shorter events, 0.2 us)
Async XLA Ops:
  0.0 43.2 %copy-start = (bf16[1024,512]{1,0:T(8,128)(2,1)S(1)}, bf16[1024,512]{1,0:T(8,128)(2,1)}, u32[]{:S(2)}) copy-start(bf16[1024,512]{1,0:T(8,128)(2,1)} %param.16) | copy-start | bytes 3145732
  0.0 134.6 %copy-start.1 = (s32[16]{0:T(128)S(1)}, s32[16]{0:T(128)}, u32[]{:S(2)}) copy-start(s32[16]{0:T(128)} %param.12) | copy-start | bytes 196
  25.2 110.1 %copy-start.2 = (s32[16]{0:T(128)S(1)}, s32[16]{0:T(128)}, u32[]{:S(2)}) copy-start(s32[16]{0:T(128)} %param.13) | copy-start | bytes 196
where the time goes:
time: 175 us
  blocking collectives  140 us (80%)
  matrix products  22.2 us (13%)
  local copies, waits for them, and re-layouts  8.89 us (5%)
  other arithmetic  3.7 us (2%)
    psum x1, blocking collectives, body(): key_total, value_total = lax.psum((key_share, value_share), 'wide')  59.2 us
    all_gather x1, blocking collectives, body(): lax.all_gather(tokens, 'wide', axis=1, tiled=True)  24.9 us
    all_gather x1, blocking collectives, body(): lax.all_gather(attended.reshape(head_pairs, query_group * HEAD_SIZE), 'wi...  19.9 us
    all_gather x1, blocking collectives, body(): everything = lax.all_gather(query_vector, 'wide', axis=1, tiled=True)  17.8 us
    all_gather x1, blocking collectives, body(): lax.all_gather(norm_gain, 'wide', axis=0, tiled=True)  17.8 us
    transpose x1, local copies, waits for them, and re-layouts, body(): weight_per_head = output_projection.reshape(query_group, KEY_VALUE_HEADS,...  8.19 us
    dot_general x1, matrix products, body(): jnp.dot(normed, w_query, preferred_element_type=jnp.float32)  8.03 us

commit v1 on v0

v1 whole, which is shorter than its diff:
```python
import functools
import math

import jax
import jax.numpy as jnp
from jax import lax
from jax.experimental import pallas as pl
from jax.experimental.pallas import tpu as pltpu
from jax.sharding import PartitionSpec as P

QUERY_HEADS = 64
KEY_VALUE_HEADS = 4
HEAD_SIZE = 128
QUERY_GROUP = QUERY_HEADS // KEY_VALUE_HEADS

EPS = 1e-05
ROPE_BASE = 500000.0
MIB = 1 << 20
F32 = jnp.float32
BF16 = jnp.bfloat16


def call(kernel, out_shape, args, near=(), smem=(), scratch=(), limit=4 * MIB, flops=0, read=0):
    operands, specs = [], []
    for i, arg in enumerate(args):
        if i in near:
            arg = pltpu.with_memory_space_constraint(arg, pltpu.VMEM)
        operands.append(arg)
        specs.append(pl.BlockSpec(memory_space=pltpu.SMEM if i in smem else pltpu.VMEM))
    return pl.pallas_call(
        kernel,
        out_shape=out_shape,
        in_specs=specs,
        out_specs=jax.tree.map(lambda _: pl.BlockSpec(memory_space=pltpu.VMEM), out_shape),
        scratch_shapes=list(scratch),
        compiler_params=pltpu.CompilerParams(vmem_limit_bytes=limit),
        cost_estimate=pl.CostEstimate(flops=flops, bytes_accessed=read, transcendentals=0),
    )(*operands)


def prepare_kernel(tokens_ref, gain_ref, slot_ref, scaled_ref, squares_ref):
    rows = tokens_ref.shape[0]
    wide_f = tokens_ref[...].astype(F32)
    squares = jnp.sum(wide_f * wide_f, axis=1, keepdims=True)
    scaled = (wide_f * gain_ref[...].astype(F32)).astype(BF16)
    picked = lax.broadcasted_iota(jnp.int32, (rows, rows), 0) == slot_ref[...]
    scaled_ref[...] = jnp.dot(
        picked.astype(BF16), scaled, preferred_element_type=F32
    ).astype(BF16)
    turned = jnp.sum(jnp.where(picked, jnp.transpose(jnp.broadcast_to(squares, (rows, rows))), 0.0), axis=1, keepdims=True)
    squares_ref[...] = jnp.broadcast_to(turned, squares_ref.shape)


def share_kernel(scaled_ref, key_ref, value_ref, key_share_ref, value_share_ref):
    key_share_ref[...] = jnp.dot(scaled_ref[...], key_ref[...], preferred_element_type=F32)
    value_share_ref[...] = jnp.dot(scaled_ref[...], value_ref[...], preferred_element_type=F32)


def add_blocks(offsets, place, blocks_ref, weight_ref, total):
    features = blocks_ref.shape[2]
    for k, offset in enumerate(offsets):
        start = pl.multiple_of((place ^ offset) * features, features)
        total = total + jnp.dot(
            blocks_ref[k], weight_ref[pl.ds(start, features), :], preferred_element_type=F32
        )
    return total


def query_kernel(offsets, place_ref, blocks_ref, weight_ref, *rest):
    total = rest[0][...] if len(rest) > 1 else jnp.zeros(rest[-1].shape, F32)
    rest[-1][...] = add_blocks(offsets, place_ref[0], blocks_ref, weight_ref, total)


def message_kernel(
    offsets, pairs, place_ref, blocks_ref, weight_ref, total_ref, key_ref, value_ref, squares_ref, message_ref
):
    query = add_blocks(offsets, place_ref[0], blocks_ref, weight_ref, total_ref[...])
    rows = query.shape[0]
    held = query.shape[1] // HEAD_SIZE
    for target in range(message_ref.shape[0]):
        head, first = target * pairs // rows, target * pairs % rows
        slots = slice(first, first + pairs)
        columns = slice(head * HEAD_SIZE, (head + 1) * HEAD_SIZE)
        sent = range(head, held, KEY_VALUE_HEADS) if held % KEY_VALUE_HEADS == 0 else range(held)
        at = 0
        for j in sent:
            message_ref[target, at : at + pairs, :] = query[slots, j * HEAD_SIZE : (j + 1) * HEAD_SIZE]
            at += pairs
        message_ref[target, at : at + pairs, :] = key_ref[slots, columns]
        message_ref[target, at + pairs : at + 2 * pairs, :] = value_ref[slots, columns]
        message_ref[target, at + 2 * pairs : at + 3 * pairs, :] = squares_ref[slots, :]


def rotated(values, cosines, sines):
    even = lax.broadcasted_iota(jnp.int32, values.shape, 1) % 2 == 0
    swapped = jnp.where(
        even, -pltpu.roll(values, HEAD_SIZE - 1, 1), pltpu.roll(values, 1, 1)
    )
    return values * cosines + swapped * sines


def attend_kernel(
    pairs, width, lengths_ref, query_ref, rest_ref, cos_ref, sin_ref, keys_ref, values_ref, out_ref, wide_ref
):
    group = query_ref.shape[0]
    at = rest_ref.shape[1] - 3 * pairs
    summed = jnp.sum(rest_ref[:, at:, :], axis=0)
    score_scale = 1.0 / math.sqrt(HEAD_SIZE)
    for i in range(pairs):
        length = lengths_ref[i]
        scale = lax.rsqrt(summed[2 * pairs + i : 2 * pairs + i + 1, :] * (1.0 / width) + EPS)
        cosines, sines = cos_ref[i : i + 1, :], sin_ref[i : i + 1, :]
        query = rotated(query_ref[:, i, :] * scale, cosines, sines).astype(BF16)
        key = jnp.broadcast_to(summed[i : i + 1, :] * scale, (8, HEAD_SIZE))
        key = rotated(key, cosines, sines)[0:1, :].astype(BF16).astype(F32)
        value = (summed[pairs + i : pairs + i + 1, :] * scale).astype(BF16).astype(F32)
        own = jnp.sum(query.astype(F32) * key, axis=1, keepdims=True) * score_scale
        scores = (
            lax.dot_general(
                query, keys_ref[i], (((1,), (1,)), ((), ())), preferred_element_type=F32
            )
            * score_scale
        )
        valid = lax.broadcasted_iota(jnp.int32, scores.shape, 1) < length
        scores = jnp.where(valid, scores, -jnp.inf)
        top = jnp.maximum(jnp.max(scores, axis=1, keepdims=True), own)
        weights = jnp.exp(scores - top)
        own_w = jnp.exp(own - top)
        share = 1.0 / (jnp.sum(weights, axis=1, keepdims=True) + own_w)
        own_p = (own_w * share).astype(BF16).astype(F32)
        blended = (
            jnp.dot((weights * share).astype(BF16), values_ref[i], preferred_element_type=F32)
            + own_p * value
        )
        for g in range(group):
            wide_ref[i : i + 1, g * HEAD_SIZE : (g + 1) * HEAD_SIZE] = blended[g : g + 1, :]
    out_ref[...] = wide_ref[...].astype(BF16)


def project_kernel(
    pairs, head_offsets, slot_offsets, place_ref, slot_ref, mine_ref, other_ref, weight_ref, out_ref, left_ref
):
    heads, half, _ = mine_ref.shape
    rows, columns = out_ref.shape
    devices_of_head = rows // pairs
    group_place = place_ref[0] % devices_of_head
    head_place = place_ref[0] // devices_of_head
    position = lax.broadcasted_iota(jnp.int32, (rows, half), 1)

    def picked(offsets):
        device = jnp.zeros_like(position)
        for k, offset in enumerate(offsets):
            device = jnp.where(position // pairs == k, group_place ^ offset, device)
        return (slot_ref[...] == device * pairs + position % pairs).astype(BF16)

    mine_pick, other_pick = picked(slot_offsets[: half // pairs]), picked(slot_offsets[half // pairs :])
    for z, offset in enumerate(head_offsets):
        head = head_place ^ offset
        ordered = (
            jnp.dot(mine_pick, mine_ref[z], preferred_element_type=F32)
            + jnp.dot(other_pick, other_ref[z], preferred_element_type=F32)
        ).astype(BF16)
        for g in range(QUERY_GROUP):
            start = pl.multiple_of((g * heads + head) * HEAD_SIZE, HEAD_SIZE)
            left_ref[:, pl.ds(start, HEAD_SIZE)] = ordered[:, g * HEAD_SIZE : (g + 1) * HEAD_SIZE]
    depth = weight_ref.shape[0]
    step = min(1024, depth)

    def add(k, total):
        at = pl.multiple_of(k * step, step)
        return total + jnp.dot(
            left_ref[:, pl.ds(at, step)], weight_ref[pl.ds(at, step), :], preferred_element_type=F32
        )

    total = lax.fori_loop(0, depth // step, add, jnp.zeros((rows, columns), F32))
    out_ref[...] = total.astype(BF16)


def swap(array, bit, count):
    return lax.ppermute(array, "wide", [(i, i ^ bit) for i in range(count)])


def body(
    count,
    tokens,
    norm_gain,
    slot_of_row,
    lengths,
    w_query,
    key_projection,
    value_projection,
    output_projection,
    slot_key_cache,
    slot_value_cache,
):
    place = lax.axis_index("wide")
    rows, features = tokens.shape
    pairs = slot_key_cache.shape[0]
    width = w_query.shape[0]
    query_columns = w_query.shape[1]
    held = query_columns // HEAD_SIZE
    devices_of_head = rows // pairs
    bits = [1 << b for b in reversed(range(count.bit_length() - 1))]
    places = place.astype(jnp.int32).reshape(1)

    scaled, squares = call(
        prepare_kernel,
        (
            jax.ShapeDtypeStruct((rows, features), BF16),
            jax.ShapeDtypeStruct((rows, HEAD_SIZE), F32),
        ),
        (tokens, norm_gain.reshape(1, features), slot_of_row.reshape(1, rows)),
    )
    shares = jax.ShapeDtypeStruct((rows, key_projection.shape[1]), F32)
    key_share, value_share = call(
        share_kernel,
        (shares, shares),
        (scaled, key_projection, value_projection),
        near=(1, 2),
        flops=4 * rows * key_projection.size,
        read=4 * key_projection.size,
    )

    blocks, offsets, total = scaled[None], [0], None
    done = 0
    for bit in bits:
        arrived = swap(blocks, bit, count)
        if len(offsets) - done >= 4 or bit == 1:
            part = blocks[done:]
            total = call(
                functools.partial(query_kernel, tuple(offsets[done:])),
                jax.ShapeDtypeStruct((rows, query_columns), F32),
                (places, part, w_query) + (() if total is None else (total,)),
                near=(1, 2),
                smem=(0,),
                flops=2 * part.size * query_columns,
                read=2 * part.shape[0] * features * query_columns,
            )
            done = len(offsets)
        if bit > 1:
            blocks = jnp.concatenate([blocks, arrived], 0)
        offsets = offsets + [o ^ bit for o in offsets]
    half = count // 2
    sent = held // KEY_VALUE_HEADS if held % KEY_VALUE_HEADS == 0 else held
    message = call(
        functools.partial(message_kernel, tuple(offsets[half:]), pairs),
        jax.ShapeDtypeStruct((count, pairs * (sent + 3), HEAD_SIZE), F32),
        (places, arrived, w_query, total, key_share, value_share, squares),
        near=(1, 2),
        smem=(0,),
        flops=2 * arrived.size * query_columns,
        read=2 * half * features * query_columns,
    )

    got = lax.all_to_all(message, "wide", 0, 0, tiled=True)
    if sent == 1 and held % KEY_VALUE_HEADS == 0:
        query_rows = got
    else:
        query_rows = (
            got[:, : pairs * sent].reshape(count, sent, pairs, HEAD_SIZE).reshape(-1, pairs, HEAD_SIZE)
        )
        if held % KEY_VALUE_HEADS:
            head = place // devices_of_head
            query_rows = lax.dynamic_index_in_dim(
                query_rows.reshape(QUERY_GROUP, KEY_VALUE_HEADS, pairs, HEAD_SIZE), head, 1, False
            )
    first = (place * pairs) % rows
    own_lengths = lax.dynamic_slice_in_dim(lengths, first, pairs, 0)
    index = jnp.arange(HEAD_SIZE, dtype=jnp.int32)
    rate = ROPE_BASE ** (-(index - index % 2).astype(F32) / HEAD_SIZE)
    angle = own_lengths.astype(F32)[:, None] * rate[None, :]
    cache_bytes = 2 * slot_key_cache.size
    attended = call(
        functools.partial(attend_kernel, pairs, width),
        jax.ShapeDtypeStruct((pairs, QUERY_GROUP * HEAD_SIZE), BF16),
        (own_lengths, query_rows, got, jnp.cos(angle), jnp.sin(angle), slot_key_cache, slot_value_cache),
        near=(5, 6),
        smem=(0,),
        scratch=(pltpu.VMEM((pairs, QUERY_GROUP * HEAD_SIZE), F32),),
        limit=8 * MIB,
        flops=4 * QUERY_GROUP * slot_key_cache.size,
        read=2 * cache_bytes,
    )

    mine = attended[None]
    for bit in bits:
        other = swap(mine, bit, count)
        if bit > 1:
            mine = jnp.concatenate([mine, other], 0 if bit >= devices_of_head else 1)
    head_offsets, slot_offsets = [0], [0]
    for bit in bits:
        if bit >= devices_of_head:
            head_offsets = head_offsets + [o ^ (bit // devices_of_head) for o in head_offsets]
        else:
            slot_offsets = slot_offsets + [o ^ bit for o in slot_offsets]
    return call(
        functools.partial(project_kernel, pairs, tuple(head_offsets), tuple(slot_offsets)),
        jax.ShapeDtypeStruct((rows, output_projection.shape[1]), BF16),
        (places, slot_of_row.reshape(rows, 1), mine, other, output_projection),
        near=(4,),
        smem=(0,),
        scratch=(pltpu.VMEM((rows, output_projection.shape[0]), BF16),),
        flops=2 * rows * output_projection.size,
        read=2 * output_projection.size,
    )


def solution(mesh):
    placed = (
        P("groups", "wide"),
        P("wide"),
        P("groups"),
        P("groups"),
        P(None, "wide"),
        P("wide", None),
        P("wide", None),
        P(None, "wide"),
        P(("groups", "wide"), None, None),
        P(("groups", "wide"), None, None),
    )
    return jax.shard_map(
        functools.partial(body, mesh.shape["wide"]),
        mesh=mesh,
        in_specs=placed,
        out_specs=P("groups", "wide"),
        check_vma=False,
    )
```

time: 175 us -> 83 us (0.47)
  blocking collectives: 140 us -> 0 us
  waiting for transfers between devices: 0 us -> 29.6 us
  matrix products: 22.2 us -> 0 us
  local copies, waits for them, and re-layouts: 8.89 us -> 25.7 us
  starting transfers between devices: 0 us -> 14.5 us
  Pallas kernels: 0 us -> 11.5 us
  other arithmetic: 3.7 us -> 1.06 us
    all_gather x4 -> x0, blocking collectives: 80.4 us -> none  [the longest x1 24.9 us: body(): lax.all_gather(tokens, 'wide', axis=1, tiled=True)]
    psum x1 -> x0, blocking collectives: 59.2 us -> none  [body(): key_total, value_total = lax.psum((key_share, value_share), 'wide')]
    unnamed x8 -> x20, local copies, waits for them, and re-layouts: 0.09 us -> 24.9 us
    dot_general x10 -> x0, matrix products: 22.2 us -> none  [the longest x1 8.03 us: body(): jnp.dot(normed, w_query, preferred_element_type=jnp.float32)]
    ppermute x0 -> x8, waiting for transfers between devices: none -> 21.8 us  [swap(): return lax.ppermute(array, 'wide', [(i, i ^ bit) for i in range(count)])]
    pallas_call x0 -> x7, Pallas kernels: none -> 11.5 us  [call(): pl.pallas_call(kernel, out_shape=out_shape, in_specs=specs, out_specs=jax...]
    ppermute x0 -> x8, starting transfers between devices: none -> 8.23 us  [swap(): return lax.ppermute(array, 'wide', [(i, i ^ bit) for i in range(count)])]
    transpose x1 -> x0, local copies, waits for them, and re-layouts: 8.19 us -> none  [body(): weight_per_head = output_projection.reshape(query_group, KEY_VALUE_HEADS,...]
  transfers between devices with their start and end apart: 0 -> 9, of which waited for: 0 -> 8; matrix products, arithmetic and copies ran while one was open for 0% -> 1% of each run, Pallas kernels for 0% -> 2%
where the time goes in v1:
time: 83 us; the launch traced here: 82.4 us
  waiting for transfers between devices  29.6 us (36%)
  local copies, waits for them, and re-layouts  25.7 us (31%)
  starting transfers between devices  14.5 us (17%)
  Pallas kernels  11.5 us (14%)
  other arithmetic  1.06 us (1%)
    unnamed x20, local copies, waits for them, and re-layouts  24.9 us
    ppermute x8, waiting for transfers between devices, swap(): return lax.ppermute(array, 'wide', [(i, i ^ bit) for i in range(count)])  21.8 us
    pallas_call x7, Pallas kernels, call(): pl.pallas_call(kernel, out_shape=out_shape, in_specs=specs, out_specs=jax...  11.5 us
    ppermute x8, starting transfers between devices, swap(): return lax.ppermute(array, 'wide', [(i, i ^ bit) for i in range(count)])  8.23 us
    all_to_all x1, waiting for transfers between devices, body(): got = lax.all_to_all(message, 'wide', 0, 0, tiled=True)  7.81 us
    all_to_all x1, starting transfers between devices, body(): got = lax.all_to_all(message, 'wide', 0, 0, tiled=True)  6.24 us
  transfers between devices with their start and end apart: 9, of which 8 were waited for; matrix products, arithmetic and copies ran while one was open for 1% of the time, Pallas kernels for 2%

profile of v1, /device:TPU:0, one launch (start us, length us, event | category | flops | bytes accessed | tf_op | source)
XLA Modules:
  0.0 82.4 jit_solution(4247281508937587276)
XLA Ops:
  0.0 0.7 reshape.30.gain_ref
  0.7 0.0 copy-start.7
  0.7 0.8 copy-done.7
  1.4 0.0 copy-start.8
  1.4 0.7 copy-done.8
  2.1 0.2 shard_map.100
  2.3 4.0 %collective-permute-start = (bf16[1,16,1024]{2,1,0:T(8,128)(2,1)S(1)}, bf16[1,16,1024]{2,1,0:T(8,128)(2,1)S(1)}, u32[]{:S(2)}, u32[]{:S(2)}) collective-permute-start(bf16[1,16,1024]{2,1,0:T(8,128)(2,1)S(1)} %bitcast.5), channel_id=1, source_target_pairs={{0,8},{1,9},{2,10},{3,11},{4,12},{5,13},{6,14},{7,15},{8,0},{9,1},... | collective-permute-start | bytes 98312 | tf_op jit(solution)/shard_map/ppermute | solution.py:180
  6.4 2.2 %collective-permute-done = bf16[1,16,1024]{2,1,0:T(8,128)(2,1)S(1)} collective-permute-done((bf16[1,16,1024]{2,1,0:T(8,128)(2,1)S(1)}, bf16[1,16,1024]{2,1,0:T(8,128)(2,1)S(1)}, u32[]{:S(2)}, u32[]{:S(2)}) %collective-permute-start) | collective-permute-done | bytes 32800 | tf_op jit(solution)/shard_map/ppermute | solution.py:180
  8.6 1.6 %collective-permute-start.1 = (bf16[2,16,1024]{2,1,0:T(8,128)(2,1)S(1)}, bf16[2,16,1024]{2,1,0:T(8,128)(2,1)S(1)}, u32[]{:S(2)}, u32[]{:S(2)}) collective-permute-start(bf16[2,16,1024]{2,1,0:T(8,128)(2,1)S(1)} %pad_maximum_fusion.3), channel_id=1, source_target_pairs={{0,4},{1,5},{2,6},{3,7},{4,0},{5,1},{6,2},{7,3},{8,12},{9,13},{10,... | collective-permute-start | bytes 196616 | tf_op jit(solution)/shard_map/ppermute | solution.py:180
  10.2 2.7 %collective-permute-done.1 = bf16[2,16,1024]{2,1,0:T(8,128)(2,1)S(1)} collective-permute-done((bf16[2,16,1024]{2,1,0:T(8,128)(2,1)S(1)}, bf16[2,16,1024]{2,1,0:T(8,128)(2,1)S(1)}, u32[]{:S(2)}, u32[]{:S(2)}) %collective-permute-start.1) | collective-permute-done | bytes 65568 | tf_op jit(solution)/shard_map/ppermute | solution.py:180
  13.0 1.8 %collective-permute-start.2 = (bf16[4,16,1024]{2,1,0:T(8,128)(2,1)S(1)}, bf16[4,16,1024]{2,1,0:T(8,128)(2,1)S(1)}, u32[]{:S(2)}, u32[]{:S(2)}) collective-permute-start(bf16[4,16,1024]{2,1,0:T(8,128)(2,1)S(1)} %pad_maximum_fusion.1.blocks_ref), channel_id=1, source_target_pairs={{0,2},{1,3},{2,0},{3,1},{4,6},{5,7},{6,4},{7,5},{8,10},{9,11},{10,... | collective-permute-start | bytes 393224 | tf_op jit(solution)/shard_map/ppermute | solution.py:180
  14.8 3.2 %collective-permute-done.2.blocks_ref = bf16[4,16,1024]{2,1,0:T(8,128)(2,1)S(1)} collective-permute-done((bf16[4,16,1024]{2,1,0:T(8,128)(2,1)S(1)}, bf16[4,16,1024]{2,1,0:T(8,128)(2,1)S(1)}, u32[]{:S(2)}, u32[]{:S(2)}) %collective-permute-start.2) | collective-permute-done | bytes 131104 | tf_op jit(solution)/shard_map/ppermute | solution.py:180
  18.0 0.1 collective-permute-start.3
  18.1 0.0 copy-start.5
  18.1 1.2 %copy-done.5 = bf16[1024,512]{1,0:T(8,128)(2,1)S(1)} copy-done((bf16[1024,512]{1,0:T(8,128)(2,1)S(1)}, bf16[1024,512]{1,0:T(8,128)(2,1)}, u32[]{:S(2)}) %copy-start.5) | copy-done | bytes 1048600
  19.4 0.0 copy-start.6
  19.4 1.2 %copy-done.6 = bf16[1024,512]{1,0:T(8,128)(2,1)S(1)} copy-done((bf16[1024,512]{1,0:T(8,128)(2,1)S(1)}, bf16[1024,512]{1,0:T(8,128)(2,1)}, u32[]{:S(2)}) %copy-start.6) | copy-done | bytes 1048600
  20.6 0.4 shard_map.103
  21.0 0.7 fusion.4
  21.7 0.0 copy-start
  21.7 5.8 %copy-done = bf16[16384,512]{1,0:T(8,128)(2,1)S(1)} copy-done((bf16[16384,512]{1,0:T(8,128)(2,1)S(1)}, bf16[16384,512]{1,0:T(8,128)(2,1)}, u32[]{:S(2)}) %copy-start) | copy-done | bytes 16777240
  27.5 0.0 copy-start.1
  27.5 0.6 shard_map.101.rest_0_
  28.1 5.1 %copy-done.1 = bf16[16384,512]{1,0:T(8,128)(2,1)S(1)} copy-done((bf16[16384,512]{1,0:T(8,128)(2,1)S(1)}, bf16[16384,512]{1,0:T(8,128)(2,1)}, u32[]{:S(2)}) %copy-start.1) | copy-done | bytes 16777240
  33.2 0.6 shard_map.102.total_ref
  33.9 0.0 copy-start.9
  33.9 0.0 collective-permute-done.3.blocks_ref
  33.9 1.9 %shard_map.104 = f32[16,16,128]{2,1,0:T(8,128)} custom-call(s32[1]{0:T(128)} %bitcast.place_ref, bf16[8,16,1024]{2,1,0:T(8,128)(2,1)S(1)} %collective-permute-done.3.blocks_ref, bf16[16384,512]{1,0:T(8,128)(2,1)S(1)} %copy-done.1, f32[16,512]{1,0:T(8,128)S(1)} %shard_map.102.total_ref, f32[16,512]{1,0:T(8,128)S(1)} %get-tuple-element.10.key_ref, ...), custom_call_target="tpu_custom_call" | custom-call | flops 134217728 | bytes 8388608 | tf_op jit(solution)/shard_map/pallas_call | solution.py:30
  35.8 6.2 %all-to-all-start = ((f32[16,16,128]{2,1,0:T(8,128)}), f32[16,16,128]{2,1,0:T(8,128)S(1)}, u32[]{:S(2)}, u32[]{:S(2)}) async-start(f32[16,16,128]{2,1,0:T(8,128)} %shard_map.104), calls=%async_computation | async-start | bytes 262144 | tf_op jit(solution)/shard_map/all_to_all | solution.py:255
  42.0 0.1 multiply_sine_fusion
  42.1 7.8 %all-to-all-done.query_ref.rest_ref = f32[16,16,128]{2,1,0:T(8,128)S(1)} async-done(((f32[16,16,128]{2,1,0:T(8,128)}), f32[16,16,128]{2,1,0:T(8,128)S(1)}, u32[]{:S(2)}, u32[]{:S(2)}) %all-to-all-start) | async-done | bytes 131104 | tf_op jit(solution)/shard_map/all_to_all | solution.py:255
  49.9 2.2 %copy-done.3 = bf16[4,4096,128]{2,1,0:T(8,128)(2,1)S(1)} copy-done((bf16[4,4096,128]{2,1,0:T(8,128)(2,1)S(1)}, bf16[4,4096,128]{2,1,0:T(8,128)(2,1)}, u32[]{:S(2)}) %copy-start.3) | copy-done | bytes 4194328
  52.1 2.2 %copy-done.4 = bf16[4,4096,128]{2,1,0:T(8,128)(2,1)S(1)} copy-done((bf16[4,4096,128]{2,1,0:T(8,128)(2,1)S(1)}, bf16[4,4096,128]{2,1,0:T(8,128)(2,1)}, u32[]{:S(2)}) %copy-start.4) | copy-done | bytes 4194328
  54.3 3.7 %shard_map.105 = bf16[4,2048]{1,0:T(4,128)(2,1)S(1)} custom-call(s32[4]{0:T(128)S(1)} %get-tuple-element.14.lengths_ref, f32[16,16,128]{2,1,0:T(8,128)S(1)} %all-to-all-done.query_ref.rest_ref, f32[16,16,128]{2,1,0:T(8,128)S(1)} %all-to-all-done.query_ref.rest_ref, f32[4,128]{1,0:T(4,128)S(1)} %get-tuple-element.16.cos_ref, ...), custom_call_target="tpu_custom_call" | custom-call | flops 134217728 | bytes 8388608 | tf_op jit(solution)/shard_map/pallas_call | solution.py:30
  58.0 0.5 collective-permute-start.4
  58.5 4.2 %collective-permute-done.4 = bf16[1,4,2048]{2,1,0:T(4,128)(2,1)S(1)} collective-permute-done((bf16[1,4,2048]{2,1,0:T(4,128)(2,1)S(1)}, bf16[1,4,2048]{2,1,0:T(4,128)(2,1)S(1)}, u32[]{:S(2)}, u32[]{:S(2)}) %collective-permute-start.4) | collective-permute-done | bytes 16416 | tf_op jit(solution)/shard_map/ppermute | solution.py:180
  62.7 0.1 collective-permute-start.5
  62.8 3.9 %collective-permute-done.5 = bf16[2,4,2048]{2,1,0:T(4,128)(2,1)S(1)} collective-permute-done((bf16[2,4,2048]{2,1,0:T(4,128)(2,1)S(1)}, bf16[2,4,2048]{2,1,0:T(4,128)(2,1)S(1)}, u32[]{:S(2)}, u32[]{:S(2)}) %collective-permute-start.5) | collective-permute-done | bytes 32800 | tf_op jit(solution)/shard_map/ppermute | solution.py:180
  66.7 0.1 pad_maximum_fusion.4
  66.8 0.1 collective-permute-start.6
  66.9 4.3 %collective-permute-done.6 = bf16[4,4,2048]{2,1,0:T(4,128)(2,1)S(1)} collective-permute-done((bf16[4,4,2048]{2,1,0:T(4,128)(2,1)S(1)}, bf16[4,4,2048]{2,1,0:T(4,128)(2,1)S(1)}, u32[]{:S(2)}, u32[]{:S(2)}) %collective-permute-start.6) | collective-permute-done | bytes 65568 | tf_op jit(solution)/shard_map/ppermute | solution.py:180
  71.1 0.1 pad_maximum_fusion.2.mine_ref
  71.2 0.1 collective-permute-start.7
  71.3 0.0 copy-done.9
  71.3 0.1 copy.11.slot_ref
  71.4 1.2 %collective-permute-done.7.other_ref = bf16[4,8,2048]{2,1,0:T(8,128)(2,1)S(1)} collective-permute-done((bf16[4,8,2048]{2,1,0:T(8,128)(2,1)S(1)}, bf16[4,8,2048]{2,1,0:T(8,128)(2,1)S(1)}, u32[]{:S(2)}, u32[]{:S(2)}) %collective-permute-start.7) | collective-permute-done | bytes 131104 | tf_op jit(solution)/shard_map/ppermute | solution.py:180
  72.6 5.8 %copy-done.2 = bf16[8192,1024]{1,0:T(8,128)(2,1)S(1)} copy-done((bf16[8192,1024]{1,0:T(8,128)(2,1)S(1)}, bf16[8192,1024]{1,0:T(8,128)(2,1)}, u32[]{:S(2)}) %copy-start.2) | copy-done | bytes 16777240
  78.4 4.1 %shard_map.106 = bf16[16,1024]{1,0:T(8,128)(2,1)} custom-call(s32[1]{0:T(128)} %bitcast.place_ref, s32[16,1]{1,0:T(8,128)S(1)} %copy.11.slot_ref, bf16[4,8,2048]{2,1,0:T(8,128)(2,1)S(1)} %pad_maximum_fusion.2.mine_ref, bf16[4,8,2048]{2,1,0:T(8,128)(2,1)S(1)} %collective-permute-done.7.other_ref, bf16[8192,1024]{1,0:T(8,128)(2,1)S(1)} %copy-done.2), custom_call_target="tpu_custom_call" | custom-call | flops 268435456 | bytes 16777216 | tf_op jit(solution)/shard_map/pallas_call | solution.py:30
  (8 shorter events, 0.1 us)
Async XLA Ops:
  0.7 0.8 copy-start.7
  1.4 0.7 copy-start.8
  2.3 6.3 %collective-permute-start = (bf16[1,16,1024]{2,1,0:T(8,128)(2,1)S(1)}, bf16[1,16,1024]{2,1,0:T(8,128)(2,1)S(1)}, u32[]{:S(2)}, u32[]{:S(2)}) collective-permute-start(bf16[1,16,1024]{2,1,0:T(8,128)(2,1)S(1)} %bitcast.5), channel_id=1, source_target_pairs={{0,8},{1,9},{2,10},{3,11},{4,12},{5,13},{6,14},{7,15},{8,0},{9,1},... | collective-permute-start | bytes 98312 | tf_op jit(solution)/shard_map/ppermute | solution.py:180
  8.6 4.3 %collective-permute-start.1 = (bf16[2,16,1024]{2,1,0:T(8,128)(2,1)S(1)}, bf16[2,16,1024]{2,1,0:T(8,128)(2,1)S(1)}, u32[]{:S(2)}, u32[]{:S(2)}) collective-permute-start(bf16[2,16,1024]{2,1,0:T(8,128)(2,1)S(1)} %pad_maximum_fusion.3), channel_id=1, source_target_pairs={{0,4},{1,5},{2,6},{3,7},{4,0},{5,1},{6,2},{7,3},{8,12},{9,13},{10,... | collective-permute-start | bytes 196616 | tf_op jit(solution)/shard_map/ppermute | solution.py:180
  13.0 5.0 %collective-permute-start.2 = (bf16[4,16,1024]{2,1,0:T(8,128)(2,1)S(1)}, bf16[4,16,1024]{2,1,0:T(8,128)(2,1)S(1)}, u32[]{:S(2)}, u32[]{:S(2)}) collective-permute-start(bf16[4,16,1024]{2,1,0:T(8,128)(2,1)S(1)} %pad_maximum_fusion.1.blocks_ref), channel_id=1, source_target_pairs={{0,2},{1,3},{2,0},{3,1},{4,6},{5,7},{6,4},{7,5},{8,10},{9,11},{10,... | collective-permute-start | bytes 393224 | tf_op jit(solution)/shard_map/ppermute | solution.py:180
  18.0 15.9 %collective-permute-start.3 = (bf16[8,16,1024]{2,1,0:T(8,128)(2,1)S(1)}, bf16[8,16,1024]{2,1,0:T(8,128)(2,1)S(1)}, u32[]{:S(2)}, u32[]{:S(2)}) collective-permute-start(bf16[8,16,1024]{2,1,0:T(8,128)(2,1)S(1)} %pad_maximum_fusion), channel_id=1, source_target_pairs={{0,1},{1,0},{2,3},{3,2},{4,5},{5,4},{6,7},{7,6},{8,9},{9,8},{10,11... | collective-permute-start | bytes 786440 | tf_op jit(solution)/shard_map/ppermute | solution.py:180
  18.1 1.2 %copy-start.5 = (bf16[1024,512]{1,0:T(8,128)(2,1)S(1)}, bf16[1024,512]{1,0:T(8,128)(2,1)}, u32[]{:S(2)}) copy-start(bf16[1024,512]{1,0:T(8,128)(2,1)} %key_ref.1) | copy-start | bytes 3145732
  19.4 1.2 %copy-start.6 = (bf16[1024,512]{1,0:T(8,128)(2,1)S(1)}, bf16[1024,512]{1,0:T(8,128)(2,1)}, u32[]{:S(2)}) copy-start(bf16[1024,512]{1,0:T(8,128)(2,1)} %value_ref.1) | copy-start | bytes 3145732
  21.7 5.8 %copy-start = (bf16[16384,512]{1,0:T(8,128)(2,1)S(1)}, bf16[16384,512]{1,0:T(8,128)(2,1)}, u32[]{:S(2)}) copy-start(bf16[16384,512]{1,0:T(8,128)(2,1)} %weight_ref.6) | copy-start | bytes 50331652
  27.5 5.8 %copy-start.1 = (bf16[16384,512]{1,0:T(8,128)(2,1)S(1)}, bf16[16384,512]{1,0:T(8,128)(2,1)}, u32[]{:S(2)}) copy-start(bf16[16384,512]{1,0:T(8,128)(2,1)} %weight_ref.6) | copy-start | bytes 50331652
  33.9 37.4 %copy-start.9 = (s32[16]{0:T(128)S(1)}, s32[16]{0:T(128)}, u32[]{:S(2)}) copy-start(s32[16]{0:T(128)} %param.12) | copy-start | bytes 196
  35.8 14.2 %all-to-all-start = ((f32[16,16,128]{2,1,0:T(8,128)}), f32[16,16,128]{2,1,0:T(8,128)S(1)}, u32[]{:S(2)}, u32[]{:S(2)}) async-start(f32[16,16,128]{2,1,0:T(8,128)} %shard_map.104), calls=%async_computation | async-start | bytes 262144 | tf_op jit(solution)/shard_map/all_to_all | solution.py:255
  49.9 2.2 %copy-start.3 = (bf16[4,4096,128]{2,1,0:T(8,128)(2,1)S(1)}, bf16[4,4096,128]{2,1,0:T(8,128)(2,1)}, u32[]{:S(2)}) copy-start(bf16[4,4096,128]{2,1,0:T(8,128)(2,1)} %keys_ref.1) | copy-start | bytes 12582916
  52.1 2.2 %copy-start.4 = (bf16[4,4096,128]{2,1,0:T(8,128)(2,1)S(1)}, bf16[4,4096,128]{2,1,0:T(8,128)(2,1)}, u32[]{:S(2)}) copy-start(bf16[4,4096,128]{2,1,0:T(8,128)(2,1)} %values_ref.1) | copy-start | bytes 12582916
  58.0 4.7 %collective-permute-start.4 = (bf16[1,4,2048]{2,1,0:T(4,128)(2,1)S(1)}, bf16[1,4,2048]{2,1,0:T(4,128)(2,1)S(1)}, u32[]{:S(2)}, u32[]{:S(2)}) collective-permute-start(bf16[1,4,2048]{2,1,0:T(4,128)(2,1)S(1)} %bitcast.9), channel_id=1, source_target_pairs={{0,8},{1,9},{2,10},{3,11},{4,12},{5,13},{6,14},{7,15},{8,0},{9,1},... | collective-permute-start | bytes 49160 | tf_op jit(solution)/shard_map/ppermute | solution.py:180
  62.7 4.0 %collective-permute-start.5 = (bf16[2,4,2048]{2,1,0:T(4,128)(2,1)S(1)}, bf16[2,4,2048]{2,1,0:T(4,128)(2,1)S(1)}, u32[]{:S(2)}, u32[]{:S(2)}) collective-permute-start(bf16[2,4,2048]{2,1,0:T(4,128)(2,1)S(1)} %pad_maximum_fusion.5), channel_id=1, source_target_pairs={{0,4},{1,5},{2,6},{3,7},{4,0},{5,1},{6,2},{7,3},{8,12},{9,13},{10,... | collective-permute-start | bytes 98312 | tf_op jit(solution)/shard_map/ppermute | solution.py:180
  66.8 4.3 %collective-permute-start.6 = (bf16[4,4,2048]{2,1,0:T(4,128)(2,1)S(1)}, bf16[4,4,2048]{2,1,0:T(4,128)(2,1)S(1)}, u32[]{:S(2)}, u32[]{:S(2)}) collective-permute-start(bf16[4,4,2048]{2,1,0:T(4,128)(2,1)S(1)} %pad_maximum_fusion.4), channel_id=1, source_target_pairs={{0,2},{1,3},{2,0},{3,1},{4,6},{5,7},{6,4},{7,5},{8,10},{9,11},{10,... | collective-permute-start | bytes 196616 | tf_op jit(solution)/shard_map/ppermute | solution.py:180
  71.2 1.4 %collective-permute-start.7 = (bf16[4,8,2048]{2,1,0:T(8,128)(2,1)S(1)}, bf16[4,8,2048]{2,1,0:T(8,128)(2,1)S(1)}, u32[]{:S(2)}, u32[]{:S(2)}) collective-permute-start(bf16[4,8,2048]{2,1,0:T(8,128)(2,1)S(1)} %pad_maximum_fusion.2.mine_ref), channel_id=1, source_target_pairs={{0,1},{1,0},{2,3},{3,2},{4,5},{5,4},{6,7},{7,6},{8,9},{9,8},{10,11... | collective-permute-start | bytes 393224 | tf_op jit(solution)/shard_map/ppermute | solution.py:180
  72.6 5.8 %copy-start.2 = (bf16[8192,1024]{1,0:T(8,128)(2,1)S(1)}, bf16[8192,1024]{1,0:T(8,128)(2,1)}, u32[]{:S(2)}) copy-start(bf16[8192,1024]{1,0:T(8,128)(2,1)} %weight_ref.7) | copy-start | bytes 50331652

commit v2 on v1

--- a/solution.py
+++ b/solution.py
@@ -3,6 +3,7 @@
 
 import jax
 import jax.numpy as jnp
+import numpy as np
 from jax import lax
 from jax.experimental import pallas as pl
 from jax.experimental.pallas import tpu as pltpu
@@ -20,13 +21,17 @@
 BF16 = jnp.bfloat16
 
 
-def call(kernel, out_shape, args, near=(), smem=(), scratch=(), limit=4 * MIB, flops=0, read=0):
+def call(kernel, out_shape, args, near=(), far=(), smem=(), scratch=(), limit=4 * MIB, flops=0, read=0):
     operands, specs = [], []
     for i, arg in enumerate(args):
+        space = pltpu.SMEM if i in smem else pltpu.VMEM
         if i in near:
             arg = pltpu.with_memory_space_constraint(arg, pltpu.VMEM)
+        if i in far:
+            arg = pltpu.with_memory_space_constraint(arg, pltpu.HBM)
+            space = pltpu.HBM
         operands.append(arg)
-        specs.append(pl.BlockSpec(memory_space=pltpu.SMEM if i in smem else pltpu.VMEM))
+        specs.append(pl.BlockSpec(memory_space=space))
     return pl.pallas_call(
         kernel,
         out_shape=out_shape,
@@ -38,11 +43,22 @@
     )(*operands)
 
 
-def prepare_kernel(tokens_ref, gain_ref, slot_ref, scaled_ref, squares_ref):
-    rows = tokens_ref.shape[0]
+def prepare_kernel(far_tokens, far_gain, far_slot, scaled_ref, squares_ref, tokens_ref, gain_ref, slot_ref, sems):
+    copies = [
+        pltpu.make_async_copy(far, near, sems.at[i])
+        for i, (far, near) in enumerate(
+            ((far_tokens, tokens_ref), (far_gain, gain_ref), (far_slot, slot_ref))
+        )
+    ]
+    for copy in copies:
+        copy.start()
+    for copy in copies:
+        copy.wait()
+    rows, features = tokens_ref.shape
     wide_f = tokens_ref[...].astype(F32)
     squares = jnp.sum(wide_f * wide_f, axis=1, keepdims=True)
-    scaled = (wide_f * gain_ref[...].astype(F32)).astype(BF16)
+    gain = gain_ref[...].astype(F32).reshape(1, features)
+    scaled = (wide_f * gain).astype(BF16)
     picked = lax.broadcasted_iota(jnp.int32, (rows, rows), 0) == slot_ref[...]
     scaled_ref[...] = jnp.dot(
         picked.astype(BF16), scaled, preferred_element_type=F32
@@ -51,30 +67,75 @@
     squares_ref[...] = jnp.broadcast_to(turned, squares_ref.shape)
 
 
-def share_kernel(scaled_ref, key_ref, value_ref, key_share_ref, value_share_ref):
-    key_share_ref[...] = jnp.dot(scaled_ref[...], key_ref[...], preferred_element_type=F32)
-    value_share_ref[...] = jnp.dot(scaled_ref[...], value_ref[...], preferred_element_type=F32)
-
-
-def add_blocks(offsets, place, blocks_ref, weight_ref, total):
+def join_kernel(mine_ref, arrived_ref, after_ref, joined_ref):
+    count = mine_ref.shape[0]
+    joined_ref[:count] = mine_ref[...]
+    joined_ref[count:] = arrived_ref[...]
+
+
+def weight_rows(place, offset, features, weight_ref):
+    return weight_ref.at[pl.ds(pl.multiple_of((place ^ offset) * features, features), features), :]
+
+
+def window_kernel(offsets, ahead, shares, blocks_ref, weight_ref, *refs):
+    refs = list(refs)
+    key_ref, value_ref = (refs.pop(0), refs.pop(0)) if shares else (None, None)
+    total_in = None if shares else refs.pop(0)
+    total_ref = refs.pop(0)
+    key_share_ref, value_share_ref = (refs.pop(0), refs.pop(0)) if shares else (None, None)
+    ahead_ref = refs.pop(0) if ahead else None
+    held_ref, sems = refs.pop(0), refs.pop(0)
     features = blocks_ref.shape[2]
+    place = lax.axis_index("wide")
+    copies = []
+    if shares:
+        near_key, near_value = refs
+        copies += [
+            pltpu.make_async_copy(key_ref, near_key, sems.at[0]),
+            pltpu.make_async_copy(value_ref, near_value, sems.at[1]),
+        ]
     for k, offset in enumerate(offsets):
-        start = pl.multiple_of((place ^ offset) * features, features)
-        total = total + jnp.dot(
-            blocks_ref[k], weight_ref[pl.ds(start, features), :], preferred_element_type=F32
-        )
-    return total
-
-
-def query_kernel(offsets, place_ref, blocks_ref, weight_ref, *rest):
-    total = rest[0][...] if len(rest) > 1 else jnp.zeros(rest[-1].shape, F32)
-    rest[-1][...] = add_blocks(offsets, place_ref[0], blocks_ref, weight_ref, total)
+        copies.append(
+            pltpu.make_async_copy(
+                weight_rows(place, offset, features, weight_ref), held_ref.at[k], sems.at[len(copies)]
+            )
+        )
+    fetched = []
+    for k, offset in enumerate(ahead):
+        fetched.append(
+            pltpu.make_async_copy(
+                weight_rows(place, offset, features, weight_ref),
+                ahead_ref.at[k],
+                sems.at[len(copies) + len(fetched)],
+            )
+        )
+    for copy in copies + fetched:
+        copy.start()
+    first = blocks_ref.shape[0] - len(offsets)
+    if shares:
+        copies[0].wait()
+        key_share_ref[...] = jnp.dot(blocks_ref[0], near_key[...], preferred_element_type=F32)
+        copies[1].wait()
+        value_share_ref[...] = jnp.dot(blocks_ref[0], near_value[...], preferred_element_type=F32)
+        copies = copies[2:]
+    total = jnp.zeros(total_ref.shape, F32) if total_in is None else total_in[...]
+    for k, copy in enumerate(copies):
+        copy.wait()
+        total = total + jnp.dot(blocks_ref[first + k], held_ref[k], preferred_element_type=F32)
+    total_ref[...] = total
+    for copy in fetched:
+        copy.wait()
 
 
 def message_kernel(
-    offsets, pairs, place_ref, blocks_ref, weight_ref, total_ref, key_ref, value_ref, squares_ref, message_ref
+    pairs, blocks_ref, total_ref, key_ref, value_ref, squares_ref, *refs
 ):
-    query = add_blocks(offsets, place_ref[0], blocks_ref, weight_ref, total_ref[...])
+    message_ref = refs[-1]
+    query, block = total_ref[...], 0
+    for weight_ref in refs[:-1]:
+        for k in range(weight_ref.shape[0]):
+            query = query + jnp.dot(blocks_ref[block], weight_ref[k], preferred_element_type=F32)
+            block += 1
     rows = query.shape[0]
     held = query.shape[1] // HEAD_SIZE
     for target in range(message_ref.shape[0]):
@@ -100,16 +161,22 @@
 
 
 def attend_kernel(
-    pairs, width, lengths_ref, query_ref, rest_ref, cos_ref, sin_ref, keys_ref, values_ref, out_ref, wide_ref
+    pairs, width, lengths_ref, rate_ref, query_ref, rest_ref, keys_ref, values_ref, out_ref, wide_ref
 ):
     group = query_ref.shape[0]
+    first = (lax.axis_index("wide") * pairs) % lengths_ref.shape[0]
+    positions = jnp.concatenate(
+        [jnp.full((1, HEAD_SIZE), lengths_ref[first + i], jnp.int32) for i in range(pairs)], 0
+    )
+    angle = positions.astype(F32) * rate_ref[...]
+    all_cosines, all_sines = jnp.cos(angle), jnp.sin(angle)
     at = rest_ref.shape[1] - 3 * pairs
     summed = jnp.sum(rest_ref[:, at:, :], axis=0)
     score_scale = 1.0 / math.sqrt(HEAD_SIZE)
     for i in range(pairs):
-        length = lengths_ref[i]
+        length = lengths_ref[first + i]
         scale = lax.rsqrt(summed[2 * pairs + i : 2 * pairs + i + 1, :] * (1.0 / width) + EPS)
-        cosines, sines = cos_ref[i : i + 1, :], sin_ref[i : i + 1, :]
+        cosines, sines = all_cosines[i : i + 1, :], all_sines[i : i + 1, :]
         query = rotated(query_ref[:, i, :] * scale, cosines, sines).astype(BF16)
         key = jnp.broadcast_to(summed[i : i + 1, :] * scale, (8, HEAD_SIZE))
         key = rotated(key, cosines, sines)[0:1, :].astype(BF16).astype(F32)
@@ -138,20 +205,22 @@
 
 
 def project_kernel(
-    pairs, head_offsets, slot_offsets, place_ref, slot_ref, mine_ref, other_ref, weight_ref, out_ref, left_ref
+    pairs, head_offsets, slot_offsets, slot_ref, mine_ref, other_ref, weight_ref, out_ref, left_ref
 ):
     heads, half, _ = mine_ref.shape
     rows, columns = out_ref.shape
     devices_of_head = rows // pairs
-    group_place = place_ref[0] % devices_of_head
-    head_place = place_ref[0] // devices_of_head
+    place = lax.axis_index("wide")
+    group_place = place % devices_of_head
+    head_place = place // devices_of_head
+    slot_of_row = jnp.transpose(jnp.broadcast_to(slot_ref[...], (rows, rows)))[:, 0:1]
     position = lax.broadcasted_iota(jnp.int32, (rows, half), 1)
 
     def picked(offsets):
         device = jnp.zeros_like(position)
         for k, offset in enumerate(offsets):
             device = jnp.where(position // pairs == k, group_place ^ offset, device)
-        return (slot_ref[...] == device * pairs + position % pairs).astype(BF16)
+        return (slot_of_row == device * pairs + position % pairs).astype(BF16)
 
     mine_pick, other_pick = picked(slot_offsets[: half // pairs]), picked(slot_offsets[half // pairs :])
     for z, offset in enumerate(head_offsets):
@@ -193,7 +262,6 @@
     slot_key_cache,
     slot_value_cache,
 ):
-    place = lax.axis_index("wide")
     rows, features = tokens.shape
     pairs = slot_key_cache.shape[0]
     width = w_query.shape[0]
@@ -201,7 +269,6 @@
     held = query_columns // HEAD_SIZE
     devices_of_head = rows // pairs
     bits = [1 << b for b in reversed(range(count.bit_length() - 1))]
-    places = place.astype(jnp.int32).reshape(1)
 
     scaled, squares = call(
         prepare_kernel,
@@ -209,47 +276,74 @@
             jax.ShapeDtypeStruct((rows, features), BF16),
             jax.ShapeDtypeStruct((rows, HEAD_SIZE), F32),
         ),
-        (tokens, norm_gain.reshape(1, features), slot_of_row.reshape(1, rows)),
-    )
+        (tokens, norm_gain, slot_of_row.reshape(1, rows)),
+        far=(0, 1, 2),
+        scratch=(
+            pltpu.VMEM((rows, features), BF16),
+            pltpu.VMEM((features,), BF16),
+            pltpu.VMEM((1, rows), jnp.int32),
+            pltpu.SemaphoreType.DMA((3,)),
+        ),
+    )
+
+    half = count // 2
+    last = [0]
+    for bit in bits[:-1]:
+        last = last + [o ^ bit for o in last]
+    last = [o ^ bits[-1] for o in last]
+    cuts = [0, half // 4, 3 * half // 4, half]
+    block_bytes = 2 * features * query_columns
+    totals = jax.ShapeDtypeStruct((rows, query_columns), F32)
     shares = jax.ShapeDtypeStruct((rows, key_projection.shape[1]), F32)
-    key_share, value_share = call(
-        share_kernel,
-        (shares, shares),
-        (scaled, key_projection, value_projection),
-        near=(1, 2),
-        flops=4 * rows * key_projection.size,
-        read=4 * key_projection.size,
-    )
-
-    blocks, offsets, total = scaled[None], [0], None
-    done = 0
-    for bit in bits:
+    blocks, offsets, new, total, fetched = scaled[None], [0], [0], None, []
+    for step, bit in enumerate(bits):
         arrived = swap(blocks, bit, count)
-        if len(offsets) - done >= 4 or bit == 1:
-            part = blocks[done:]
-            total = call(
-                functools.partial(query_kernel, tuple(offsets[done:])),
-                jax.ShapeDtypeStruct((rows, query_columns), F32),
-                (places, part, w_query) + (() if total is None else (total,)),
-                near=(1, 2),
-                smem=(0,),
-                flops=2 * part.size * query_columns,
-                read=2 * part.shape[0] * features * query_columns,
+        ahead = tuple(last[cuts[step] : cuts[step + 1]]) if step < 3 else ()
+        outs, args, scratch = [totals], [blocks, w_query], []
+        if step == 0:
+            outs += [shares, shares]
+            args += [key_projection, value_projection]
+            scratch = [pltpu.VMEM(key_projection.shape, BF16), pltpu.VMEM(value_projection.shape, BF16)]
+        else:
+            args.append(total)
+        if ahead:
+            outs.append(pltpu.VMEM((len(ahead), features, query_columns), BF16))
+        got = call(
+            functools.partial(window_kernel, tuple(new), ahead, step == 0),
+            tuple(outs),
+            tuple(args),
+            near=(0,),
+            far=(1, 2, 3) if step == 0 else (1,),
+            scratch=[
+                pltpu.VMEM((len(new), features, query_columns), BF16),
+                pltpu.SemaphoreType.DMA((len(new) + len(ahead) + 2,)),
+                *scratch,
+            ],
+            limit=8 * MIB,
+            flops=2 * rows * len(new) * features * query_columns,
+            read=(len(new) + len(ahead)) * block_bytes,
+        )
+        total = got[0]
+        if step == 0:
+            key_share, value_share = got[1:3]
+        if ahead:
+            fetched.append(got[-1])
+        if bit > 1:
+            blocks = call(
+                join_kernel,
+                jax.ShapeDtypeStruct((2 * len(offsets), rows, features), BF16),
+                (blocks, arrived, total),
             )
-            done = len(offsets)
-        if bit > 1:
-            blocks = jnp.concatenate([blocks, arrived], 0)
-        offsets = offsets + [o ^ bit for o in offsets]
-    half = count // 2
+        new = [o ^ bit for o in offsets]
+        offsets = offsets + new
     sent = held // KEY_VALUE_HEADS if held % KEY_VALUE_HEADS == 0 else held
     message = call(
-        functools.partial(message_kernel, tuple(offsets[half:]), pairs),
+        functools.partial(message_kernel, pairs),
         jax.ShapeDtypeStruct((count, pairs * (sent + 3), HEAD_SIZE), F32),
-        (places, arrived, w_query, total, key_share, value_share, squares),
-        near=(1, 2),
-        smem=(0,),
+        (arrived, total, key_share, value_share, squares, *fetched),
+        near=(0, *range(5, 5 + len(fetched))),
         flops=2 * arrived.size * query_columns,
-        read=2 * half * features * query_columns,
+        read=half * block_bytes,
     )
 
     got = lax.all_to_all(message, "wide", 0, 0, tiled=True)
@@ -260,21 +354,18 @@
             got[:, : pairs * sent].reshape(count, sent, pairs, HEAD_SIZE).reshape(-1, pairs, HEAD_SIZE)
         )
         if held % KEY_VALUE_HEADS:
-            head = place // devices_of_head
+            head = lax.axis_index("wide") // devices_of_head
             query_rows = lax.dynamic_index_in_dim(
                 query_rows.reshape(QUERY_GROUP, KEY_VALUE_HEADS, pairs, HEAD_SIZE), head, 1, False
             )
-    first = (place * pairs) % rows
-    own_lengths = lax.dynamic_slice_in_dim(lengths, first, pairs, 0)
-    index = jnp.arange(HEAD_SIZE, dtype=jnp.int32)
-    rate = ROPE_BASE ** (-(index - index % 2).astype(F32) / HEAD_SIZE)
-    angle = own_lengths.astype(F32)[:, None] * rate[None, :]
+    index = np.arange(HEAD_SIZE)
+    rate = (ROPE_BASE ** (-(index - index % 2) / HEAD_SIZE)).astype(np.float32)[None, :]
     cache_bytes = 2 * slot_key_cache.size
     attended = call(
         functools.partial(attend_kernel, pairs, width),
         jax.ShapeDtypeStruct((pairs, QUERY_GROUP * HEAD_SIZE), BF16),
-        (own_lengths, query_rows, got, jnp.cos(angle), jnp.sin(angle), slot_key_cache, slot_value_cache),
-        near=(5, 6),
+        (lengths, jnp.asarray(rate), query_rows, got, slot_key_cache, slot_value_cache),
+        near=(4, 5),
         smem=(0,),
         scratch=(pltpu.VMEM((pairs, QUERY_GROUP * HEAD_SIZE), F32),),
         limit=8 * MIB,
@@ -296,9 +387,8 @@
     return call(
         functools.partial(project_kernel, pairs, tuple(head_offsets), tuple(slot_offsets)),
         jax.ShapeDtypeStruct((rows, output_projection.shape[1]), BF16),
-        (places, slot_of_row.reshape(rows, 1), mine, other, output_projection),
-        near=(4,),
-        smem=(0,),
+        (slot_of_row.reshape(1, rows), mine, other, output_projection),
+        near=(3,),
         scratch=(pltpu.VMEM((rows, output_projection.shape[0]), BF16),),
         flops=2 * rows * output_projection.size,
         read=2 * output_projection.size,

time: 83 us -> 57.6 us (0.69)
  local copies, waits for them, and re-layouts: 25.7 us -> 0.06 us
  waiting for transfers between devices: 29.6 us -> 15.1 us
  blocking collectives: 0 us -> 13.8 us
  Pallas kernels: 11.5 us -> 20 us
  starting transfers between devices: 14.5 us -> 8.1 us
  other arithmetic: 1.06 us -> 0.15 us
    unnamed x20 -> x18, local copies, waits for them, and re-layouts: 24.9 us -> 0.06 us
    all_to_all x0 -> x1, blocking collectives: none -> 13.8 us  [body(): got = lax.all_to_all(message, 'wide', 0, 0, tiled=True)]
    pallas_call x7 -> x11, Pallas kernels: 11.5 us -> 20 us  [call(): pl.pallas_call(kernel, out_shape=out_shape, in_specs=specs, out_specs=jax...]
    all_to_all x1 -> x0, waiting for transfers between devices: 7.81 us -> none  [body(): got = lax.all_to_all(message, 'wide', 0, 0, tiled=True)]
    ppermute x8, waiting for transfers between devices: 21.8 us -> 15.1 us  [swap(): return lax.ppermute(array, 'wide', [(i, i ^ bit) for i in range(count)])]
    all_to_all x1 -> x0, starting transfers between devices: 6.24 us -> none  [body(): got = lax.all_to_all(message, 'wide', 0, 0, tiled=True)]
  transfers between devices with their start and end apart: 9 -> 8, of which waited for: 8 -> 6; matrix products, arithmetic and copies ran while one was open for 1% -> 0% of each run, Pallas kernels for 2% -> 17%
where the time goes in v2:
time: 57.6 us; the launch traced here: 57.4 us
  Pallas kernels  20 us (35%)
  waiting for transfers between devices  15.1 us (26%)
  blocking collectives  13.8 us (24%)
  starting transfers between devices  8.1 us (14%)
    pallas_call x11, Pallas kernels, call(): pl.pallas_call(kernel, out_shape=out_shape, in_specs=specs, out_specs=jax...  20 us
    ppermute x8, waiting for transfers between devices, swap(): return lax.ppermute(array, 'wide', [(i, i ^ bit) for i in range(count)])  15.1 us
    all_to_all x1, blocking collectives, body(): got = lax.all_to_all(message, 'wide', 0, 0, tiled=True)  13.8 us
    ppermute x8, starting transfers between devices, swap(): return lax.ppermute(array, 'wide', [(i, i ^ bit) for i in range(count)])  8.1 us
  transfers between devices with their start and end apart: 8, of which 6 were waited for; matrix products, arithmetic and copies ran while one was open for 0% of the time, Pallas kernels for 17%

profile of v2, /device:TPU:0, one launch (start us, length us, event | category | flops | bytes accessed | tf_op | source)
XLA Modules:
  0.0 57.4 jit_solution(17962600334932625516)
XLA Ops:
  0.0 1.0 %shard_map.109 = (bf16[16,1024]{1,0:T(8,128)(2,1)S(1)}, f32[16,128]{1,0:T(8,128)S(1)}) custom-call(bf16[16,1024]{1,0:T(8,128)(2,1)} %far_tokens.1, bf16[1024]{0:T(1024)(128)(2,1)} %far_gain.1, s32[1,16]{1,0:T(1,128)} %bitcast.12), custom_call_target="tpu_custom_call" | custom-call | tf_op jit(solution)/shard_map/pallas_call | solution.py:35
  1.0 4.1 %collective-permute-start = (bf16[1,16,1024]{2,1,0:T(8,128)(2,1)S(1)}, bf16[1,16,1024]{2,1,0:T(8,128)(2,1)S(1)}, u32[]{:S(2)}, u32[]{:S(2)}) collective-permute-start(bf16[1,16,1024]{2,1,0:T(8,128)(2,1)S(1)} %bitcast.9), channel_id=1, source_target_pairs={{0,8},{1,9},{2,10},{3,11},{4,12},{5,13},{6,14},{7,15},{8,0},{9,1},... | collective-permute-start | bytes 98312 | tf_op jit(solution)/shard_map/ppermute | solution.py:249
  5.1 2.5 %shard_map.110 = (f32[16,512]{1,0:T(8,128)S(1)}, f32[16,512]{1,0:T(8,128)S(1)}, f32[16,512]{1,0:T(8,128)S(1)}, bf16[2,1024,512]{2,1,0:T(8,128)(2,1)S(1)}) custom-call(bf16[1,16,1024]{2,1,0:T(8,128)(2,1)S(1)} %bitcast.10, bf16[16384,512]{1,0:T(8,128)(2,1)} %weight_ref.8, bf16[1024,512]{1,0:T(8,128)(2,1)} %refs_0_.1, bf16[1024,512]{1,0:T(8,128)(2,1)} %refs_1_.1), custom_call_target="tpu_custom_call" | custom-call | flops 16777216 | bytes 3145728 | tf_op jit(solution)/shard_map/pallas_call | solution.py:35
  7.7 0.0 collective-permute-done.arrived_ref
  7.7 1.6 %collective-permute-start.1 = (bf16[2,16,1024]{2,1,0:T(8,128)(2,1)S(1)}, bf16[2,16,1024]{2,1,0:T(8,128)(2,1)S(1)}, u32[]{:S(2)}, u32[]{:S(2)}) collective-permute-start(bf16[2,16,1024]{2,1,0:T(8,128)(2,1)S(1)} %shard_map.111.blocks_ref.mine_ref), channel_id=1, source_target_pairs={{0,4},{1,5},{2,6},{3,7},{4,0},{5,1},{6,2},{7,3},{8,12},{9,13},{10,... | collective-permute-start | bytes 196616 | tf_op jit(solution)/shard_map/ppermute | solution.py:249
  9.3 2.5 %shard_map.112 = (f32[16,512]{1,0:T(8,128)S(1)}, bf16[4,1024,512]{2,1,0:T(8,128)(2,1)S(1)}) custom-call(bf16[2,16,1024]{2,1,0:T(8,128)(2,1)S(1)} %shard_map.111.blocks_ref.mine_ref, bf16[16384,512]{1,0:T(8,128)(2,1)} %weight_ref.8, f32[16,512]{1,0:T(8,128)S(1)} %get-tuple-element.16.after_ref.refs_0_), custom_call_target="tpu_custom_call" | custom-call | flops 16777216 | bytes 5242880 | tf_op jit(solution)/shard_map/pallas_call | solution.py:35
  11.9 0.1 collective-permute-done.1.arrived_ref
  12.0 1.6 %collective-permute-start.2 = (bf16[4,16,1024]{2,1,0:T(8,128)(2,1)S(1)}, bf16[4,16,1024]{2,1,0:T(8,128)(2,1)S(1)}, u32[]{:S(2)}, u32[]{:S(2)}) collective-permute-start(bf16[4,16,1024]{2,1,0:T(8,128)(2,1)S(1)} %shard_map.113.blocks_ref.mine_ref), channel_id=1, source_target_pairs={{0,2},{1,3},{2,0},{3,1},{4,6},{5,7},{6,4},{7,5},{8,10},{9,11},{10,... | collective-permute-start | bytes 393224 | tf_op jit(solution)/shard_map/ppermute | solution.py:249
  13.6 2.2 %shard_map.114 = (f32[16,512]{1,0:T(8,128)S(1)}, bf16[2,1024,512]{2,1,0:T(8,128)(2,1)S(1)}) custom-call(bf16[4,16,1024]{2,1,0:T(8,128)(2,1)S(1)} %shard_map.113.blocks_ref.mine_ref, bf16[16384,512]{1,0:T(8,128)(2,1)} %weight_ref.8, f32[16,512]{1,0:T(8,128)S(1)} %get-tuple-element.17.after_ref.refs_0_), custom_call_target="tpu_custom_call" | custom-call | flops 33554432 | bytes 4194304 | tf_op jit(solution)/shard_map/pallas_call | solution.py:35
  15.9 1.2 %collective-permute-done.2.arrived_ref = bf16[4,16,1024]{2,1,0:T(8,128)(2,1)S(1)} collective-permute-done((bf16[4,16,1024]{2,1,0:T(8,128)(2,1)S(1)}, bf16[4,16,1024]{2,1,0:T(8,128)(2,1)S(1)}, u32[]{:S(2)}, u32[]{:S(2)}) %collective-permute-start.2) | collective-permute-done | bytes 131104 | tf_op jit(solution)/shard_map/ppermute | solution.py:249
  17.1 0.1 collective-permute-start.3
  17.2 0.0 copy-start.1
  17.2 0.0 slice-start
  17.2 0.0 slice-start.1
  17.2 2.6 %shard_map.116.total_ref = f32[16,512]{1,0:T(8,128)S(1)} custom-call(bf16[8,16,1024]{2,1,0:T(8,128)(2,1)S(1)} %shard_map.115.blocks_ref, bf16[16384,512]{1,0:T(8,128)(2,1)} %weight_ref.8, f32[16,512]{1,0:T(8,128)S(1)} %get-tuple-element.18.after_ref.refs_0_), custom_call_target="tpu_custom_call" | custom-call | flops 67108864 | bytes 4194304 | tf_op jit(solution)/shard_map/pallas_call | solution.py:35
  19.8 0.0 collective-permute-done.3.blocks_ref
  19.9 0.0 copy-start
  19.9 0.0 copy-start.3
  19.9 0.0 copy-start.4
  19.9 0.0 slice-start.2
  19.9 1.2 %shard_map.117 = f32[16,16,128]{2,1,0:T(8,128)S(1)} custom-call(bf16[8,16,1024]{2,1,0:T(8,128)(2,1)S(1)} %collective-permute-done.3.blocks_ref, f32[16,512]{1,0:T(8,128)S(1)} %shard_map.116.total_ref, f32[16,512]{1,0:T(8,128)S(1)} %get-tuple-element.19.key_ref, f32[16,512]{1,0:T(8,128)S(1)} %get-tuple-element.20.value_ref, ...), custom_call_target="tpu_custom_call" | custom-call | flops 134217728 | bytes 8388608 | tf_op jit(solution)/shard_map/pallas_call | solution.py:35
  21.1 13.8 %all_to_all.5.query_ref.rest_ref = f32[16,16,128]{2,1,0:T(8,128)S(1)} all-to-all(f32[16,16,128]{2,1,0:T(8,128)S(1)} %shard_map.117), channel_id=1, replica_groups=mesh['groups'=2,'wide'=16] {'wide'}, dimensions={0} | all-to-all | bytes 262144 | tf_op jit(solution)/shard_map/all_to_all | solution.py:349
  34.9 0.0 copy-done.1
  34.9 0.0 copy-done
  34.9 0.0 copy-done.3
  34.9 0.0 copy-done.4
  35.0 0.0 slice-start.3
  35.0 0.0 copy-start.2
  35.0 3.7 %shard_map.118 = bf16[4,2048]{1,0:T(4,128)(2,1)S(1)} custom-call(s32[16]{0:T(128)S(1)} %copy-done.3, f32[1,128]{1,0:T(1,128)S(1)} %copy-done.4, f32[16,16,128]{2,1,0:T(8,128)S(1)} %all_to_all.5.query_ref.rest_ref, f32[16,16,128]{2,1,0:T(8,128)S(1)} %all_to_all.5.query_ref.rest_ref, bf16[4,4096,128]{2,1,0:T(8,128)(2,1)S(1)} %copy-done, ...), custom_call_target="tpu_custom_call" | custom-call | flops 134217728 | bytes 8388608 | tf_op jit(solution)/shard_map/pallas_call | solution.py:35
  38.7 0.5 collective-permute-start.4
  39.2 4.2 %collective-permute-done.4 = bf16[1,4,2048]{2,1,0:T(4,128)(2,1)S(1)} collective-permute-done((bf16[1,4,2048]{2,1,0:T(4,128)(2,1)S(1)}, bf16[1,4,2048]{2,1,0:T(4,128)(2,1)S(1)}, u32[]{:S(2)}, u32[]{:S(2)}) %collective-permute-start.4) | collective-permute-done | bytes 16416 | tf_op jit(solution)/shard_map/ppermute | solution.py:249
  43.4 0.1 collective-permute-start.5
  43.5 3.9 %collective-permute-done.5 = bf16[2,4,2048]{2,1,0:T(4,128)(2,1)S(1)} collective-permute-done((bf16[2,4,2048]{2,1,0:T(4,128)(2,1)S(1)}, bf16[2,4,2048]{2,1,0:T(4,128)(2,1)S(1)}, u32[]{:S(2)}, u32[]{:S(2)}) %collective-permute-start.5) | collective-permute-done | bytes 32800 | tf_op jit(solution)/shard_map/ppermute | solution.py:249
  47.4 0.1 pad_maximum_fusion.1
  47.4 0.1 collective-permute-start.6
  47.5 4.3 %collective-permute-done.6 = bf16[4,4,2048]{2,1,0:T(4,128)(2,1)S(1)} collective-permute-done((bf16[4,4,2048]{2,1,0:T(4,128)(2,1)S(1)}, bf16[4,4,2048]{2,1,0:T(4,128)(2,1)S(1)}, u32[]{:S(2)}, u32[]{:S(2)}) %collective-permute-start.6) | collective-permute-done | bytes 65568 | tf_op jit(solution)/shard_map/ppermute | solution.py:249
  51.8 0.1 pad_maximum_fusion.mine_ref
  51.8 0.1 collective-permute-start.7
  51.9 1.3 %collective-permute-done.7.other_ref = bf16[4,8,2048]{2,1,0:T(8,128)(2,1)S(1)} collective-permute-done((bf16[4,8,2048]{2,1,0:T(8,128)(2,1)S(1)}, bf16[4,8,2048]{2,1,0:T(8,128)(2,1)S(1)}, u32[]{:S(2)}, u32[]{:S(2)}) %collective-permute-start.7) | collective-permute-done | bytes 131104 | tf_op jit(solution)/shard_map/ppermute | solution.py:249
  53.3 0.0 slice-done
  53.3 0.0 slice-done.1
  53.3 0.0 slice-done.2
  53.3 0.0 slice-done.3
  53.3 0.0 copy-done.2
  53.3 4.1 %shard_map.119 = bf16[16,1024]{1,0:T(8,128)(2,1)} custom-call(s32[1,16]{1,0:T(1,128)S(1)} %bitcast.13, bf16[4,8,2048]{2,1,0:T(8,128)(2,1)S(1)} %pad_maximum_fusion.mine_ref, bf16[4,8,2048]{2,1,0:T(8,128)(2,1)S(1)} %collective-permute-done.7.other_ref, bf16[8192,1024]{1,0:T(8,128)(2,1)S(1)} %bitcast.4), custom_call_target="tpu_custom_call" | custom-call | flops 268435456 | bytes 16777216 | tf_op jit(solution)/shard_map/pallas_call | solution.py:35
  (5 shorter events, 0.1 us)
Async XLA Ops:
  1.0 6.6 %collective-permute-start = (bf16[1,16,1024]{2,1,0:T(8,128)(2,1)S(1)}, bf16[1,16,1024]{2,1,0:T(8,128)(2,1)S(1)}, u32[]{:S(2)}, u32[]{:S(2)}) collective-permute-start(bf16[1,16,1024]{2,1,0:T(8,128)(2,1)S(1)} %bitcast.9), channel_id=1, source_target_pairs={{0,8},{1,9},{2,10},{3,11},{4,12},{5,13},{6,14},{7,15},{8,0},{9,1},... | collective-permute-start | bytes 98312 | tf_op jit(solution)/shard_map/ppermute | solution.py:249
  7.7 4.3 %collective-permute-start.1 = (bf16[2,16,1024]{2,1,0:T(8,128)(2,1)S(1)}, bf16[2,16,1024]{2,1,0:T(8,128)(2,1)S(1)}, u32[]{:S(2)}, u32[]{:S(2)}) collective-permute-start(bf16[2,16,1024]{2,1,0:T(8,128)(2,1)S(1)} %shard_map.111.blocks_ref.mine_ref), channel_id=1, source_target_pairs={{0,4},{1,5},{2,6},{3,7},{4,0},{5,1},{6,2},{7,3},{8,12},{9,13},{10,... | collective-permute-start | bytes 196616 | tf_op jit(solution)/shard_map/ppermute | solution.py:249
  12.0 5.0 %collective-permute-start.2 = (bf16[4,16,1024]{2,1,0:T(8,128)(2,1)S(1)}, bf16[4,16,1024]{2,1,0:T(8,128)(2,1)S(1)}, u32[]{:S(2)}, u32[]{:S(2)}) collective-permute-start(bf16[4,16,1024]{2,1,0:T(8,128)(2,1)S(1)} %shard_map.113.blocks_ref.mine_ref), channel_id=1, source_target_pairs={{0,2},{1,3},{2,0},{3,1},{4,6},{5,7},{6,4},{7,5},{8,10},{9,11},{10,... | collective-permute-start | bytes 393224 | tf_op jit(solution)/shard_map/ppermute | solution.py:249
  17.1 2.8 %collective-permute-start.3 = (bf16[8,16,1024]{2,1,0:T(8,128)(2,1)S(1)}, bf16[8,16,1024]{2,1,0:T(8,128)(2,1)S(1)}, u32[]{:S(2)}, u32[]{:S(2)}) collective-permute-start(bf16[8,16,1024]{2,1,0:T(8,128)(2,1)S(1)} %shard_map.115.blocks_ref), channel_id=1, source_target_pairs={{0,1},{1,0},{2,3},{3,2},{4,5},{5,4},{6,7},{7,6},{8,9},{9,8},{10,11... | collective-permute-start | bytes 786440 | tf_op jit(solution)/shard_map/ppermute | solution.py:249
  17.2 17.8 %copy-start.1 = (bf16[4,4096,128]{2,1,0:T(8,128)(2,1)S(1)}, bf16[4,4096,128]{2,1,0:T(8,128)(2,1)}, u32[]{:S(2)}) copy-start(bf16[4,4096,128]{2,1,0:T(8,128)(2,1)} %values_ref.1) | copy-start | bytes 12582916
  17.2 36.1 %slice-start = ((s8[16777216]{0:T(1024)(128)(4,1)}), s8[4194304]{0:T(1024)(128)(4,1)S(1)}, s32[]{:S(2)}) async-start(s8[16777216]{0:T(1024)(128)(4,1)} %bitcast.3), calls=%async_computation.1 | async-start | bytes 8388608
  17.2 36.1 %slice-start.1 = ((s8[16777216]{0:T(1024)(128)(4,1)}), s8[4194304]{0:T(1024)(128)(4,1)S(1)}, s32[]{:S(2)}) async-start(s8[16777216]{0:T(1024)(128)(4,1)} %bitcast.3), calls=%async_computation.2 | async-start | bytes 8388608
  19.9 15.1 %copy-start = (bf16[4,4096,128]{2,1,0:T(8,128)(2,1)S(1)}, bf16[4,4096,128]{2,1,0:T(8,128)(2,1)}, u32[]{:S(2)}) copy-start(bf16[4,4096,128]{2,1,0:T(8,128)(2,1)} %keys_ref.1) | copy-start | bytes 12582916
  19.9 15.1 %copy-start.3 = (s32[16]{0:T(128)S(1)}, s32[16]{0:T(128)}, u32[]{:S(2)}) copy-start(s32[16]{0:T(128)} %lengths_ref.1) | copy-start | bytes 196
  19.9 15.1 %copy-start.4 = (f32[1,128]{1,0:T(1,128)S(1)}, f32[1,128]{1,0:T(1,128)}, u32[]{:S(2)}) copy-start(f32[1,128]{1,0:T(1,128)} %constant.2.clone.rate_ref) | copy-start | bytes 1540
  19.9 33.4 %slice-start.2 = ((s8[16777216]{0:T(1024)(128)(4,1)}), s8[4194304]{0:T(1024)(128)(4,1)S(1)}, s32[]{:S(2)}) async-start(s8[16777216]{0:T(1024)(128)(4,1)} %bitcast.3), calls=%async_computation.3 | async-start | bytes 8388608
  35.0 18.3 %slice-start.3 = ((s8[16777216]{0:T(1024)(128)(4,1)}), s8[4194304]{0:T(1024)(128)(4,1)S(1)}, s32[]{:S(2)}) async-start(s8[16777216]{0:T(1024)(128)(4,1)} %bitcast.3), calls=%async_computation.4 | async-start | bytes 8388608
  35.0 18.3 %copy-start.2 = (s32[16]{0:T(128)S(1)}, s32[16]{0:T(128)}, u32[]{:S(2)}) copy-start(s32[16]{0:T(128)} %param.13) | copy-start | bytes 196
  38.7 4.7 %collective-permute-start.4 = (bf16[1,4,2048]{2,1,0:T(4,128)(2,1)S(1)}, bf16[1,4,2048]{2,1,0:T(4,128)(2,1)S(1)}, u32[]{:S(2)}, u32[]{:S(2)}) collective-permute-start(bf16[1,4,2048]{2,1,0:T(4,128)(2,1)S(1)} %bitcast.5), channel_id=1, source_target_pairs={{0,8},{1,9},{2,10},{3,11},{4,12},{5,13},{6,14},{7,15},{8,0},{9,1},... | collective-permute-start | bytes 49160 | tf_op jit(solution)/shard_map/ppermute | solution.py:249
  43.4 4.0 %collective-permute-start.5 = (bf16[2,4,2048]{2,1,0:T(4,128)(2,1)S(1)}, bf16[2,4,2048]{2,1,0:T(4,128)(2,1)S(1)}, u32[]{:S(2)}, u32[]{:S(2)}) collective-permute-start(bf16[2,4,2048]{2,1,0:T(4,128)(2,1)S(1)} %pad_maximum_fusion.2), channel_id=1, source_target_pairs={{0,4},{1,5},{2,6},{3,7},{4,0},{5,1},{6,2},{7,3},{8,12},{9,13},{10,... | collective-permute-start | bytes 98312 | tf_op jit(solution)/shard_map/ppermute | solution.py:249
  47.4 4.3 %collective-permute-start.6 = (bf16[4,4,2048]{2,1,0:T(4,128)(2,1)S(1)}, bf16[4,4,2048]{2,1,0:T(4,128)(2,1)S(1)}, u32[]{:S(2)}, u32[]{:S(2)}) collective-permute-start(bf16[4,4,2048]{2,1,0:T(4,128)(2,1)S(1)} %pad_maximum_fusion.1), channel_id=1, source_target_pairs={{0,2},{1,3},{2,0},{3,1},{4,6},{5,7},{6,4},{7,5},{8,10},{9,11},{10,... | collective-permute-start | bytes 196616 | tf_op jit(solution)/shard_map/ppermute | solution.py:249
  51.8 1.4 %collective-permute-start.7 = (bf16[4,8,2048]{2,1,0:T(8,128)(2,1)S(1)}, bf16[4,8,2048]{2,1,0:T(8,128)(2,1)S(1)}, u32[]{:S(2)}, u32[]{:S(2)}) collective-permute-start(bf16[4,8,2048]{2,1,0:T(8,128)(2,1)S(1)} %pad_maximum_fusion.mine_ref), channel_id=1, source_target_pairs={{0,1},{1,0},{2,3},{3,2},{4,5},{5,4},{6,7},{7,6},{8,9},{9,8},{10,11... | collective-permute-start | bytes 393224 | tf_op jit(solution)/shard_map/ppermute | solution.py:249

commit v3 on v1

v3 whole, which is shorter than its diff:
```python
import functools
import math

import jax
import jax.numpy as jnp
import numpy as np
from jax import lax
from jax.experimental import pallas as pl
from jax.experimental.pallas import tpu as pltpu
from jax.sharding import PartitionSpec as P

QUERY_HEADS = 64
KEY_VALUE_HEADS = 4
HEAD_SIZE = 128
QUERY_GROUP = QUERY_HEADS // KEY_VALUE_HEADS

EPS = 1e-05
ROPE_BASE = 500000.0
MIB = 1 << 20
F32 = jnp.float32
BF16 = jnp.bfloat16


def call(kernel, out_shape, args, near=(), far=(), smem=(), scratch=(), limit=4 * MIB, flops=0, read=0):
    operands, specs = [], []
    for i, arg in enumerate(args):
        space = pltpu.SMEM if i in smem else pltpu.VMEM
        if i in near:
            arg = pltpu.with_memory_space_constraint(arg, pltpu.VMEM)
        if i in far:
            arg = pltpu.with_memory_space_constraint(arg, pltpu.HBM)
            space = pltpu.HBM
        operands.append(arg)
        specs.append(pl.BlockSpec(memory_space=space))
    return pl.pallas_call(
        kernel,
        out_shape=out_shape,
        in_specs=specs,
        out_specs=jax.tree.map(lambda _: pl.BlockSpec(memory_space=pltpu.VMEM), out_shape),
        scratch_shapes=list(scratch),
        compiler_params=pltpu.CompilerParams(vmem_limit_bytes=limit),
        cost_estimate=pl.CostEstimate(flops=flops, bytes_accessed=read, transcendentals=0),
    )(*operands)


def prepare_kernel(far_tokens, far_gain, far_slot, scaled_ref, squares_ref, tokens_ref, gain_ref, slot_ref, sems):
    copies = [
        pltpu.make_async_copy(far, near, sems.at[i])
        for i, (far, near) in enumerate(
            ((far_tokens, tokens_ref), (far_gain, gain_ref), (far_slot, slot_ref))
        )
    ]
    for copy in copies:
        copy.start()
    for copy in copies:
        copy.wait()
    rows, features = tokens_ref.shape
    wide_f = tokens_ref[...].astype(F32)
    squares = jnp.sum(wide_f * wide_f, axis=1, keepdims=True)
    gain = gain_ref[...].astype(F32).reshape(1, features)
    scaled = (wide_f * gain).astype(BF16)
    picked = lax.broadcasted_iota(jnp.int32, (rows, rows), 0) == slot_ref[...]
    scaled_ref[...] = jnp.dot(
        picked.astype(BF16), scaled, preferred_element_type=F32
    ).astype(BF16)
    turned = jnp.sum(jnp.where(picked, jnp.transpose(jnp.broadcast_to(squares, (rows, rows))), 0.0), axis=1, keepdims=True)
    squares_ref[...] = jnp.broadcast_to(turned, squares_ref.shape)


def join_kernel(mine_ref, arrived_ref, after_ref, joined_ref):
    count = mine_ref.shape[0]
    joined_ref[:count] = mine_ref[...]
    joined_ref[count:] = arrived_ref[...]


def share_kernel(scaled_ref, far_key, far_value, far_query, key_share_ref, value_share_ref, key_ref, value_ref, sems):
    copies = [
        pltpu.make_async_copy(far_key, key_ref, sems.at[0]),
        pltpu.make_async_copy(far_value, value_ref, sems.at[1]),
    ]
    for copy in copies:
        copy.start()
    copies[0].wait()
    key_share_ref[...] = jnp.dot(scaled_ref[...], key_ref[...], preferred_element_type=F32)
    copies[1].wait()
    value_share_ref[...] = jnp.dot(scaled_ref[...], value_ref[...], preferred_element_type=F32)


def products(offsets, first, blocks_ref, weight_ref, total):
    features = blocks_ref.shape[2]
    place = lax.axis_index("wide")
    for k, offset in enumerate(offsets):
        start = pl.multiple_of((place ^ offset) * features, features)
        total = total + jnp.dot(
            blocks_ref[first + k], weight_ref[pl.ds(start, features), :], preferred_element_type=F32
        )
    return total


def query_kernel(offsets, first, blocks_ref, weight_ref, total_ref, out_ref):
    out_ref[...] = products(offsets, first, blocks_ref, weight_ref, total_ref[...])


def query_turns_kernel(offsets, pairs, blocks_ref, weight_ref, lengths_ref, rate_ref, out_ref, turns_ref):
    out_ref[...] = products(offsets, 0, blocks_ref, weight_ref, jnp.zeros(out_ref.shape, F32))
    own = (lax.axis_index("wide") * pairs) % lengths_ref.shape[0]
    positions = jnp.concatenate(
        [jnp.full((1, HEAD_SIZE), lengths_ref[own + i], jnp.int32) for i in range(pairs)], 0
    )
    angle = positions.astype(F32) * rate_ref[...]
    turns_ref[0] = jnp.cos(angle)
    turns_ref[1] = jnp.sin(angle)


def message_kernel(
    offsets, pairs, blocks_ref, weight_ref, total_ref, key_ref, value_ref, squares_ref, message_ref
):
    query = products(offsets, 0, blocks_ref, weight_ref, total_ref[...])
    rows = query.shape[0]
    held = query.shape[1] // HEAD_SIZE
    for target in range(message_ref.shape[0]):
        head, first = target * pairs // rows, target * pairs % rows
        slots = slice(first, first + pairs)
        columns = slice(head * HEAD_SIZE, (head + 1) * HEAD_SIZE)
        sent = range(head, held, KEY_VALUE_HEADS) if held % KEY_VALUE_HEADS == 0 else range(held)
        at = 0
        for j in sent:
            message_ref[target, at : at + pairs, :] = query[slots, j * HEAD_SIZE : (j + 1) * HEAD_SIZE]
            at += pairs
        message_ref[target, at : at + pairs, :] = key_ref[slots, columns]
        message_ref[target, at + pairs : at + 2 * pairs, :] = value_ref[slots, columns]
        message_ref[target, at + 2 * pairs : at + 3 * pairs, :] = squares_ref[slots, :]


def rotated(values, cosines, sines):
    even = lax.broadcasted_iota(jnp.int32, values.shape, 1) % 2 == 0
    swapped = jnp.where(
        even, -pltpu.roll(values, HEAD_SIZE - 1, 1), pltpu.roll(values, 1, 1)
    )
    return values * cosines + swapped * sines


def side_by_side(ref, members, start, size):
    parts = [ref[i, start : start + size, :] for i in members]
    return parts[0] if len(parts) == 1 else jnp.concatenate(parts, axis=1)


def folded(op, array):
    tiles = [array[:, at : at + HEAD_SIZE] for at in range(0, array.shape[1], HEAD_SIZE)]
    while len(tiles) > 1:
        tiles = [op(*tiles[k : k + 2]) if k + 1 < len(tiles) else tiles[k] for k in range(0, len(tiles), 2)]
    return tiles[0]


def attend_kernel(
    pairs, width, lengths_ref, turns_ref, query_ref, rest_ref, keys_ref, values_ref, out_ref, scores_ref, wide_ref
):
    group = query_ref.shape[0]
    length = keys_ref.shape[1]
    first = (lax.axis_index("wide") * pairs) % lengths_ref.shape[0]
    at = rest_ref.shape[1] - 3 * pairs
    summed = jnp.sum(rest_ref[:, at:, :], axis=0)
    score_scale = 1.0 / math.sqrt(HEAD_SIZE)
    step = math.gcd(length, 512)
    many = 2 if pairs % 2 == 0 else 1
    parts = []
    for base in range(0, pairs, many):
        members = range(base, base + many)
        queries, owns, values, limits = [], [], [], []
        for i in members:
            scale = lax.rsqrt(summed[2 * pairs + i : 2 * pairs + i + 1, :] * (1.0 / width) + EPS)
            cosines, sines = turns_ref[0, i : i + 1, :], turns_ref[1, i : i + 1, :]
            query = rotated(query_ref[:, i, :] * scale, cosines, sines).astype(BF16)
            key = jnp.broadcast_to(summed[i : i + 1, :] * scale, (8, HEAD_SIZE))
            key = rotated(key, cosines, sines)[0:1, :].astype(BF16).astype(F32)
            values.append((summed[pairs + i : pairs + i + 1, :] * scale).astype(BF16).astype(F32))
            owns.append(jnp.sum(query.astype(F32) * key, axis=1, keepdims=True))
            limits.append(jnp.full((group, step), lengths_ref[first + i], jnp.int32))
            blank = jnp.zeros_like(query)
            queries.append(
                query
                if many == 1
                else jnp.concatenate([query if j == i else blank for j in members], axis=1)
            )
        stacked = jnp.concatenate(queries, axis=0)
        own = jnp.concatenate(owns, axis=0)
        limit = jnp.concatenate(limits, axis=0)
        column = lax.broadcasted_iota(jnp.int32, (many * group, step), 1)
        tops = jnp.broadcast_to(own, (many * group, HEAD_SIZE))
        place = base // many
        for start in range(0, length, step):
            scores = lax.dot_general(
                stacked,
                side_by_side(keys_ref, members, start, step),
                (((1,), (1,)), ((), ())),
                preferred_element_type=F32,
            )
            scores = jnp.where(column < limit - start, scores, -jnp.inf)
            scores_ref[place, :, start : start + step] = scores
            tops = jnp.maximum(tops, folded(jnp.maximum, scores))
        parts.append((members, place, own, tops, values))
    factor = score_scale * math.log2(math.e)
    weighed = []
    for members, place, own, tops, values in parts:
        top = jnp.max(tops, axis=1, keepdims=True)
        own_w = jnp.exp2((own - top) * factor)
        sums = jnp.zeros_like(tops)
        for start in range(0, length, step):
            weights = jnp.exp2((scores_ref[place, :, start : start + step] - top) * factor)
            scores_ref[place, :, start : start + step] = weights
            sums = sums + folded(jnp.add, weights)
        share = 1.0 / (own_w + jnp.sum(sums, axis=1, keepdims=True))
        weighed.append((members, place, share, (own_w * share).astype(BF16).astype(F32), values))
    for members, place, share, own_p, values in weighed:
        blended = jnp.zeros((many * group, many * HEAD_SIZE), F32)
        for start in range(0, length, step):
            blended = blended + jnp.dot(
                (scores_ref[place, :, start : start + step] * share).astype(BF16),
                side_by_side(values_ref, members, start, step),
                preferred_element_type=F32,
            )
        for k, i in enumerate(members):
            rows = slice(k * group, (k + 1) * group)
            result = blended[rows, k * HEAD_SIZE : (k + 1) * HEAD_SIZE] + own_p[rows] * values[k]
            for g in range(group):
                wide_ref[i : i + 1, g * HEAD_SIZE : (g + 1) * HEAD_SIZE] = result[g : g + 1, :]
    out_ref[...] = wide_ref[...].astype(BF16)


def place_rows(pairs, head_offsets, slot_offsets, slot_ref, pieces, left_ref, before_ref=None):
    rows = left_ref.shape[0]
    heads, held, _ = pieces[0].shape
    devices_of_head = rows // pairs
    place = lax.axis_index("wide")
    group_place = place % devices_of_head
    head_place = place // devices_of_head
    slot_of_row = jnp.transpose(jnp.broadcast_to(slot_ref[...], (rows, rows)))[:, 0:1]
    position = lax.broadcasted_iota(jnp.int32, (rows, held), 1)
    picks = []
    for offsets in slot_offsets:
        device = jnp.zeros_like(position)
        for k, offset in enumerate(offsets):
            device = jnp.where(position // pairs == k, group_place ^ offset, device)
        picks.append((slot_of_row == device * pairs + position % pairs).astype(BF16))
    for z, offset in enumerate(head_offsets):
        head = head_place ^ offset
        ordered = sum(
            jnp.dot(pick, piece[z], preferred_element_type=F32) for pick, piece in zip(picks, pieces)
        ).astype(BF16)
        for g in range(QUERY_GROUP):
            start = pl.multiple_of((g * heads + head) * HEAD_SIZE, HEAD_SIZE)
            columns = ordered[:, g * HEAD_SIZE : (g + 1) * HEAD_SIZE]
            if before_ref is not None:
                columns = columns + before_ref[:, pl.ds(start, HEAD_SIZE)]
            left_ref[:, pl.ds(start, HEAD_SIZE)] = columns


def assemble_kernel(pairs, head_offsets, slot_offsets, slot_ref, *refs):
    place_rows(pairs, head_offsets, slot_offsets, slot_ref, refs[:-1], refs[-1])


def project_kernel(
    pairs, head_offsets, slot_offsets, slot_ref, piece_ref, before_ref, weight_ref, out_ref, left_ref
):
    place_rows(pairs, head_offsets, slot_offsets, slot_ref, (piece_ref,), left_ref, before_ref)
    out_ref[...] = jnp.dot(
        left_ref[...], weight_ref[...], preferred_element_type=F32
    ).astype(BF16)


def swap(array, bit, count):
    return lax.ppermute(array, "wide", [(i, i ^ bit) for i in range(count)])


def body(
    count,
    tokens,
    norm_gain,
    slot_of_row,
    lengths,
    w_query,
    key_projection,
    value_projection,
    output_projection,
    slot_key_cache,
    slot_value_cache,
):
    rows, features = tokens.shape
    pairs = slot_key_cache.shape[0]
    width = w_query.shape[0]
    query_columns = w_query.shape[1]
    held = query_columns // HEAD_SIZE
    devices_of_head = rows // pairs
    bits = [1 << b for b in reversed(range(count.bit_length() - 1))]

    scaled, squares = call(
        prepare_kernel,
        (
            jax.ShapeDtypeStruct((rows, features), BF16),
            jax.ShapeDtypeStruct((rows, HEAD_SIZE), F32),
        ),
        (tokens, norm_gain, slot_of_row.reshape(1, rows)),
        far=(0, 1, 2),
        scratch=(
            pltpu.VMEM((rows, features), BF16),
            pltpu.VMEM((features,), BF16),
            pltpu.VMEM((1, rows), jnp.int32),
            pltpu.SemaphoreType.DMA((3,)),
        ),
    )

    index = np.arange(HEAD_SIZE)
    rate = (ROPE_BASE ** (-(index - index % 2) / HEAD_SIZE)).astype(np.float32)[None, :]
    totals = jax.ShapeDtypeStruct((rows, query_columns), F32)
    shares = jax.ShapeDtypeStruct((rows, key_projection.shape[1]), F32)

    def query(offsets, first, array, total):
        return call(
            functools.partial(query_kernel, tuple(offsets), first),
            totals,
            (array, w_query, total),
            near=(0, 1),
            flops=2 * rows * len(offsets) * features * query_columns,
            read=2 * len(offsets) * features * query_columns,
        )

    *outer, bit, core = bits
    blocks, offsets, new, total = scaled[None], [0], [0], None
    for far in (*outer, bit):
        arrived = swap(blocks, far, count)
        if len(offsets) == 1:
            after = key_share, value_share = call(
                share_kernel,
                (shares, shares),
                (scaled, key_projection, value_projection, w_query),
                near=(0,),
                far=(1, 2, 3),
                scratch=(
                    pltpu.VMEM(key_projection.shape, BF16),
                    pltpu.VMEM(value_projection.shape, BF16),
                    pltpu.SemaphoreType.DMA((2,)),
                ),
                flops=4 * rows * key_projection.size,
                read=8 * w_query.size,
            )
        elif total is None:
            after = total, turns = call(
                functools.partial(query_turns_kernel, tuple(offsets), pairs),
                (totals, jax.ShapeDtypeStruct((2, pairs, HEAD_SIZE), F32)),
                (blocks, w_query, lengths, jnp.asarray(rate)),
                near=(0, 1),
                smem=(2,),
                flops=2 * rows * len(offsets) * features * query_columns,
                read=2 * len(offsets) * features * query_columns,
            )
        else:
            total = query(new, len(offsets) - len(new), blocks, total)
            after = (total,)
        blocks = call(
            join_kernel,
            jax.ShapeDtypeStruct((2 * len(offsets), rows, features), BF16),
            (blocks, arrived, after[0]),
        )
        new = [o ^ far for o in offsets]
        offsets = offsets + new
    arrived = swap(blocks, core, count)
    total = query(new, len(offsets) - len(new), blocks, total)
    sent = held // KEY_VALUE_HEADS if held % KEY_VALUE_HEADS == 0 else held
    message = call(
        functools.partial(message_kernel, tuple(o ^ core for o in offsets), pairs),
        jax.ShapeDtypeStruct((count, pairs * (sent + 3), HEAD_SIZE), F32),
        (arrived, w_query, total, key_share, value_share, squares),
        near=(0, 1),
        flops=2 * arrived.size * query_columns,
        read=2 * len(offsets) * features * query_columns,
    )

    got = lax.all_to_all(message, "wide", 0, 0, tiled=True)
    if sent == 1 and held % KEY_VALUE_HEADS == 0:
        query_rows = got
    else:
        query_rows = (
            got[:, : pairs * sent].reshape(count, sent, pairs, HEAD_SIZE).reshape(-1, pairs, HEAD_SIZE)
        )
        if held % KEY_VALUE_HEADS:
            head = lax.axis_index("wide") // devices_of_head
            query_rows = lax.dynamic_index_in_dim(
                query_rows.reshape(QUERY_GROUP, KEY_VALUE_HEADS, pairs, HEAD_SIZE), head, 1, False
            )
    cache_bytes = 2 * slot_key_cache.size
    attended = call(
        functools.partial(attend_kernel, pairs, width),
        jax.ShapeDtypeStruct((pairs, QUERY_GROUP * HEAD_SIZE), BF16),
        (lengths, turns, query_rows, got, slot_key_cache, slot_value_cache),
        near=(4, 5),
        smem=(0,),
        scratch=(
            pltpu.VMEM(
                ((pairs + 1) // 2, min(pairs, 2) * QUERY_GROUP, slot_key_cache.shape[1]), F32
            ),
            pltpu.VMEM((pairs, QUERY_GROUP * HEAD_SIZE), F32),
        ),
        limit=8 * MIB,
        flops=4 * QUERY_GROUP * slot_key_cache.size,
        read=2 * cache_bytes,
    )

    mine = attended[None]
    head_offsets, slot_offsets = [0], [0]
    for far in outer:
        arrived = swap(mine, far, count)
        if far >= devices_of_head:
            mine = jnp.concatenate([mine, arrived], 0)
            head_offsets = head_offsets + [o ^ (far // devices_of_head) for o in head_offsets]
        else:
            mine = jnp.concatenate([mine, arrived], 1)
            slot_offsets = slot_offsets + [o ^ far for o in slot_offsets]
    across = swap(mine, bit, count)
    beside = swap(mine, core, count)
    both = swap(across, core, count)
    slot_row = slot_of_row.reshape(1, rows)
    left = jax.ShapeDtypeStruct((rows, output_projection.shape[0]), BF16)
    before = call(
        functools.partial(
            assemble_kernel,
            pairs,
            tuple(head_offsets),
            tuple(tuple(o ^ b for o in slot_offsets) for b in (0, core, bit)),
        ),
        left,
        (slot_row, mine, beside, across),
    )
    return call(
        functools.partial(
            project_kernel,
            pairs,
            tuple(head_offsets),
            (tuple(o ^ bit ^ core for o in slot_offsets),),
        ),
        jax.ShapeDtypeStruct((rows, output_projection.shape[1]), BF16),
        (slot_row, both, before, output_projection),
        near=(3,),
        scratch=(pltpu.VMEM(left.shape, BF16),),
        flops=2 * rows * output_projection.size,
        read=2 * output_projection.size,
    )


def solution(mesh):
    placed = (
        P("groups", "wide"),
        P("wide"),
        P("groups"),
        P("groups"),
        P(None, "wide"),
        P("wide", None),
        P("wide", None),
        P(None, "wide"),
        P(("groups", "wide"), None, None),
        P(("groups", "wide"), None, None),
    )
    return jax.shard_map(
        functools.partial(body, mesh.shape["wide"]),
        mesh=mesh,
        in_specs=placed,
        out_specs=P("groups", "wide"),
        check_vma=False,
    )
```

time: 83 us -> 54.4 us (0.66)
  local copies, waits for them, and re-layouts: 25.7 us -> 0.05 us
  blocking collectives: 0 us -> 14.2 us
  waiting for transfers between devices: 29.6 us -> 18.3 us
  starting transfers between devices: 14.5 us -> 8.93 us
  Pallas kernels: 11.5 us -> 12.6 us
  other arithmetic: 1.06 us -> 0.08 us
    unnamed x20, local copies, waits for them, and re-layouts: 24.9 us -> 0.05 us
    all_to_all x0 -> x1, blocking collectives: none -> 14.2 us  [body(): got = lax.all_to_all(message, 'wide', 0, 0, tiled=True)]
    all_to_all x1 -> x0, waiting for transfers between devices: 7.81 us -> none  [body(): got = lax.all_to_all(message, 'wide', 0, 0, tiled=True)]
    all_to_all x1 -> x0, starting transfers between devices: 6.24 us -> none  [body(): got = lax.all_to_all(message, 'wide', 0, 0, tiled=True)]
    ppermute x8 -> x9, waiting for transfers between devices: 21.8 us -> 18.3 us  [swap(): return lax.ppermute(array, 'wide', [(i, i ^ bit) for i in range(count)])]
    pallas_call x7 -> x12, Pallas kernels: 11.5 us -> 12.6 us  [call(): pl.pallas_call(kernel, out_shape=out_shape, in_specs=specs, out_specs=jax...]
    ppermute x8 -> x9, starting transfers between devices: 8.23 us -> 8.93 us  [swap(): return lax.ppermute(array, 'wide', [(i, i ^ bit) for i in range(count)])]
  transfers between devices with their start and end apart: 9 -> 9, of which waited for: 8 -> 8; matrix products, arithmetic and copies ran while one was open for 1% -> 0% of each run, Pallas kernels for 2% -> 8%
where the time goes in v3:
time: 54.4 us; the launch traced here: 54.2 us
  waiting for transfers between devices  18.3 us (34%)
  blocking collectives  14.2 us (26%)
  Pallas kernels  12.6 us (23%)
  starting transfers between devices  8.93 us (16%)
    ppermute x9, waiting for transfers between devices, swap(): return lax.ppermute(array, 'wide', [(i, i ^ bit) for i in range(count)])  18.3 us
    all_to_all x1, blocking collectives, body(): got = lax.all_to_all(message, 'wide', 0, 0, tiled=True)  14.2 us
    pallas_call x12, Pallas kernels, call(): pl.pallas_call(kernel, out_shape=out_shape, in_specs=specs, out_specs=jax...  12.6 us
    ppermute x9, starting transfers between devices, swap(): return lax.ppermute(array, 'wide', [(i, i ^ bit) for i in range(count)])  8.93 us
  transfers between devices with their start and end apart: 9, of which 8 were waited for; matrix products, arithmetic and copies ran while one was open for 0% of the time, Pallas kernels for 8%

profile of v3, /device:TPU:0, one launch (start us, length us, event | category | flops | bytes accessed | tf_op | source)
XLA Modules:
  0.0 54.2 jit_solution(8199922338886789212)
XLA Ops:
  0.0 0.0 copy-start.5
  0.0 0.0 copy-start
  0.0 0.0 copy-start.4
  0.0 1.2 %shard_map.109 = (bf16[16,1024]{1,0:T(8,128)(2,1)S(1)}, f32[16,128]{1,0:T(8,128)S(1)}) custom-call(bf16[16,1024]{1,0:T(8,128)(2,1)} %far_tokens.1, bf16[1024]{0:T(1024)(128)(2,1)} %far_gain.1, s32[1,16]{1,0:T(1,128)} %bitcast.10), custom_call_target="tpu_custom_call" | custom-call | tf_op jit(solution)/shard_map/pallas_call | solution.py:35
  1.2 4.1 %collective-permute-start = (bf16[1,16,1024]{2,1,0:T(8,128)(2,1)S(1)}, bf16[1,16,1024]{2,1,0:T(8,128)(2,1)S(1)}, u32[]{:S(2)}, u32[]{:S(2)}) collective-permute-start(bf16[1,16,1024]{2,1,0:T(8,128)(2,1)S(1)} %bitcast.8), channel_id=1, source_target_pairs={{0,8},{1,9},{2,10},{3,11},{4,12},{5,13},{6,14},{7,15},{8,0},{9,1},... | collective-permute-start | bytes 98312 | tf_op jit(solution)/shard_map/ppermute | solution.py:272
  5.3 1.8 %shard_map.110 = (f32[16,512]{1,0:T(8,128)S(1)}, f32[16,512]{1,0:T(8,128)S(1)}) custom-call(bf16[16,1024]{1,0:T(8,128)(2,1)S(1)} %get-tuple-element.11.scaled_ref, bf16[1024,512]{1,0:T(8,128)(2,1)} %far_key.1, bf16[1024,512]{1,0:T(8,128)(2,1)} %far_value.1, bf16[16384,512]{1,0:T(8,128)(2,1)} %weight_ref.8), custom_call_target="tpu_custom_call" | custom-call | flops 33554432 | bytes 67108864 | tf_op jit(solution)/shard_map/pallas_call | solution.py:35
  7.1 0.4 collective-permute-done.arrived_ref
  7.5 2.0 %collective-permute-start.1 = (bf16[2,16,1024]{2,1,0:T(8,128)(2,1)S(1)}, bf16[2,16,1024]{2,1,0:T(8,128)(2,1)S(1)}, u32[]{:S(2)}, u32[]{:S(2)}) collective-permute-start(bf16[2,16,1024]{2,1,0:T(8,128)(2,1)S(1)} %shard_map.111.blocks_ref.mine_ref), channel_id=1, source_target_pairs={{0,4},{1,5},{2,6},{3,7},{4,0},{5,1},{6,2},{7,3},{8,12},{9,13},{10,... | collective-permute-start | bytes 196616 | tf_op jit(solution)/shard_map/ppermute | solution.py:272
  9.6 0.0 copy-done.5
  9.6 0.0 copy-done
  9.6 0.0 copy-done.4
  9.6 0.9 %shard_map.112 = (f32[16,512]{1,0:T(8,128)S(1)}, f32[2,4,128]{2,1,0:T(4,128)S(1)}) custom-call(bf16[2,16,1024]{2,1,0:T(8,128)(2,1)S(1)} %shard_map.111.blocks_ref.mine_ref, bf16[16384,512]{1,0:T(8,128)(2,1)S(1)} %copy-done, s32[16]{0:T(128)S(1)} %copy-done.4, f32[1,128]{1,0:T(1,128)S(1)} %copy-done.5), custom_call_target="tpu_custom_call" | custom-call | flops 33554432 | bytes 2097152 | tf_op jit(solution)/shard_map/pallas_call | solution.py:35
  10.5 1.3 %collective-permute-done.1.arrived_ref = bf16[2,16,1024]{2,1,0:T(8,128)(2,1)S(1)} collective-permute-done((bf16[2,16,1024]{2,1,0:T(8,128)(2,1)S(1)}, bf16[2,16,1024]{2,1,0:T(8,128)(2,1)S(1)}, u32[]{:S(2)}, u32[]{:S(2)}) %collective-permute-start.1) | collective-permute-done | bytes 65568 | tf_op jit(solution)/shard_map/ppermute | solution.py:272
  11.8 2.0 %collective-permute-start.2 = (bf16[4,16,1024]{2,1,0:T(8,128)(2,1)S(1)}, bf16[4,16,1024]{2,1,0:T(8,128)(2,1)S(1)}, u32[]{:S(2)}, u32[]{:S(2)}) collective-permute-start(bf16[4,16,1024]{2,1,0:T(8,128)(2,1)S(1)} %shard_map.113.blocks_ref.mine_ref), channel_id=1, source_target_pairs={{0,2},{1,3},{2,0},{3,1},{4,6},{5,7},{6,4},{7,5},{8,10},{9,11},{10,... | collective-permute-start | bytes 393224 | tf_op jit(solution)/shard_map/ppermute | solution.py:272
  13.8 0.4 shard_map.114.after_ref.total_ref
  14.2 2.6 %collective-permute-done.2.arrived_ref = bf16[4,16,1024]{2,1,0:T(8,128)(2,1)S(1)} collective-permute-done((bf16[4,16,1024]{2,1,0:T(8,128)(2,1)S(1)}, bf16[4,16,1024]{2,1,0:T(8,128)(2,1)S(1)}, u32[]{:S(2)}, u32[]{:S(2)}) %collective-permute-start.2) | collective-permute-done | bytes 131104 | tf_op jit(solution)/shard_map/ppermute | solution.py:272
  16.9 0.0 copy-start.1
  16.9 0.0 copy-start.2
  16.9 0.1 collective-permute-start.3
  17.0 0.0 slice-start
  17.0 0.0 slice-start.1
  17.0 0.7 %shard_map.116.total_ref = f32[16,512]{1,0:T(8,128)S(1)} custom-call(bf16[8,16,1024]{2,1,0:T(8,128)(2,1)S(1)} %shard_map.115.blocks_ref, bf16[16384,512]{1,0:T(8,128)(2,1)S(1)} %copy-done, f32[16,512]{1,0:T(8,128)S(1)} %shard_map.114.after_ref.total_ref), custom_call_target="tpu_custom_call" | custom-call | flops 67108864 | bytes 4194304 | tf_op jit(solution)/shard_map/pallas_call | solution.py:35
  17.7 0.0 copy-start.3
  17.7 0.8 %collective-permute-done.3.blocks_ref = bf16[8,16,1024]{2,1,0:T(8,128)(2,1)S(1)} collective-permute-done((bf16[8,16,1024]{2,1,0:T(8,128)(2,1)S(1)}, bf16[8,16,1024]{2,1,0:T(8,128)(2,1)S(1)}, u32[]{:S(2)}, u32[]{:S(2)}) %collective-permute-start.3) | collective-permute-done | bytes 262176 | tf_op jit(solution)/shard_map/ppermute | solution.py:272
  18.5 0.0 slice-start.2
  18.5 1.2 %shard_map.117 = f32[16,16,128]{2,1,0:T(8,128)S(1)} custom-call(bf16[8,16,1024]{2,1,0:T(8,128)(2,1)S(1)} %collective-permute-done.3.blocks_ref, bf16[16384,512]{1,0:T(8,128)(2,1)S(1)} %copy-done, f32[16,512]{1,0:T(8,128)S(1)} %shard_map.116.total_ref, f32[16,512]{1,0:T(8,128)S(1)} %get-tuple-element.12.after_ref.key_ref, ...), custom_call_target="tpu_custom_call" | custom-call | flops 134217728 | bytes 8388608 | tf_op jit(solution)/shard_map/pallas_call | solution.py:35
  19.7 14.2 %all_to_all.5.query_ref.rest_ref = f32[16,16,128]{2,1,0:T(8,128)S(1)} all-to-all(f32[16,16,128]{2,1,0:T(8,128)S(1)} %shard_map.117), channel_id=1, replica_groups=mesh['groups'=2,'wide'=16] {'wide'}, dimensions={0} | all-to-all | bytes 262144 | tf_op jit(solution)/shard_map/all_to_all | solution.py:378
  33.8 0.0 copy-done.1
  33.8 0.0 copy-done.2
  33.9 2.8 %shard_map.118 = bf16[4,2048]{1,0:T(4,128)(2,1)S(1)} custom-call(s32[16]{0:T(128)S(1)} %copy-done.4, f32[2,4,128]{2,1,0:T(4,128)S(1)} %get-tuple-element.13.turns_ref, f32[16,16,128]{2,1,0:T(8,128)S(1)} %all_to_all.5.query_ref.rest_ref, f32[16,16,128]{2,1,0:T(8,128)S(1)} %all_to_all.5.query_ref.rest_ref, bf16[4,4096,128]{2,1,0:T(8,128)(2,1)S(1)} %copy-done.1, ...), custom_call_target="tpu_custom_call" | custom-call | flops 134217728 | bytes 8388608 | tf_op jit(solution)/shard_map/pallas_call | solution.py:35
  36.6 0.5 collective-permute-start.4
  37.1 4.2 %collective-permute-done.4 = bf16[1,4,2048]{2,1,0:T(4,128)(2,1)S(1)} collective-permute-done((bf16[1,4,2048]{2,1,0:T(4,128)(2,1)S(1)}, bf16[1,4,2048]{2,1,0:T(4,128)(2,1)S(1)}, u32[]{:S(2)}, u32[]{:S(2)}) %collective-permute-start.4) | collective-permute-done | bytes 16416 | tf_op jit(solution)/shard_map/ppermute | solution.py:272
  41.4 0.1 collective-permute-start.5
  41.4 3.9 %collective-permute-done.5 = bf16[2,4,2048]{2,1,0:T(4,128)(2,1)S(1)} collective-permute-done((bf16[2,4,2048]{2,1,0:T(4,128)(2,1)S(1)}, bf16[2,4,2048]{2,1,0:T(4,128)(2,1)S(1)}, u32[]{:S(2)}, u32[]{:S(2)}) %collective-permute-start.5) | collective-permute-done | bytes 32800 | tf_op jit(solution)/shard_map/ppermute | solution.py:272
  45.3 0.1 pad_maximum_fusion.refs_0_
  45.4 0.1 collective-permute-start.6
  45.5 0.1 collective-permute-start.8
  45.6 4.2 %collective-permute-done.6.refs_2_ = bf16[4,4,2048]{2,1,0:T(4,128)(2,1)S(1)} collective-permute-done((bf16[4,4,2048]{2,1,0:T(4,128)(2,1)S(1)}, bf16[4,4,2048]{2,1,0:T(4,128)(2,1)S(1)}, u32[]{:S(2)}, u32[]{:S(2)}) %collective-permute-start.6) | collective-permute-done | bytes 65568 | tf_op jit(solution)/shard_map/ppermute | solution.py:272
  49.7 0.0 collective-permute-start.7
  49.7 0.0 collective-permute-done.8.refs_1_
  49.7 0.0 copy-done.3
  49.7 0.5 shard_map.119.before_ref
  50.2 0.8 %collective-permute-done.7.piece_ref = bf16[4,4,2048]{2,1,0:T(4,128)(2,1)S(1)} collective-permute-done((bf16[4,4,2048]{2,1,0:T(4,128)(2,1)S(1)}, bf16[4,4,2048]{2,1,0:T(4,128)(2,1)S(1)}, u32[]{:S(2)}, u32[]{:S(2)}) %collective-permute-start.7) | collective-permute-done | bytes 65568 | tf_op jit(solution)/shard_map/ppermute | solution.py:272
  51.0 0.0 slice-done
  51.0 0.0 slice-done.1
  51.0 0.0 slice-done.2
  51.0 0.0 slice-done.3
  51.0 3.2 %shard_map.120 = bf16[16,1024]{1,0:T(8,128)(2,1)} custom-call(s32[1,16]{1,0:T(1,128)S(1)} %bitcast.12, bf16[4,4,2048]{2,1,0:T(4,128)(2,1)S(1)} %collective-permute-done.7.piece_ref, bf16[16,8192]{1,0:T(8,128)(2,1)S(1)} %shard_map.119.before_ref, bf16[8192,1024]{1,0:T(8,128)(2,1)S(1)} %bitcast.4), custom_call_target="tpu_custom_call" | custom-call | flops 268435456 | bytes 16777216 | tf_op jit(solution)/shard_map/pallas_call | solution.py:35
  (6 shorter events, 0.1 us)
Async XLA Ops:
  0.0 9.6 %copy-start.5 = (f32[1,128]{1,0:T(1,128)S(1)}, f32[1,128]{1,0:T(1,128)}, u32[]{:S(2)}) copy-start(f32[1,128]{1,0:T(1,128)} %constant.2.clone.rate_ref) | copy-start | bytes 1540
  0.0 9.6 %copy-start = (bf16[16384,512]{1,0:T(8,128)(2,1)S(1)}, bf16[16384,512]{1,0:T(8,128)(2,1)}, u32[]{:S(2)}) copy-start(bf16[16384,512]{1,0:T(8,128)(2,1)} %weight_ref.8) | copy-start | bytes 50331652
  0.0 9.6 %copy-start.4 = (s32[16]{0:T(128)S(1)}, s32[16]{0:T(128)}, u32[]{:S(2)}) copy-start(s32[16]{0:T(128)} %lengths_ref.3) | copy-start | bytes 196
  1.2 6.4 %collective-permute-start = (bf16[1,16,1024]{2,1,0:T(8,128)(2,1)S(1)}, bf16[1,16,1024]{2,1,0:T(8,128)(2,1)S(1)}, u32[]{:S(2)}, u32[]{:S(2)}) collective-permute-start(bf16[1,16,1024]{2,1,0:T(8,128)(2,1)S(1)} %bitcast.8), channel_id=1, source_target_pairs={{0,8},{1,9},{2,10},{3,11},{4,12},{5,13},{6,14},{7,15},{8,0},{9,1},... | collective-permute-start | bytes 98312 | tf_op jit(solution)/shard_map/ppermute | solution.py:272
  7.5 4.3 %collective-permute-start.1 = (bf16[2,16,1024]{2,1,0:T(8,128)(2,1)S(1)}, bf16[2,16,1024]{2,1,0:T(8,128)(2,1)S(1)}, u32[]{:S(2)}, u32[]{:S(2)}) collective-permute-start(bf16[2,16,1024]{2,1,0:T(8,128)(2,1)S(1)} %shard_map.111.blocks_ref.mine_ref), channel_id=1, source_target_pairs={{0,4},{1,5},{2,6},{3,7},{4,0},{5,1},{6,2},{7,3},{8,12},{9,13},{10,... | collective-permute-start | bytes 196616 | tf_op jit(solution)/shard_map/ppermute | solution.py:272
  11.8 5.0 %collective-permute-start.2 = (bf16[4,16,1024]{2,1,0:T(8,128)(2,1)S(1)}, bf16[4,16,1024]{2,1,0:T(8,128)(2,1)S(1)}, u32[]{:S(2)}, u32[]{:S(2)}) collective-permute-start(bf16[4,16,1024]{2,1,0:T(8,128)(2,1)S(1)} %shard_map.113.blocks_ref.mine_ref), channel_id=1, source_target_pairs={{0,2},{1,3},{2,0},{3,1},{4,6},{5,7},{6,4},{7,5},{8,10},{9,11},{10,... | collective-permute-start | bytes 393224 | tf_op jit(solution)/shard_map/ppermute | solution.py:272
  16.9 17.0 %copy-start.1 = (bf16[4,4096,128]{2,1,0:T(8,128)(2,1)S(1)}, bf16[4,4096,128]{2,1,0:T(8,128)(2,1)}, u32[]{:S(2)}) copy-start(bf16[4,4096,128]{2,1,0:T(8,128)(2,1)} %keys_ref.1) | copy-start | bytes 12582916
  16.9 17.0 %copy-start.2 = (bf16[4,4096,128]{2,1,0:T(8,128)(2,1)S(1)}, bf16[4,4096,128]{2,1,0:T(8,128)(2,1)}, u32[]{:S(2)}) copy-start(bf16[4,4096,128]{2,1,0:T(8,128)(2,1)} %values_ref.1) | copy-start | bytes 12582916
  16.9 1.6 %collective-permute-start.3 = (bf16[8,16,1024]{2,1,0:T(8,128)(2,1)S(1)}, bf16[8,16,1024]{2,1,0:T(8,128)(2,1)S(1)}, u32[]{:S(2)}, u32[]{:S(2)}) collective-permute-start(bf16[8,16,1024]{2,1,0:T(8,128)(2,1)S(1)} %shard_map.115.blocks_ref), channel_id=1, source_target_pairs={{0,1},{1,0},{2,3},{3,2},{4,5},{5,4},{6,7},{7,6},{8,9},{9,8},{10,11... | collective-permute-start | bytes 786440 | tf_op jit(solution)/shard_map/ppermute | solution.py:272
  17.0 34.0 %slice-start = ((s8[16777216]{0:T(1024)(128)(4,1)}), s8[4194304]{0:T(1024)(128)(4,1)S(1)}, s32[]{:S(2)}) async-start(s8[16777216]{0:T(1024)(128)(4,1)} %bitcast.3), calls=%async_computation.1 | async-start | bytes 8388608
  17.0 34.0 %slice-start.1 = ((s8[16777216]{0:T(1024)(128)(4,1)}), s8[4194304]{0:T(1024)(128)(4,1)S(1)}, s32[]{:S(2)}) async-start(s8[16777216]{0:T(1024)(128)(4,1)} %bitcast.3), calls=%async_computation.2 | async-start | bytes 8388608
  17.7 32.1 %copy-start.3 = (s32[16]{0:T(128)S(1)}, s32[16]{0:T(128)}, u32[]{:S(2)}) copy-start(s32[16]{0:T(128)} %param.13) | copy-start | bytes 196
  18.5 32.5 %slice-start.2 = ((s8[16777216]{0:T(1024)(128)(4,1)}), s8[4194304]{0:T(1024)(128)(4,1)S(1)}, s32[]{:S(2)}) async-start(s8[16777216]{0:T(1024)(128)(4,1)} %bitcast.3), calls=%async_computation.3 | async-start | bytes 8388608
  18.5 32.5 %slice-start.3 = ((s8[16777216]{0:T(1024)(128)(4,1)}), s8[4194304]{0:T(1024)(128)(4,1)S(1)}, s32[]{:S(2)}) async-start(s8[16777216]{0:T(1024)(128)(4,1)} %bitcast.3), calls=%async_computation.4 | async-start | bytes 8388608
  36.6 4.7 %collective-permute-start.4 = (bf16[1,4,2048]{2,1,0:T(4,128)(2,1)S(1)}, bf16[1,4,2048]{2,1,0:T(4,128)(2,1)S(1)}, u32[]{:S(2)}, u32[]{:S(2)}) collective-permute-start(bf16[1,4,2048]{2,1,0:T(4,128)(2,1)S(1)} %bitcast.5), channel_id=1, source_target_pairs={{0,8},{1,9},{2,10},{3,11},{4,12},{5,13},{6,14},{7,15},{8,0},{9,1},... | collective-permute-start | bytes 49160 | tf_op jit(solution)/shard_map/ppermute | solution.py:272
  41.4 4.0 %collective-permute-start.5 = (bf16[2,4,2048]{2,1,0:T(4,128)(2,1)S(1)}, bf16[2,4,2048]{2,1,0:T(4,128)(2,1)S(1)}, u32[]{:S(2)}, u32[]{:S(2)}) collective-permute-start(bf16[2,4,2048]{2,1,0:T(4,128)(2,1)S(1)} %pad_maximum_fusion.1), channel_id=1, source_target_pairs={{0,4},{1,5},{2,6},{3,7},{4,0},{5,1},{6,2},{7,3},{8,12},{9,13},{10,... | collective-permute-start | bytes 98312 | tf_op jit(solution)/shard_map/ppermute | solution.py:272
  45.4 4.3 %collective-permute-start.6 = (bf16[4,4,2048]{2,1,0:T(4,128)(2,1)S(1)}, bf16[4,4,2048]{2,1,0:T(4,128)(2,1)S(1)}, u32[]{:S(2)}, u32[]{:S(2)}) collective-permute-start(bf16[4,4,2048]{2,1,0:T(4,128)(2,1)S(1)} %pad_maximum_fusion.refs_0_), channel_id=1, source_target_pairs={{0,2},{1,3},{2,0},{3,1},{4,6},{5,7},{6,4},{7,5},{8,10},{9,11},{10,... | collective-permute-start | bytes 196616 | tf_op jit(solution)/shard_map/ppermute | solution.py:272
  45.5 4.3 %collective-permute-start.8 = (bf16[4,4,2048]{2,1,0:T(4,128)(2,1)S(1)}, bf16[4,4,2048]{2,1,0:T(4,128)(2,1)S(1)}, u32[]{:S(2)}, u32[]{:S(2)}) collective-permute-start(bf16[4,4,2048]{2,1,0:T(4,128)(2,1)S(1)} %pad_maximum_fusion.refs_0_), channel_id=1, source_target_pairs={{0,1},{1,0},{2,3},{3,2},{4,5},{5,4},{6,7},{7,6},{8,9},{9,8},{10,11... | collective-permute-start | bytes 196616 | tf_op jit(solution)/shard_map/ppermute | solution.py:272
  49.7 1.3 %collective-permute-start.7 = (bf16[4,4,2048]{2,1,0:T(4,128)(2,1)S(1)}, bf16[4,4,2048]{2,1,0:T(4,128)(2,1)S(1)}, u32[]{:S(2)}, u32[]{:S(2)}) collective-permute-start(bf16[4,4,2048]{2,1,0:T(4,128)(2,1)S(1)} %collective-permute-done.6.refs_2_), channel_id=1, source_target_pairs={{0,1},{1,0},{2,3},{3,2},{4,5},{5,4},{6,7},{7,6},{8,9},{9,8},{10,11... | collective-permute-start | bytes 196616 | tf_op jit(solution)/shard_map/ppermute | solution.py:272

commit v4 on v3

--- a/solution.py
+++ b/solution.py
@@ -67,6 +67,10 @@
     squares_ref[...] = jnp.broadcast_to(turned, squares_ref.shape)
 
 
+def pass_kernel(array_ref, after_ref, same_ref):
+    same_ref[...] = array_ref[...]
+
+
 def join_kernel(mine_ref, arrived_ref, after_ref, joined_ref):
     count = mine_ref.shape[0]
     joined_ref[:count] = mine_ref[...]
@@ -101,7 +105,7 @@
     out_ref[...] = products(offsets, first, blocks_ref, weight_ref, total_ref[...])
 
 
-def query_turns_kernel(offsets, pairs, blocks_ref, weight_ref, lengths_ref, rate_ref, out_ref, turns_ref):
+def query_turns_kernel(offsets, pairs, blocks_ref, weight_ref, lengths_ref, rate_ref, out_ref, turns_ref, limits_ref):
     out_ref[...] = products(offsets, 0, blocks_ref, weight_ref, jnp.zeros(out_ref.shape, F32))
     own = (lax.axis_index("wide") * pairs) % lengths_ref.shape[0]
     positions = jnp.concatenate(
@@ -110,6 +114,7 @@
     angle = positions.astype(F32) * rate_ref[...]
     turns_ref[0] = jnp.cos(angle)
     turns_ref[1] = jnp.sin(angle)
+    limits_ref[...] = positions
 
 
 def message_kernel(
@@ -153,11 +158,10 @@
 
 
 def attend_kernel(
-    pairs, width, lengths_ref, turns_ref, query_ref, rest_ref, keys_ref, values_ref, out_ref, scores_ref, wide_ref
+    pairs, width, limits_ref, turns_ref, query_ref, rest_ref, keys_ref, values_ref, out_ref, scores_ref, wide_ref
 ):
     group = query_ref.shape[0]
     length = keys_ref.shape[1]
-    first = (lax.axis_index("wide") * pairs) % lengths_ref.shape[0]
     at = rest_ref.shape[1] - 3 * pairs
     summed = jnp.sum(rest_ref[:, at:, :], axis=0)
     score_scale = 1.0 / math.sqrt(HEAD_SIZE)
@@ -175,7 +179,7 @@
             key = rotated(key, cosines, sines)[0:1, :].astype(BF16).astype(F32)
             values.append((summed[pairs + i : pairs + i + 1, :] * scale).astype(BF16).astype(F32))
             owns.append(jnp.sum(query.astype(F32) * key, axis=1, keepdims=True))
-            limits.append(jnp.full((group, step), lengths_ref[first + i], jnp.int32))
+            limits.append(jnp.broadcast_to(limits_ref[i : i + 1, :], (group, HEAD_SIZE)))
             blank = jnp.zeros_like(query)
             queries.append(
                 query
@@ -185,7 +189,7 @@
         stacked = jnp.concatenate(queries, axis=0)
         own = jnp.concatenate(owns, axis=0)
         limit = jnp.concatenate(limits, axis=0)
-        column = lax.broadcasted_iota(jnp.int32, (many * group, step), 1)
+        column = lax.broadcasted_iota(jnp.int32, (many * group, HEAD_SIZE), 1)
         tops = jnp.broadcast_to(own, (many * group, HEAD_SIZE))
         place = base // many
         for start in range(0, length, step):
@@ -195,30 +199,30 @@
                 (((1,), (1,)), ((), ())),
                 preferred_element_type=F32,
             )
-            scores = jnp.where(column < limit - start, scores, -jnp.inf)
-            scores_ref[place, :, start : start + step] = scores
-            tops = jnp.maximum(tops, folded(jnp.maximum, scores))
+            for at in range(0, step, HEAD_SIZE):
+                tile = jnp.where(
+                    column < limit - (start + at), scores[:, at : at + HEAD_SIZE], -jnp.inf
+                )
+                scores_ref[place, :, start + at : start + at + HEAD_SIZE] = tile
+                tops = jnp.maximum(tops, tile)
         parts.append((members, place, own, tops, values))
     factor = score_scale * math.log2(math.e)
-    weighed = []
     for members, place, own, tops, values in parts:
         top = jnp.max(tops, axis=1, keepdims=True)
         own_w = jnp.exp2((own - top) * factor)
         sums = jnp.zeros_like(tops)
+        blended = jnp.zeros((many * group, many * HEAD_SIZE), F32)
         for start in range(0, length, step):
             weights = jnp.exp2((scores_ref[place, :, start : start + step] - top) * factor)
-            scores_ref[place, :, start : start + step] = weights
             sums = sums + folded(jnp.add, weights)
-        share = 1.0 / (own_w + jnp.sum(sums, axis=1, keepdims=True))
-        weighed.append((members, place, share, (own_w * share).astype(BF16).astype(F32), values))
-    for members, place, share, own_p, values in weighed:
-        blended = jnp.zeros((many * group, many * HEAD_SIZE), F32)
-        for start in range(0, length, step):
             blended = blended + jnp.dot(
-                (scores_ref[place, :, start : start + step] * share).astype(BF16),
+                weights.astype(BF16),
                 side_by_side(values_ref, members, start, step),
                 preferred_element_type=F32,
             )
+        share = 1.0 / (own_w + jnp.sum(sums, axis=1, keepdims=True))
+        blended = blended * share
+        own_p = (own_w * share).astype(BF16).astype(F32)
         for k, i in enumerate(members):
             rows = slice(k * group, (k + 1) * group)
             result = blended[rows, k * HEAD_SIZE : (k + 1) * HEAD_SIZE] + own_p[rows] * values[k]
@@ -227,9 +231,9 @@
     out_ref[...] = wide_ref[...].astype(BF16)
 
 
-def place_rows(pairs, head_offsets, slot_offsets, slot_ref, pieces, left_ref, before_ref=None):
-    rows = left_ref.shape[0]
-    heads, held, _ = pieces[0].shape
+def project_half(pairs, head_offsets, slot_offsets, slot_ref, pieces, weight_ref, total):
+    rows = slot_ref.shape[1]
+    held = pieces[0].shape[1]
     devices_of_head = rows // pairs
     place = lax.axis_index("wide")
     group_place = place % devices_of_head
@@ -242,29 +246,43 @@
         for k, offset in enumerate(offsets):
             device = jnp.where(position // pairs == k, group_place ^ offset, device)
         picks.append((slot_of_row == device * pairs + position % pairs).astype(BF16))
-    for z, offset in enumerate(head_offsets):
-        head = head_place ^ offset
-        ordered = sum(
+    ordered = [
+        sum(
             jnp.dot(pick, piece[z], preferred_element_type=F32) for pick, piece in zip(picks, pieces)
         ).astype(BF16)
-        for g in range(QUERY_GROUP):
-            start = pl.multiple_of((g * heads + head) * HEAD_SIZE, HEAD_SIZE)
-            columns = ordered[:, g * HEAD_SIZE : (g + 1) * HEAD_SIZE]
-            if before_ref is not None:
-                columns = columns + before_ref[:, pl.ds(start, HEAD_SIZE)]
-            left_ref[:, pl.ds(start, HEAD_SIZE)] = columns
-
-
-def assemble_kernel(pairs, head_offsets, slot_offsets, slot_ref, *refs):
-    place_rows(pairs, head_offsets, slot_offsets, slot_ref, refs[:-1], refs[-1])
-
-
-def project_kernel(
-    pairs, head_offsets, slot_offsets, slot_ref, piece_ref, before_ref, weight_ref, out_ref, left_ref
+        for z in range(len(head_offsets))
+    ]
+    for g in range(QUERY_GROUP):
+        columns = slice(g * HEAD_SIZE, (g + 1) * HEAD_SIZE)
+        weights = []
+        for offset in head_offsets:
+            start = (g * KEY_VALUE_HEADS + (head_place ^ offset)) * HEAD_SIZE
+            weights.append(weight_ref[pl.ds(pl.multiple_of(start, HEAD_SIZE), HEAD_SIZE), :])
+        total = total + jnp.dot(
+            jnp.concatenate([o[:, columns] for o in ordered], axis=1),
+            jnp.concatenate(weights, axis=0),
+            preferred_element_type=F32,
+        )
+    return total
+
+
+def first_half_kernel(pairs, head_offsets, slot_offsets, slot_ref, mine_ref, other_ref, weight_ref, out_ref):
+    out_ref[...] = project_half(
+        pairs,
+        head_offsets,
+        slot_offsets,
+        slot_ref,
+        (mine_ref, other_ref),
+        weight_ref,
+        jnp.zeros(out_ref.shape, F32),
+    )
+
+
+def second_half_kernel(
+    pairs, head_offsets, slot_offsets, slot_ref, mine_ref, other_ref, weight_ref, half_ref, out_ref
 ):
-    place_rows(pairs, head_offsets, slot_offsets, slot_ref, (piece_ref,), left_ref, before_ref)
-    out_ref[...] = jnp.dot(
-        left_ref[...], weight_ref[...], preferred_element_type=F32
+    out_ref[...] = project_half(
+        pairs, head_offsets, slot_offsets, slot_ref, (mine_ref, other_ref), weight_ref, half_ref[...]
     ).astype(BF16)
 
 
@@ -344,9 +362,13 @@
                 read=8 * w_query.size,
             )
         elif total is None:
-            after = total, turns = call(
+            after = total, turns, limits = call(
                 functools.partial(query_turns_kernel, tuple(offsets), pairs),
-                (totals, jax.ShapeDtypeStruct((2, pairs, HEAD_SIZE), F32)),
+                (
+                    totals,
+                    jax.ShapeDtypeStruct((2, pairs, HEAD_SIZE), F32),
+                    jax.ShapeDtypeStruct((pairs, HEAD_SIZE), jnp.int32),
+                ),
                 (blocks, w_query, lengths, jnp.asarray(rate)),
                 near=(0, 1),
                 smem=(2,),
@@ -391,9 +413,8 @@
     attended = call(
         functools.partial(attend_kernel, pairs, width),
         jax.ShapeDtypeStruct((pairs, QUERY_GROUP * HEAD_SIZE), BF16),
-        (lengths, turns, query_rows, got, slot_key_cache, slot_value_cache),
+        (limits, turns, query_rows, got, slot_key_cache, slot_value_cache),
         near=(4, 5),
-        smem=(0,),
         scratch=(
             pltpu.VMEM(
                 ((pairs + 1) // 2, min(pairs, 2) * QUERY_GROUP, slot_key_cache.shape[1]), F32
@@ -406,43 +427,35 @@
     )
 
     mine = attended[None]
-    head_offsets, slot_offsets = [0], [0]
-    for far in outer:
-        arrived = swap(mine, far, count)
-        if far >= devices_of_head:
-            mine = jnp.concatenate([mine, arrived], 0)
-            head_offsets = head_offsets + [o ^ (far // devices_of_head) for o in head_offsets]
-        else:
-            mine = jnp.concatenate([mine, arrived], 1)
+    slot_offsets = [0]
+    for far in bits:
+        if core < far < devices_of_head:
+            mine = jnp.concatenate([mine, swap(mine, far, count)], 1)
             slot_offsets = slot_offsets + [o ^ far for o in slot_offsets]
-    across = swap(mine, bit, count)
+    high, low = bits[0] // devices_of_head, bits[1] // devices_of_head
+    mine = jnp.concatenate([mine, swap(mine, bits[0], count)], 0)
+    across = swap(mine, bits[1], count)
     beside = swap(mine, core, count)
+    slots = (tuple(slot_offsets), tuple(o ^ core for o in slot_offsets))
+    slot_row = slot_of_row.reshape(1, rows)
+    columns = output_projection.shape[1]
+    half = call(
+        functools.partial(first_half_kernel, pairs, (0, high), slots),
+        jax.ShapeDtypeStruct((rows, columns), F32),
+        (slot_row, mine, beside, output_projection),
+        near=(3,),
+        flops=rows * output_projection.size,
+        read=output_projection.size,
+    )
+    across = call(pass_kernel, jax.ShapeDtypeStruct(across.shape, BF16), (across, half))
     both = swap(across, core, count)
-    slot_row = slot_of_row.reshape(1, rows)
-    left = jax.ShapeDtypeStruct((rows, output_projection.shape[0]), BF16)
-    before = call(
-        functools.partial(
-            assemble_kernel,
-            pairs,
-            tuple(head_offsets),
-            tuple(tuple(o ^ b for o in slot_offsets) for b in (0, core, bit)),
-        ),
-        left,
-        (slot_row, mine, beside, across),
-    )
     return call(
-        functools.partial(
-            project_kernel,
-            pairs,
-            tuple(head_offsets),
-            (tuple(o ^ bit ^ core for o in slot_offsets),),
-        ),
-        jax.ShapeDtypeStruct((rows, output_projection.shape[1]), BF16),
-        (slot_row, both, before, output_projection),
+        functools.partial(second_half_kernel, pairs, (low, low ^ high), slots),
+        jax.ShapeDtypeStruct((rows, columns), BF16),
+        (slot_row, across, both, output_projection, half),
         near=(3,),
-        scratch=(pltpu.VMEM(left.shape, BF16),),
-        flops=2 * rows * output_projection.size,
-        read=2 * output_projection.size,
+        flops=rows * output_projection.size,
+        read=output_projection.size,
     )
 
 

time: 54.4 us -> 53 us (0.974)
  waiting for transfers between devices: 18.3 us -> 17.5 us
  Pallas kernels: 12.6 us -> 12 us
    ppermute x9, waiting for transfers between devices: 18.3 us -> 17.5 us  [swap(): return lax.ppermute(array, 'wide', [(i, i ^ bit) for i in range(count)])]
    pallas_call x12 -> x13, Pallas kernels: 12.6 us -> 12 us  [call(): pl.pallas_call(kernel, out_shape=out_shape, in_specs=specs, out_specs=jax...]
  transfers between devices with their start and end apart: 9 -> 9, of which waited for: 8 -> 9; matrix products, arithmetic and copies ran while one was open for 0% -> 0% of each run, Pallas kernels for 8% -> 10%
where the time goes in v4:
time: 53 us; the launch traced here: 52.8 us
  waiting for transfers between devices  17.5 us (33%)
  blocking collectives  14.2 us (27%)
  Pallas kernels  12 us (23%)
  starting transfers between devices  8.93 us (17%)
    ppermute x9, waiting for transfers between devices, swap(): return lax.ppermute(array, 'wide', [(i, i ^ bit) for i in range(count)])  17.5 us
    all_to_all x1, blocking collectives, body(): got = lax.all_to_all(message, 'wide', 0, 0, tiled=True)  14.2 us
    pallas_call x13, Pallas kernels, call(): pl.pallas_call(kernel, out_shape=out_shape, in_specs=specs, out_specs=jax...  12 us
    ppermute x9, starting transfers between devices, swap(): return lax.ppermute(array, 'wide', [(i, i ^ bit) for i in range(count)])  8.93 us
  transfers between devices with their start and end apart: 9, of which 9 were waited for; matrix products, arithmetic and copies ran while one was open for 0% of the time, Pallas kernels for 10%

profile of v4, /device:TPU:0, one launch (start us, length us, event | category | flops | bytes accessed | tf_op | source)
XLA Modules:
  0.0 52.8 jit_solution(14943133756247566168)
XLA Ops:
  0.0 0.0 copy-start.5
  0.0 0.0 copy-start
  0.0 0.0 copy-start.4
  0.0 1.2 %shard_map.109 = (bf16[16,1024]{1,0:T(8,128)(2,1)S(1)}, f32[16,128]{1,0:T(8,128)S(1)}) custom-call(bf16[16,1024]{1,0:T(8,128)(2,1)} %far_tokens.1, bf16[1024]{0:T(1024)(128)(2,1)} %far_gain.1, s32[1,16]{1,0:T(1,128)} %bitcast.10), custom_call_target="tpu_custom_call" | custom-call | tf_op jit(solution)/shard_map/pallas_call | solution.py:35
  1.2 4.1 %collective-permute-start = (bf16[1,16,1024]{2,1,0:T(8,128)(2,1)S(1)}, bf16[1,16,1024]{2,1,0:T(8,128)(2,1)S(1)}, u32[]{:S(2)}, u32[]{:S(2)}) collective-permute-start(bf16[1,16,1024]{2,1,0:T(8,128)(2,1)S(1)} %bitcast.8), channel_id=1, source_target_pairs={{0,8},{1,9},{2,10},{3,11},{4,12},{5,13},{6,14},{7,15},{8,0},{9,1},... | collective-permute-start | bytes 98312 | tf_op jit(solution)/shard_map/ppermute | solution.py:290
  5.3 1.8 %shard_map.110 = (f32[16,512]{1,0:T(8,128)S(1)}, f32[16,512]{1,0:T(8,128)S(1)}) custom-call(bf16[16,1024]{1,0:T(8,128)(2,1)S(1)} %get-tuple-element.12.scaled_ref, bf16[1024,512]{1,0:T(8,128)(2,1)} %far_key.1, bf16[1024,512]{1,0:T(8,128)(2,1)} %far_value.1, bf16[16384,512]{1,0:T(8,128)(2,1)} %weight_ref.9), custom_call_target="tpu_custom_call" | custom-call | flops 33554432 | bytes 67108864 | tf_op jit(solution)/shard_map/pallas_call | solution.py:35
  7.1 0.4 collective-permute-done.arrived_ref
  7.5 2.0 %collective-permute-start.1 = (bf16[2,16,1024]{2,1,0:T(8,128)(2,1)S(1)}, bf16[2,16,1024]{2,1,0:T(8,128)(2,1)S(1)}, u32[]{:S(2)}, u32[]{:S(2)}) collective-permute-start(bf16[2,16,1024]{2,1,0:T(8,128)(2,1)S(1)} %shard_map.111.blocks_ref.mine_ref), channel_id=1, source_target_pairs={{0,4},{1,5},{2,6},{3,7},{4,0},{5,1},{6,2},{7,3},{8,12},{9,13},{10,... | collective-permute-start | bytes 196616 | tf_op jit(solution)/shard_map/ppermute | solution.py:290
  9.6 0.0 copy-done.5
  9.6 0.0 copy-done
  9.6 0.0 copy-done.4
  9.6 0.9 %shard_map.112 = (f32[16,512]{1,0:T(8,128)S(1)}, f32[2,4,128]{2,1,0:T(4,128)S(1)}, s32[4,128]{1,0:T(4,128)S(1)}) custom-call(bf16[2,16,1024]{2,1,0:T(8,128)(2,1)S(1)} %shard_map.111.blocks_ref.mine_ref, bf16[16384,512]{1,0:T(8,128)(2,1)S(1)} %copy-done, s32[16]{0:T(128)S(1)} %copy-done.4, f32[1,128]{1,0:T(1,128)S(1)} %copy-done.5), custom_call_target="tpu_custom_call" | custom-call | flops 33554432 | bytes 2097152 | tf_op jit(solution)/shard_map/pallas_call | solution.py:35
  10.5 1.3 %collective-permute-done.1.arrived_ref = bf16[2,16,1024]{2,1,0:T(8,128)(2,1)S(1)} collective-permute-done((bf16[2,16,1024]{2,1,0:T(8,128)(2,1)S(1)}, bf16[2,16,1024]{2,1,0:T(8,128)(2,1)S(1)}, u32[]{:S(2)}, u32[]{:S(2)}) %collective-permute-start.1) | collective-permute-done | bytes 65568 | tf_op jit(solution)/shard_map/ppermute | solution.py:290
  11.8 2.0 %collective-permute-start.2 = (bf16[4,16,1024]{2,1,0:T(8,128)(2,1)S(1)}, bf16[4,16,1024]{2,1,0:T(8,128)(2,1)S(1)}, u32[]{:S(2)}, u32[]{:S(2)}) collective-permute-start(bf16[4,16,1024]{2,1,0:T(8,128)(2,1)S(1)} %shard_map.113.blocks_ref.mine_ref), channel_id=1, source_target_pairs={{0,2},{1,3},{2,0},{3,1},{4,6},{5,7},{6,4},{7,5},{8,10},{9,11},{10,... | collective-permute-start | bytes 393224 | tf_op jit(solution)/shard_map/ppermute | solution.py:290
  13.8 0.4 shard_map.114.after_ref.total_ref
  14.2 2.6 %collective-permute-done.2.arrived_ref = bf16[4,16,1024]{2,1,0:T(8,128)(2,1)S(1)} collective-permute-done((bf16[4,16,1024]{2,1,0:T(8,128)(2,1)S(1)}, bf16[4,16,1024]{2,1,0:T(8,128)(2,1)S(1)}, u32[]{:S(2)}, u32[]{:S(2)}) %collective-permute-start.2) | collective-permute-done | bytes 131104 | tf_op jit(solution)/shard_map/ppermute | solution.py:290
  16.9 0.0 copy-start.1
  16.9 0.0 copy-start.2
  16.9 0.1 collective-permute-start.3
  17.0 0.0 slice-start
  17.0 0.0 slice-start.1
  17.0 0.7 %shard_map.116.total_ref = f32[16,512]{1,0:T(8,128)S(1)} custom-call(bf16[8,16,1024]{2,1,0:T(8,128)(2,1)S(1)} %shard_map.115.blocks_ref, bf16[16384,512]{1,0:T(8,128)(2,1)S(1)} %copy-done, f32[16,512]{1,0:T(8,128)S(1)} %shard_map.114.after_ref.total_ref), custom_call_target="tpu_custom_call" | custom-call | flops 67108864 | bytes 4194304 | tf_op jit(solution)/shard_map/pallas_call | solution.py:35
  17.7 0.0 copy-start.3
  17.7 0.8 %collective-permute-done.3.blocks_ref = bf16[8,16,1024]{2,1,0:T(8,128)(2,1)S(1)} collective-permute-done((bf16[8,16,1024]{2,1,0:T(8,128)(2,1)S(1)}, bf16[8,16,1024]{2,1,0:T(8,128)(2,1)S(1)}, u32[]{:S(2)}, u32[]{:S(2)}) %collective-permute-start.3) | collective-permute-done | bytes 262176 | tf_op jit(solution)/shard_map/ppermute | solution.py:290
  18.5 0.0 slice-start.2
  18.5 0.0 slice-start.3
  18.5 1.2 %shard_map.117 = f32[16,16,128]{2,1,0:T(8,128)S(1)} custom-call(bf16[8,16,1024]{2,1,0:T(8,128)(2,1)S(1)} %collective-permute-done.3.blocks_ref, bf16[16384,512]{1,0:T(8,128)(2,1)S(1)} %copy-done, f32[16,512]{1,0:T(8,128)S(1)} %shard_map.116.total_ref, f32[16,512]{1,0:T(8,128)S(1)} %get-tuple-element.13.after_ref.key_ref, ...), custom_call_target="tpu_custom_call" | custom-call | flops 134217728 | bytes 8388608 | tf_op jit(solution)/shard_map/pallas_call | solution.py:35
  19.7 14.2 %all_to_all.5.query_ref.rest_ref = f32[16,16,128]{2,1,0:T(8,128)S(1)} all-to-all(f32[16,16,128]{2,1,0:T(8,128)S(1)} %shard_map.117), channel_id=1, replica_groups=mesh['groups'=2,'wide'=16] {'wide'}, dimensions={0} | all-to-all | bytes 262144 | tf_op jit(solution)/shard_map/all_to_all | solution.py:400
  33.8 0.0 copy-done.1
  33.8 0.0 copy-done.2
  33.9 2.3 %shard_map.118 = bf16[4,2048]{1,0:T(4,128)(2,1)S(1)} custom-call(s32[4,128]{1,0:T(4,128)S(1)} %get-tuple-element.14.limits_ref, f32[2,4,128]{2,1,0:T(4,128)S(1)} %get-tuple-element.15.turns_ref, f32[16,16,128]{2,1,0:T(8,128)S(1)} %all_to_all.5.query_ref.rest_ref, f32[16,16,128]{2,1,0:T(8,128)S(1)} %all_to_all.5.query_ref.rest_ref, ...), custom_call_target="tpu_custom_call" | custom-call | flops 134217728 | bytes 8388608 | tf_op jit(solution)/shard_map/pallas_call | solution.py:35
  36.1 0.1 collective-permute-start.4
  36.2 3.7 %collective-permute-done.4 = bf16[1,4,2048]{2,1,0:T(4,128)(2,1)S(1)} collective-permute-done((bf16[1,4,2048]{2,1,0:T(4,128)(2,1)S(1)}, bf16[1,4,2048]{2,1,0:T(4,128)(2,1)S(1)}, u32[]{:S(2)}, u32[]{:S(2)}) %collective-permute-start.4) | collective-permute-done | bytes 16416 | tf_op jit(solution)/shard_map/ppermute | solution.py:290
  39.9 0.5 collective-permute-start.5
  40.4 4.4 %collective-permute-done.5 = bf16[1,8,2048]{2,1,0:T(8,128)(2,1)S(1)} collective-permute-done((bf16[1,8,2048]{2,1,0:T(8,128)(2,1)S(1)}, bf16[1,8,2048]{2,1,0:T(8,128)(2,1)S(1)}, u32[]{:S(2)}, u32[]{:S(2)}) %collective-permute-start.5) | collective-permute-done | bytes 32800 | tf_op jit(solution)/shard_map/ppermute | solution.py:290
  44.8 0.1 collective-permute-start.7
  44.9 0.1 collective-permute-start.6
  45.0 1.2 %collective-permute-done.7.other_ref = bf16[2,8,2048]{2,1,0:T(8,128)(2,1)S(1)} collective-permute-done((bf16[2,8,2048]{2,1,0:T(8,128)(2,1)S(1)}, bf16[2,8,2048]{2,1,0:T(8,128)(2,1)S(1)}, u32[]{:S(2)}, u32[]{:S(2)}) %collective-permute-start.7) | collective-permute-done | bytes 65568 | tf_op jit(solution)/shard_map/ppermute | solution.py:290
  46.2 0.0 slice-done
  46.2 0.0 slice-done.1
  46.2 0.0 copy-done.3
  46.2 0.0 slice-done.2
  46.2 0.0 slice-done.3
  46.2 1.5 %shard_map.119.after_ref.half_ref = f32[16,1024]{1,0:T(8,128)S(1)} custom-call(s32[1,16]{1,0:T(1,128)S(1)} %bitcast.11, bf16[2,8,2048]{2,1,0:T(8,128)(2,1)S(1)} %pad_maximum_fusion.mine_ref, bf16[2,8,2048]{2,1,0:T(8,128)(2,1)S(1)} %collective-permute-done.7.other_ref, bf16[8192,1024]{1,0:T(8,128)(2,1)S(1)} %bitcast.4), custom_call_target="tpu_custom_call" | custom-call | flops 134217728 | bytes 8388608 | tf_op jit(solution)/shard_map/pallas_call | solution.py:35
  47.7 1.8 %collective-permute-done.6.array_ref = bf16[2,8,2048]{2,1,0:T(8,128)(2,1)S(1)} collective-permute-done((bf16[2,8,2048]{2,1,0:T(8,128)(2,1)S(1)}, bf16[2,8,2048]{2,1,0:T(8,128)(2,1)S(1)}, u32[]{:S(2)}, u32[]{:S(2)}) %collective-permute-start.6) | collective-permute-done | bytes 65568 | tf_op jit(solution)/shard_map/ppermute | solution.py:290
  49.4 0.0 collective-permute-start.8
  49.4 1.2 %collective-permute-done.8.other_ref = bf16[2,8,2048]{2,1,0:T(8,128)(2,1)S(1)} collective-permute-done((bf16[2,8,2048]{2,1,0:T(8,128)(2,1)S(1)}, bf16[2,8,2048]{2,1,0:T(8,128)(2,1)S(1)}, u32[]{:S(2)}, u32[]{:S(2)}) %collective-permute-start.8) | collective-permute-done | bytes 65568 | tf_op jit(solution)/shard_map/ppermute | solution.py:290
  50.7 2.1 %shard_map.121 = bf16[16,1024]{1,0:T(8,128)(2,1)} custom-call(s32[1,16]{1,0:T(1,128)S(1)} %bitcast.12, bf16[2,8,2048]{2,1,0:T(8,128)(2,1)S(1)} %shard_map.120.mine_ref, bf16[2,8,2048]{2,1,0:T(8,128)(2,1)S(1)} %collective-permute-done.8.other_ref, bf16[8192,1024]{1,0:T(8,128)(2,1)S(1)} %bitcast.4, f32[16,1024]{1,0:T(8,128)S(1)} %shard_map.119.after_ref.half_ref), custom_call_target="tpu_custom_call" | custom-call | flops 134217728 | bytes 8388608 | tf_op jit(solution)/shard_map/pallas_call | solution.py:35
  (7 shorter events, 0.1 us)
Async XLA Ops:
  0.0 9.6 %copy-start.5 = (f32[1,128]{1,0:T(1,128)S(1)}, f32[1,128]{1,0:T(1,128)}, u32[]{:S(2)}) copy-start(f32[1,128]{1,0:T(1,128)} %constant.2.clone.rate_ref) | copy-start | bytes 1540
  0.0 9.6 %copy-start = (bf16[16384,512]{1,0:T(8,128)(2,1)S(1)}, bf16[16384,512]{1,0:T(8,128)(2,1)}, u32[]{:S(2)}) copy-start(bf16[16384,512]{1,0:T(8,128)(2,1)} %weight_ref.9) | copy-start | bytes 50331652
  0.0 9.6 %copy-start.4 = (s32[16]{0:T(128)S(1)}, s32[16]{0:T(128)}, u32[]{:S(2)}) copy-start(s32[16]{0:T(128)} %lengths_ref.1) | copy-start | bytes 196
  1.2 6.4 %collective-permute-start = (bf16[1,16,1024]{2,1,0:T(8,128)(2,1)S(1)}, bf16[1,16,1024]{2,1,0:T(8,128)(2,1)S(1)}, u32[]{:S(2)}, u32[]{:S(2)}) collective-permute-start(bf16[1,16,1024]{2,1,0:T(8,128)(2,1)S(1)} %bitcast.8), channel_id=1, source_target_pairs={{0,8},{1,9},{2,10},{3,11},{4,12},{5,13},{6,14},{7,15},{8,0},{9,1},... | collective-permute-start | bytes 98312 | tf_op jit(solution)/shard_map/ppermute | solution.py:290
  7.5 4.3 %collective-permute-start.1 = (bf16[2,16,1024]{2,1,0:T(8,128)(2,1)S(1)}, bf16[2,16,1024]{2,1,0:T(8,128)(2,1)S(1)}, u32[]{:S(2)}, u32[]{:S(2)}) collective-permute-start(bf16[2,16,1024]{2,1,0:T(8,128)(2,1)S(1)} %shard_map.111.blocks_ref.mine_ref), channel_id=1, source_target_pairs={{0,4},{1,5},{2,6},{3,7},{4,0},{5,1},{6,2},{7,3},{8,12},{9,13},{10,... | collective-permute-start | bytes 196616 | tf_op jit(solution)/shard_map/ppermute | solution.py:290
  11.8 5.0 %collective-permute-start.2 = (bf16[4,16,1024]{2,1,0:T(8,128)(2,1)S(1)}, bf16[4,16,1024]{2,1,0:T(8,128)(2,1)S(1)}, u32[]{:S(2)}, u32[]{:S(2)}) collective-permute-start(bf16[4,16,1024]{2,1,0:T(8,128)(2,1)S(1)} %shard_map.113.blocks_ref.mine_ref), channel_id=1, source_target_pairs={{0,2},{1,3},{2,0},{3,1},{4,6},{5,7},{6,4},{7,5},{8,10},{9,11},{10,... | collective-permute-start | bytes 393224 | tf_op jit(solution)/shard_map/ppermute | solution.py:290
  16.9 17.0 %copy-start.1 = (bf16[4,4096,128]{2,1,0:T(8,128)(2,1)S(1)}, bf16[4,4096,128]{2,1,0:T(8,128)(2,1)}, u32[]{:S(2)}) copy-start(bf16[4,4096,128]{2,1,0:T(8,128)(2,1)} %keys_ref.1) | copy-start | bytes 12582916
  16.9 17.0 %copy-start.2 = (bf16[4,4096,128]{2,1,0:T(8,128)(2,1)S(1)}, bf16[4,4096,128]{2,1,0:T(8,128)(2,1)}, u32[]{:S(2)}) copy-start(bf16[4,4096,128]{2,1,0:T(8,128)(2,1)} %values_ref.1) | copy-start | bytes 12582916
  16.9 1.6 %collective-permute-start.3 = (bf16[8,16,1024]{2,1,0:T(8,128)(2,1)S(1)}, bf16[8,16,1024]{2,1,0:T(8,128)(2,1)S(1)}, u32[]{:S(2)}, u32[]{:S(2)}) collective-permute-start(bf16[8,16,1024]{2,1,0:T(8,128)(2,1)S(1)} %shard_map.115.blocks_ref), channel_id=1, source_target_pairs={{0,1},{1,0},{2,3},{3,2},{4,5},{5,4},{6,7},{7,6},{8,9},{9,8},{10,11... | collective-permute-start | bytes 786440 | tf_op jit(solution)/shard_map/ppermute | solution.py:290
  17.0 29.2 %slice-start = ((s8[16777216]{0:T(1024)(128)(4,1)}), s8[4194304]{0:T(1024)(128)(4,1)S(1)}, s32[]{:S(2)}) async-start(s8[16777216]{0:T(1024)(128)(4,1)} %bitcast.3), calls=%async_computation.1 | async-start | bytes 8388608
  17.0 29.2 %slice-start.1 = ((s8[16777216]{0:T(1024)(128)(4,1)}), s8[4194304]{0:T(1024)(128)(4,1)S(1)}, s32[]{:S(2)}) async-start(s8[16777216]{0:T(1024)(128)(4,1)} %bitcast.3), calls=%async_computation.2 | async-start | bytes 8388608
  17.7 28.5 %copy-start.3 = (s32[16]{0:T(128)S(1)}, s32[16]{0:T(128)}, u32[]{:S(2)}) copy-start(s32[16]{0:T(128)} %param.13) | copy-start | bytes 196
  18.5 27.7 %slice-start.2 = ((s8[16777216]{0:T(1024)(128)(4,1)}), s8[4194304]{0:T(1024)(128)(4,1)S(1)}, s32[]{:S(2)}) async-start(s8[16777216]{0:T(1024)(128)(4,1)} %bitcast.3), calls=%async_computation.3 | async-start | bytes 8388608
  18.5 27.7 %slice-start.3 = ((s8[16777216]{0:T(1024)(128)(4,1)}), s8[4194304]{0:T(1024)(128)(4,1)S(1)}, s32[]{:S(2)}) async-start(s8[16777216]{0:T(1024)(128)(4,1)} %bitcast.3), calls=%async_computation.4 | async-start | bytes 8388608
  36.1 3.8 %collective-permute-start.4 = (bf16[1,4,2048]{2,1,0:T(4,128)(2,1)S(1)}, bf16[1,4,2048]{2,1,0:T(4,128)(2,1)S(1)}, u32[]{:S(2)}, u32[]{:S(2)}) collective-permute-start(bf16[1,4,2048]{2,1,0:T(4,128)(2,1)S(1)} %bitcast.5), channel_id=1, source_target_pairs={{0,2},{1,3},{2,0},{3,1},{4,6},{5,7},{6,4},{7,5},{8,10},{9,11},{10,... | collective-permute-start | bytes 49160 | tf_op jit(solution)/shard_map/ppermute | solution.py:290
  39.9 4.9 %collective-permute-start.5 = (bf16[1,8,2048]{2,1,0:T(8,128)(2,1)S(1)}, bf16[1,8,2048]{2,1,0:T(8,128)(2,1)S(1)}, u32[]{:S(2)}, u32[]{:S(2)}) collective-permute-start(bf16[1,8,2048]{2,1,0:T(8,128)(2,1)S(1)} %pad_maximum_fusion.1), channel_id=1, source_target_pairs={{0,8},{1,9},{2,10},{3,11},{4,12},{5,13},{6,14},{7,15},{8,0},{9,1},... | collective-permute-start | bytes 98312 | tf_op jit(solution)/shard_map/ppermute | solution.py:290
  44.8 1.3 %collective-permute-start.7 = (bf16[2,8,2048]{2,1,0:T(8,128)(2,1)S(1)}, bf16[2,8,2048]{2,1,0:T(8,128)(2,1)S(1)}, u32[]{:S(2)}, u32[]{:S(2)}) collective-permute-start(bf16[2,8,2048]{2,1,0:T(8,128)(2,1)S(1)} %pad_maximum_fusion.mine_ref), channel_id=1, source_target_pairs={{0,1},{1,0},{2,3},{3,2},{4,5},{5,4},{6,7},{7,6},{8,9},{9,8},{10,11... | collective-permute-start | bytes 196616 | tf_op jit(solution)/shard_map/ppermute | solution.py:290
  44.9 4.5 %collective-permute-start.6 = (bf16[2,8,2048]{2,1,0:T(8,128)(2,1)S(1)}, bf16[2,8,2048]{2,1,0:T(8,128)(2,1)S(1)}, u32[]{:S(2)}, u32[]{:S(2)}) collective-permute-start(bf16[2,8,2048]{2,1,0:T(8,128)(2,1)S(1)} %pad_maximum_fusion.mine_ref), channel_id=1, source_target_pairs={{0,4},{1,5},{2,6},{3,7},{4,0},{5,1},{6,2},{7,3},{8,12},{9,13},{10,... | collective-permute-start | bytes 196616 | tf_op jit(solution)/shard_map/ppermute | solution.py:290
  49.4 1.3 %collective-permute-start.8 = (bf16[2,8,2048]{2,1,0:T(8,128)(2,1)S(1)}, bf16[2,8,2048]{2,1,0:T(8,128)(2,1)S(1)}, u32[]{:S(2)}, u32[]{:S(2)}) collective-permute-start(bf16[2,8,2048]{2,1,0:T(8,128)(2,1)S(1)} %shard_map.120.mine_ref), channel_id=1, source_target_pairs={{0,1},{1,0},{2,3},{3,2},{4,5},{5,4},{6,7},{7,6},{8,9},{9,8},{10,11... | collective-permute-start | bytes 196616 | tf_op jit(solution)/shard_map/ppermute | solution.py:290

commit v5 on v4

--- a/solution.py
+++ b/solution.py
@@ -43,50 +43,71 @@
     )(*operands)
 
 
-def prepare_kernel(far_tokens, far_gain, far_slot, scaled_ref, squares_ref, tokens_ref, gain_ref, slot_ref, sems):
-    copies = [
-        pltpu.make_async_copy(far, near, sems.at[i])
-        for i, (far, near) in enumerate(
-            ((far_tokens, tokens_ref), (far_gain, gain_ref), (far_slot, slot_ref))
-        )
-    ]
+def fetch(pairs, sems):
+    copies = [pltpu.make_async_copy(far, near, sems.at[i]) for i, (far, near) in enumerate(pairs)]
     for copy in copies:
         copy.start()
-    for copy in copies:
+    return copies
+
+
+def picked_rows(slot_ref):
+    rows = slot_ref.shape[1]
+    return lax.broadcasted_iota(jnp.int32, (rows, rows), 0) == slot_ref[...]
+
+
+def prepare_kernel(
+    far_tokens, far_gain, far_slot, far_query, scaled_ref, tokens_ref, gain_ref, slot_ref, sems
+):
+    for copy in fetch(((far_tokens, tokens_ref), (far_gain, gain_ref), (far_slot, slot_ref)), sems):
         copy.wait()
-    rows, features = tokens_ref.shape
-    wide_f = tokens_ref[...].astype(F32)
-    squares = jnp.sum(wide_f * wide_f, axis=1, keepdims=True)
-    gain = gain_ref[...].astype(F32).reshape(1, features)
-    scaled = (wide_f * gain).astype(BF16)
-    picked = lax.broadcasted_iota(jnp.int32, (rows, rows), 0) == slot_ref[...]
+    gain = gain_ref[...].astype(F32).reshape(1, gain_ref.shape[0])
+    scaled = (tokens_ref[...].astype(F32) * gain).astype(BF16)
     scaled_ref[...] = jnp.dot(
-        picked.astype(BF16), scaled, preferred_element_type=F32
+        picked_rows(slot_ref).astype(BF16), scaled, preferred_element_type=F32
     ).astype(BF16)
-    turned = jnp.sum(jnp.where(picked, jnp.transpose(jnp.broadcast_to(squares, (rows, rows))), 0.0), axis=1, keepdims=True)
-    squares_ref[...] = jnp.broadcast_to(turned, squares_ref.shape)
-
-
-def pass_kernel(array_ref, after_ref, same_ref):
-    same_ref[...] = array_ref[...]
-
-
-def join_kernel(mine_ref, arrived_ref, after_ref, joined_ref):
+
+
+def pass_kernel(array_ref, *refs):
+    refs[-1][...] = array_ref[...]
+
+
+def join_kernel(mine_ref, arrived_ref, *refs):
+    joined_ref = refs[-1]
     count = mine_ref.shape[0]
     joined_ref[:count] = mine_ref[...]
     joined_ref[count:] = arrived_ref[...]
 
 
-def share_kernel(scaled_ref, far_key, far_value, far_query, key_share_ref, value_share_ref, key_ref, value_ref, sems):
-    copies = [
-        pltpu.make_async_copy(far_key, key_ref, sems.at[0]),
-        pltpu.make_async_copy(far_value, value_ref, sems.at[1]),
-    ]
-    for copy in copies:
-        copy.start()
+def share_kernel(
+    scaled_ref,
+    far_tokens,
+    far_slot,
+    far_key,
+    far_value,
+    after_ref,
+    key_share_ref,
+    value_share_ref,
+    squares_ref,
+    tokens_ref,
+    slot_ref,
+    key_ref,
+    value_ref,
+    sems,
+):
+    copies = fetch(
+        ((far_tokens, tokens_ref), (far_slot, slot_ref), (far_key, key_ref), (far_value, value_ref)), sems
+    )
     copies[0].wait()
+    copies[1].wait()
+    rows = tokens_ref.shape[0]
+    wide_f = tokens_ref[...].astype(F32)
+    squares = jnp.sum(wide_f * wide_f, axis=1, keepdims=True)
+    turned = jnp.transpose(jnp.broadcast_to(squares, (rows, rows)))
+    squares = jnp.sum(jnp.where(picked_rows(slot_ref), turned, 0.0), axis=1, keepdims=True)
+    squares_ref[...] = jnp.broadcast_to(squares, squares_ref.shape)
+    copies[2].wait()
     key_share_ref[...] = jnp.dot(scaled_ref[...], key_ref[...], preferred_element_type=F32)
-    copies[1].wait()
+    copies[3].wait()
     value_share_ref[...] = jnp.dot(scaled_ref[...], value_ref[...], preferred_element_type=F32)
 
 
@@ -311,22 +332,20 @@
     devices_of_head = rows // pairs
     bits = [1 << b for b in reversed(range(count.bit_length() - 1))]
 
-    scaled, squares = call(
+    slot_row = slot_of_row.reshape(1, rows)
+    scaled = call(
         prepare_kernel,
-        (
-            jax.ShapeDtypeStruct((rows, features), BF16),
-            jax.ShapeDtypeStruct((rows, HEAD_SIZE), F32),
-        ),
-        (tokens, norm_gain, slot_of_row.reshape(1, rows)),
-        far=(0, 1, 2),
+        jax.ShapeDtypeStruct((rows, features), BF16),
+        (tokens, norm_gain, slot_row, w_query),
+        far=(0, 1, 2, 3),
         scratch=(
             pltpu.VMEM((rows, features), BF16),
             pltpu.VMEM((features,), BF16),
             pltpu.VMEM((1, rows), jnp.int32),
             pltpu.SemaphoreType.DMA((3,)),
         ),
-    )
-
+        read=8 * w_query.size,
+    )
     index = np.arange(HEAD_SIZE)
     rate = (ROPE_BASE ** (-(index - index % 2) / HEAD_SIZE)).astype(np.float32)[None, :]
     totals = jax.ShapeDtypeStruct((rows, query_columns), F32)
@@ -342,27 +361,12 @@
             read=2 * len(offsets) * features * query_columns,
         )
 
-    *outer, bit, core = bits
-    blocks, offsets, new, total = scaled[None], [0], [0], None
-    for far in (*outer, bit):
+    core, half = bits[-1], count // 2
+    blocks, offsets, new, after = scaled[None], [0], [0], None
+    for far in bits[:-1]:
         arrived = swap(blocks, far, count)
-        if len(offsets) == 1:
-            after = key_share, value_share = call(
-                share_kernel,
-                (shares, shares),
-                (scaled, key_projection, value_projection, w_query),
-                near=(0,),
-                far=(1, 2, 3),
-                scratch=(
-                    pltpu.VMEM(key_projection.shape, BF16),
-                    pltpu.VMEM(value_projection.shape, BF16),
-                    pltpu.SemaphoreType.DMA((2,)),
-                ),
-                flops=4 * rows * key_projection.size,
-                read=8 * w_query.size,
-            )
-        elif total is None:
-            after = total, turns, limits = call(
+        if len(offsets) == 2:
+            after, turns, limits = call(
                 functools.partial(query_turns_kernel, tuple(offsets), pairs),
                 (
                     totals,
@@ -375,26 +379,49 @@
                 flops=2 * rows * len(offsets) * features * query_columns,
                 read=2 * len(offsets) * features * query_columns,
             )
-        else:
-            total = query(new, len(offsets) - len(new), blocks, total)
-            after = (total,)
+        elif len(offsets) > 2:
+            after = query(new, len(offsets) - len(new), blocks, after)
+        if len(offsets) == 4:
+            key_share, value_share, squares = call(
+                share_kernel,
+                (shares, shares, jax.ShapeDtypeStruct((rows, HEAD_SIZE), F32)),
+                (scaled, tokens, slot_row, key_projection, value_projection, after),
+                near=(0,),
+                far=(1, 2, 3, 4),
+                scratch=(
+                    pltpu.VMEM((rows, features), BF16),
+                    pltpu.VMEM((1, rows), jnp.int32),
+                    pltpu.VMEM(key_projection.shape, BF16),
+                    pltpu.VMEM(value_projection.shape, BF16),
+                    pltpu.SemaphoreType.DMA((4,)),
+                ),
+                flops=4 * rows * key_projection.size,
+                read=4 * key_projection.size,
+            )
+        new = [o ^ far for o in offsets]
+        if 2 * len(offsets) == half:
+            break
         blocks = call(
             join_kernel,
             jax.ShapeDtypeStruct((2 * len(offsets), rows, features), BF16),
-            (blocks, arrived, after[0]),
+            (blocks, arrived) if after is None else (blocks, arrived, key_share if len(offsets) == 4 else after),
         )
-        new = [o ^ far for o in offsets]
         offsets = offsets + new
-    arrived = swap(blocks, core, count)
-    total = query(new, len(offsets) - len(new), blocks, total)
+    blocks = call(
+        pass_kernel, jax.ShapeDtypeStruct(blocks.shape, BF16), (blocks, arrived, after, key_share)
+    )
+    first = swap(blocks, core, count)
+    last = swap(arrived, core, count)
+    total = query(new, 0, arrived, after)
+    total = query([o ^ core for o in offsets], 0, first, total)
     sent = held // KEY_VALUE_HEADS if held % KEY_VALUE_HEADS == 0 else held
     message = call(
-        functools.partial(message_kernel, tuple(o ^ core for o in offsets), pairs),
+        functools.partial(message_kernel, tuple(o ^ core for o in new), pairs),
         jax.ShapeDtypeStruct((count, pairs * (sent + 3), HEAD_SIZE), F32),
-        (arrived, w_query, total, key_share, value_share, squares),
+        (last, w_query, total, key_share, value_share, squares),
         near=(0, 1),
-        flops=2 * arrived.size * query_columns,
-        read=2 * len(offsets) * features * query_columns,
+        flops=2 * last.size * query_columns,
+        read=2 * len(new) * features * query_columns,
     )
 
     got = lax.all_to_all(message, "wide", 0, 0, tiled=True)
@@ -437,7 +464,6 @@
     across = swap(mine, bits[1], count)
     beside = swap(mine, core, count)
     slots = (tuple(slot_offsets), tuple(o ^ core for o in slot_offsets))
-    slot_row = slot_of_row.reshape(1, rows)
     columns = output_projection.shape[1]
     half = call(
         functools.partial(first_half_kernel, pairs, (0, high), slots),

time: 53 us -> 52.8 us (level)
    ppermute x9 -> x10, starting transfers between devices: 8.93 us -> 8.73 us  [swap(): return lax.ppermute(array, 'wide', [(i, i ^ bit) for i in range(count)])]
    pallas_call x13 -> x14, Pallas kernels: 12 us -> 12 us  [call(): pl.pallas_call(kernel, out_shape=out_shape, in_specs=specs, out_specs=jax...]
    ppermute x9 -> x10, waiting for transfers between devices: 17.5 us -> 17.5 us  [swap(): return lax.ppermute(array, 'wide', [(i, i ^ bit) for i in range(count)])]
  transfers between devices with their start and end apart: 9 -> 10, of which waited for: 9 -> 9; matrix products, arithmetic and copies ran while one was open for 0% -> 0% of each run, Pallas kernels for 10% -> 11%
where the time goes in v5:
time: 52.8 us; the launch traced here: 52.6 us
  waiting for transfers between devices  17.5 us (33%)
  blocking collectives  14.2 us (27%)
  Pallas kernels  12 us (23%)
  starting transfers between devices  8.73 us (17%)
    ppermute x10, waiting for transfers between devices, swap(): return lax.ppermute(array, 'wide', [(i, i ^ bit) for i in range(count)])  17.5 us
    all_to_all x1, blocking collectives, body(): got = lax.all_to_all(message, 'wide', 0, 0, tiled=True)  14.2 us
    pallas_call x14, Pallas kernels, call(): pl.pallas_call(kernel, out_shape=out_shape, in_specs=specs, out_specs=jax...  12 us
    ppermute x10, starting transfers between devices, swap(): return lax.ppermute(array, 'wide', [(i, i ^ bit) for i in range(count)])  8.73 us
  transfers between devices with their start and end apart: 10, of which 9 were waited for; matrix products, arithmetic and copies ran while one was open for 0% of the time, Pallas kernels for 11%

profile of v5, /device:TPU:0, one launch (start us, length us, event | category | flops | bytes accessed | tf_op | source)
XLA Modules:
  0.0 52.6 jit_solution(2590571286934797920)
XLA Ops:
  0.0 0.0 copy-start.5
  0.0 0.0 copy-start
  0.0 1.1 %shard_map.109.scaled_ref = bf16[16,1024]{1,0:T(8,128)(2,1)S(1)} custom-call(bf16[16,1024]{1,0:T(8,128)(2,1)} %far_tokens.3, bf16[1024]{0:T(1024)(128)(2,1)} %far_gain.1, s32[1,16]{1,0:T(1,128)} %bitcast.10, bf16[16384,512]{1,0:T(8,128)(2,1)} %weight_ref.11), custom_call_target="tpu_custom_call" | custom-call | bytes 67108864 | tf_op jit(solution)/shard_map/pallas_call | solution.py:35
  1.1 4.1 %collective-permute-start = (bf16[1,16,1024]{2,1,0:T(8,128)(2,1)S(1)}, bf16[1,16,1024]{2,1,0:T(8,128)(2,1)S(1)}, u32[]{:S(2)}, u32[]{:S(2)}) collective-permute-start(bf16[1,16,1024]{2,1,0:T(8,128)(2,1)S(1)} %bitcast.5), channel_id=1, source_target_pairs={{0,8},{1,9},{2,10},{3,11},{4,12},{5,13},{6,14},{7,15},{8,0},{9,1},... | collective-permute-start | bytes 98312 | tf_op jit(solution)/shard_map/ppermute | solution.py:311
  5.2 2.2 %collective-permute-done.arrived_ref = bf16[1,16,1024]{2,1,0:T(8,128)(2,1)S(1)} collective-permute-done((bf16[1,16,1024]{2,1,0:T(8,128)(2,1)S(1)}, bf16[1,16,1024]{2,1,0:T(8,128)(2,1)S(1)}, u32[]{:S(2)}, u32[]{:S(2)}) %collective-permute-start) | collective-permute-done | bytes 32800 | tf_op jit(solution)/shard_map/ppermute | solution.py:311
  7.4 1.6 %collective-permute-start.1 = (bf16[2,16,1024]{2,1,0:T(8,128)(2,1)S(1)}, bf16[2,16,1024]{2,1,0:T(8,128)(2,1)S(1)}, u32[]{:S(2)}, u32[]{:S(2)}) collective-permute-start(bf16[2,16,1024]{2,1,0:T(8,128)(2,1)S(1)} %shard_map.110.blocks_ref.mine_ref), channel_id=1, source_target_pairs={{0,4},{1,5},{2,6},{3,7},{4,0},{5,1},{6,2},{7,3},{8,12},{9,13},{10,... | collective-permute-start | bytes 196616 | tf_op jit(solution)/shard_map/ppermute | solution.py:311
  9.0 0.0 copy-done.5
  9.0 0.0 copy-done
  9.0 0.0 copy-done.4
  9.0 0.9 %shard_map.111 = (f32[16,512]{1,0:T(8,128)S(1)}, f32[2,4,128]{2,1,0:T(4,128)S(1)}, s32[4,128]{1,0:T(4,128)S(1)}) custom-call(bf16[2,16,1024]{2,1,0:T(8,128)(2,1)S(1)} %shard_map.110.blocks_ref.mine_ref, bf16[16384,512]{1,0:T(8,128)(2,1)S(1)} %copy-done, s32[16]{0:T(128)S(1)} %copy-done.4, f32[1,128]{1,0:T(1,128)S(1)} %copy-done.5), custom_call_target="tpu_custom_call" | custom-call | flops 33554432 | bytes 2097152 | tf_op jit(solution)/shard_map/pallas_call | solution.py:35
  9.9 1.8 %collective-permute-done.1.arrived_ref = bf16[2,16,1024]{2,1,0:T(8,128)(2,1)S(1)} collective-permute-done((bf16[2,16,1024]{2,1,0:T(8,128)(2,1)S(1)}, bf16[2,16,1024]{2,1,0:T(8,128)(2,1)S(1)}, u32[]{:S(2)}, u32[]{:S(2)}) %collective-permute-start.1) | collective-permute-done | bytes 65568 | tf_op jit(solution)/shard_map/ppermute | solution.py:311
  11.7 1.8 %collective-permute-start.2 = (bf16[4,16,1024]{2,1,0:T(8,128)(2,1)S(1)}, bf16[4,16,1024]{2,1,0:T(8,128)(2,1)S(1)}, u32[]{:S(2)}, u32[]{:S(2)}) collective-permute-start(bf16[4,16,1024]{2,1,0:T(8,128)(2,1)S(1)} %shard_map.112.blocks_ref.array_ref), channel_id=1, source_target_pairs={{0,2},{1,3},{2,0},{3,1},{4,6},{5,7},{6,4},{7,5},{8,10},{9,11},{10,... | collective-permute-start | bytes 393224 | tf_op jit(solution)/shard_map/ppermute | solution.py:311
  13.5 0.4 shard_map.113.after_ref.refs_1_.total_ref
  13.9 1.9 %shard_map.114 = (f32[16,512]{1,0:T(8,128)S(1)}, f32[16,512]{1,0:T(8,128)S(1)}, f32[16,128]{1,0:T(8,128)S(1)}) custom-call(bf16[16,1024]{1,0:T(8,128)(2,1)S(1)} %shard_map.109.scaled_ref, bf16[16,1024]{1,0:T(8,128)(2,1)} %far_tokens.3, s32[1,16]{1,0:T(1,128)} %bitcast.11, bf16[1024,512]{1,0:T(8,128)(2,1)} %far_key.1, bf16[1024,512]{1,0:T(8,128)(2,1)} %far_value.1, ...), custom_call_target="tpu_custom_call" | custom-call | flops 33554432 | bytes 2097152 | tf_op jit(solution)/shard_map/pallas_call | solution.py:35
  15.8 1.0 %collective-permute-done.2.refs_0_.blocks_ref = bf16[4,16,1024]{2,1,0:T(8,128)(2,1)S(1)} collective-permute-done((bf16[4,16,1024]{2,1,0:T(8,128)(2,1)S(1)}, bf16[4,16,1024]{2,1,0:T(8,128)(2,1)S(1)}, u32[]{:S(2)}, u32[]{:S(2)}) %collective-permute-start.2) | collective-permute-done | bytes 131104 | tf_op jit(solution)/shard_map/ppermute | solution.py:311
  16.8 0.1 collective-permute-start.4
  16.8 0.5 collective-permute-start.3
  17.3 0.6 %shard_map.116.total_ref = f32[16,512]{1,0:T(8,128)S(1)} custom-call(bf16[4,16,1024]{2,1,0:T(8,128)(2,1)S(1)} %collective-permute-done.2.refs_0_.blocks_ref, bf16[16384,512]{1,0:T(8,128)(2,1)S(1)} %copy-done, f32[16,512]{1,0:T(8,128)S(1)} %shard_map.113.after_ref.refs_1_.total_ref), custom_call_target="tpu_custom_call" | custom-call | flops 67108864 | bytes 4194304 | tf_op jit(solution)/shard_map/pallas_call | solution.py:35
  18.0 0.0 copy-start.1
  18.0 0.0 copy-start.2
  18.0 0.2 collective-permute-done.4.blocks_ref
  18.2 0.0 slice-start
  18.2 0.6 %shard_map.117.total_ref = f32[16,512]{1,0:T(8,128)S(1)} custom-call(bf16[4,16,1024]{2,1,0:T(8,128)(2,1)S(1)} %collective-permute-done.4.blocks_ref, bf16[16384,512]{1,0:T(8,128)(2,1)S(1)} %copy-done, f32[16,512]{1,0:T(8,128)S(1)} %shard_map.116.total_ref), custom_call_target="tpu_custom_call" | custom-call | flops 67108864 | bytes 4194304 | tf_op jit(solution)/shard_map/pallas_call | solution.py:35
  18.8 0.0 collective-permute-done.3.blocks_ref
  18.8 0.0 slice-start.2
  18.9 0.0 slice-start.3
  18.9 0.7 %shard_map.118 = f32[16,16,128]{2,1,0:T(8,128)S(1)} custom-call(bf16[4,16,1024]{2,1,0:T(8,128)(2,1)S(1)} %collective-permute-done.3.blocks_ref, bf16[16384,512]{1,0:T(8,128)(2,1)S(1)} %copy-done, f32[16,512]{1,0:T(8,128)S(1)} %shard_map.117.total_ref, f32[16,512]{1,0:T(8,128)S(1)} %get-tuple-element.14.refs_2_.key_ref, ...), custom_call_target="tpu_custom_call" | custom-call | flops 67108864 | bytes 4194304 | tf_op jit(solution)/shard_map/pallas_call | solution.py:35
  19.5 14.2 %all_to_all.5.query_ref.rest_ref = f32[16,16,128]{2,1,0:T(8,128)S(1)} all-to-all(f32[16,16,128]{2,1,0:T(8,128)S(1)} %shard_map.118), channel_id=1, replica_groups=mesh['groups'=2,'wide'=16] {'wide'}, dimensions={0} | all-to-all | bytes 262144 | tf_op jit(solution)/shard_map/all_to_all | solution.py:427
  33.7 0.0 copy-done.1
  33.7 0.0 copy-done.2
  33.7 2.3 %shard_map.119 = bf16[4,2048]{1,0:T(4,128)(2,1)S(1)} custom-call(s32[4,128]{1,0:T(4,128)S(1)} %get-tuple-element.11.limits_ref, f32[2,4,128]{2,1,0:T(4,128)S(1)} %get-tuple-element.12.turns_ref, f32[16,16,128]{2,1,0:T(8,128)S(1)} %all_to_all.5.query_ref.rest_ref, f32[16,16,128]{2,1,0:T(8,128)S(1)} %all_to_all.5.query_ref.rest_ref, ...), custom_call_target="tpu_custom_call" | custom-call | flops 134217728 | bytes 8388608 | tf_op jit(solution)/shard_map/pallas_call | solution.py:35
  36.0 0.1 collective-permute-start.5
  36.0 3.7 %collective-permute-done.5 = bf16[1,4,2048]{2,1,0:T(4,128)(2,1)S(1)} collective-permute-done((bf16[1,4,2048]{2,1,0:T(4,128)(2,1)S(1)}, bf16[1,4,2048]{2,1,0:T(4,128)(2,1)S(1)}, u32[]{:S(2)}, u32[]{:S(2)}) %collective-permute-start.5) | collective-permute-done | bytes 16416 | tf_op jit(solution)/shard_map/ppermute | solution.py:311
  39.8 0.5 collective-permute-start.6
  40.3 4.4 %collective-permute-done.6 = bf16[1,8,2048]{2,1,0:T(8,128)(2,1)S(1)} collective-permute-done((bf16[1,8,2048]{2,1,0:T(8,128)(2,1)S(1)}, bf16[1,8,2048]{2,1,0:T(8,128)(2,1)S(1)}, u32[]{:S(2)}, u32[]{:S(2)}) %collective-permute-start.6) | collective-permute-done | bytes 32800 | tf_op jit(solution)/shard_map/ppermute | solution.py:311
  44.7 0.1 collective-permute-start.8
  44.8 0.1 collective-permute-start.7
  44.8 1.2 %collective-permute-done.8.other_ref = bf16[2,8,2048]{2,1,0:T(8,128)(2,1)S(1)} collective-permute-done((bf16[2,8,2048]{2,1,0:T(8,128)(2,1)S(1)}, bf16[2,8,2048]{2,1,0:T(8,128)(2,1)S(1)}, u32[]{:S(2)}, u32[]{:S(2)}) %collective-permute-start.8) | collective-permute-done | bytes 65568 | tf_op jit(solution)/shard_map/ppermute | solution.py:311
  46.0 0.0 slice-done
  46.0 0.0 slice-done.1
  46.0 0.0 copy-done.3
  46.0 0.0 slice-done.2
  46.0 0.0 slice-done.3
  46.0 1.5 %shard_map.120.refs_0_.half_ref = f32[16,1024]{1,0:T(8,128)S(1)} custom-call(s32[1,16]{1,0:T(1,128)S(1)} %bitcast.12, bf16[2,8,2048]{2,1,0:T(8,128)(2,1)S(1)} %pad_maximum_fusion.mine_ref, bf16[2,8,2048]{2,1,0:T(8,128)(2,1)S(1)} %collective-permute-done.8.other_ref, bf16[8192,1024]{1,0:T(8,128)(2,1)S(1)} %bitcast.4), custom_call_target="tpu_custom_call" | custom-call | flops 134217728 | bytes 8388608 | tf_op jit(solution)/shard_map/pallas_call | solution.py:35
  47.5 1.8 %collective-permute-done.7.array_ref = bf16[2,8,2048]{2,1,0:T(8,128)(2,1)S(1)} collective-permute-done((bf16[2,8,2048]{2,1,0:T(8,128)(2,1)S(1)}, bf16[2,8,2048]{2,1,0:T(8,128)(2,1)S(1)}, u32[]{:S(2)}, u32[]{:S(2)}) %collective-permute-start.7) | collective-permute-done | bytes 65568 | tf_op jit(solution)/shard_map/ppermute | solution.py:311
  49.3 0.0 collective-permute-start.9
  49.3 1.2 %collective-permute-done.9.other_ref = bf16[2,8,2048]{2,1,0:T(8,128)(2,1)S(1)} collective-permute-done((bf16[2,8,2048]{2,1,0:T(8,128)(2,1)S(1)}, bf16[2,8,2048]{2,1,0:T(8,128)(2,1)S(1)}, u32[]{:S(2)}, u32[]{:S(2)}) %collective-permute-start.9) | collective-permute-done | bytes 65568 | tf_op jit(solution)/shard_map/ppermute | solution.py:311
  50.5 2.1 %shard_map.122 = bf16[16,1024]{1,0:T(8,128)(2,1)} custom-call(s32[1,16]{1,0:T(1,128)S(1)} %bitcast.13, bf16[2,8,2048]{2,1,0:T(8,128)(2,1)S(1)} %shard_map.121.mine_ref, bf16[2,8,2048]{2,1,0:T(8,128)(2,1)S(1)} %collective-permute-done.9.other_ref, bf16[8192,1024]{1,0:T(8,128)(2,1)S(1)} %bitcast.4, f32[16,1024]{1,0:T(8,128)S(1)} %shard_map.120.refs_0_.half_ref), custom_call_target="tpu_custom_call" | custom-call | flops 134217728 | bytes 8388608 | tf_op jit(solution)/shard_map/pallas_call | solution.py:35
  (10 shorter events, 0.1 us)
Async XLA Ops:
  0.0 9.0 %copy-start.5 = (f32[1,128]{1,0:T(1,128)S(1)}, f32[1,128]{1,0:T(1,128)}, u32[]{:S(2)}) copy-start(f32[1,128]{1,0:T(1,128)} %constant.2.clone.rate_ref) | copy-start | bytes 1540
  0.0 9.0 %copy-start = (bf16[16384,512]{1,0:T(8,128)(2,1)S(1)}, bf16[16384,512]{1,0:T(8,128)(2,1)}, u32[]{:S(2)}) copy-start(bf16[16384,512]{1,0:T(8,128)(2,1)} %weight_ref.11) | copy-start | bytes 50331652
  0.0 9.0 %copy-start.4 = (s32[16]{0:T(128)S(1)}, s32[16]{0:T(128)}, u32[]{:S(2)}) copy-start(s32[16]{0:T(128)} %lengths_ref.1) | copy-start | bytes 196
  1.1 6.4 %collective-permute-start = (bf16[1,16,1024]{2,1,0:T(8,128)(2,1)S(1)}, bf16[1,16,1024]{2,1,0:T(8,128)(2,1)S(1)}, u32[]{:S(2)}, u32[]{:S(2)}) collective-permute-start(bf16[1,16,1024]{2,1,0:T(8,128)(2,1)S(1)} %bitcast.5), channel_id=1, source_target_pairs={{0,8},{1,9},{2,10},{3,11},{4,12},{5,13},{6,14},{7,15},{8,0},{9,1},... | collective-permute-start | bytes 98312 | tf_op jit(solution)/shard_map/ppermute | solution.py:311
  7.4 4.3 %collective-permute-start.1 = (bf16[2,16,1024]{2,1,0:T(8,128)(2,1)S(1)}, bf16[2,16,1024]{2,1,0:T(8,128)(2,1)S(1)}, u32[]{:S(2)}, u32[]{:S(2)}) collective-permute-start(bf16[2,16,1024]{2,1,0:T(8,128)(2,1)S(1)} %shard_map.110.blocks_ref.mine_ref), channel_id=1, source_target_pairs={{0,4},{1,5},{2,6},{3,7},{4,0},{5,1},{6,2},{7,3},{8,12},{9,13},{10,... | collective-permute-start | bytes 196616 | tf_op jit(solution)/shard_map/ppermute | solution.py:311
  11.7 5.0 %collective-permute-start.2 = (bf16[4,16,1024]{2,1,0:T(8,128)(2,1)S(1)}, bf16[4,16,1024]{2,1,0:T(8,128)(2,1)S(1)}, u32[]{:S(2)}, u32[]{:S(2)}) collective-permute-start(bf16[4,16,1024]{2,1,0:T(8,128)(2,1)S(1)} %shard_map.112.blocks_ref.array_ref), channel_id=1, source_target_pairs={{0,2},{1,3},{2,0},{3,1},{4,6},{5,7},{6,4},{7,5},{8,10},{9,11},{10,... | collective-permute-start | bytes 393224 | tf_op jit(solution)/shard_map/ppermute | solution.py:311
  16.8 1.4 %collective-permute-start.4 = (bf16[4,16,1024]{2,1,0:T(8,128)(2,1)S(1)}, bf16[4,16,1024]{2,1,0:T(8,128)(2,1)S(1)}, u32[]{:S(2)}, u32[]{:S(2)}) collective-permute-start(bf16[4,16,1024]{2,1,0:T(8,128)(2,1)S(1)} %shard_map.115), channel_id=1, source_target_pairs={{0,1},{1,0},{2,3},{3,2},{4,5},{5,4},{6,7},{7,6},{8,9},{9,8},{10,11... | collective-permute-start | bytes 393224 | tf_op jit(solution)/shard_map/ppermute | solution.py:311
  16.8 2.0 %collective-permute-start.3 = (bf16[4,16,1024]{2,1,0:T(8,128)(2,1)S(1)}, bf16[4,16,1024]{2,1,0:T(8,128)(2,1)S(1)}, u32[]{:S(2)}, u32[]{:S(2)}) collective-permute-start(bf16[4,16,1024]{2,1,0:T(8,128)(2,1)S(1)} %collective-permute-done.2.refs_0_.blocks_ref), channel_id=1, source_target_pairs={{0,1},{1,0},{2,3},{3,2},{4,5},{5,4},{6,7},{7,6},{8,9},{9,8},{10,11... | collective-permute-start | bytes 393224 | tf_op jit(solution)/shard_map/ppermute | solution.py:311
  18.0 15.7 %copy-start.1 = (bf16[4,4096,128]{2,1,0:T(8,128)(2,1)S(1)}, bf16[4,4096,128]{2,1,0:T(8,128)(2,1)}, u32[]{:S(2)}) copy-start(bf16[4,4096,128]{2,1,0:T(8,128)(2,1)} %keys_ref.1) | copy-start | bytes 12582916
  18.0 15.7 %copy-start.2 = (bf16[4,4096,128]{2,1,0:T(8,128)(2,1)S(1)}, bf16[4,4096,128]{2,1,0:T(8,128)(2,1)}, u32[]{:S(2)}) copy-start(bf16[4,4096,128]{2,1,0:T(8,128)(2,1)} %values_ref.1) | copy-start | bytes 12582916
  18.2 27.8 %slice-start = ((s8[16777216]{0:T(1024)(128)(4,1)}), s8[4194304]{0:T(1024)(128)(4,1)S(1)}, s32[]{:S(2)}) async-start(s8[16777216]{0:T(1024)(128)(4,1)} %bitcast.3), calls=%async_computation.1 | async-start | bytes 8388608
  18.2 27.8 %slice-start.1 = ((s8[16777216]{0:T(1024)(128)(4,1)}), s8[4194304]{0:T(1024)(128)(4,1)S(1)}, s32[]{:S(2)}) async-start(s8[16777216]{0:T(1024)(128)(4,1)} %bitcast.3), calls=%async_computation.2 | async-start | bytes 8388608
  18.8 27.2 %copy-start.3 = (s32[16]{0:T(128)S(1)}, s32[16]{0:T(128)}, u32[]{:S(2)}) copy-start(s32[16]{0:T(128)} %param.13) | copy-start | bytes 196
  18.8 27.2 %slice-start.2 = ((s8[16777216]{0:T(1024)(128)(4,1)}), s8[4194304]{0:T(1024)(128)(4,1)S(1)}, s32[]{:S(2)}) async-start(s8[16777216]{0:T(1024)(128)(4,1)} %bitcast.3), calls=%async_computation.3 | async-start | bytes 8388608
  18.9 27.2 %slice-start.3 = ((s8[16777216]{0:T(1024)(128)(4,1)}), s8[4194304]{0:T(1024)(128)(4,1)S(1)}, s32[]{:S(2)}) async-start(s8[16777216]{0:T(1024)(128)(4,1)} %bitcast.3), calls=%async_computation.4 | async-start | bytes 8388608
  36.0 3.8 %collective-permute-start.5 = (bf16[1,4,2048]{2,1,0:T(4,128)(2,1)S(1)}, bf16[1,4,2048]{2,1,0:T(4,128)(2,1)S(1)}, u32[]{:S(2)}, u32[]{:S(2)}) collective-permute-start(bf16[1,4,2048]{2,1,0:T(4,128)(2,1)S(1)} %bitcast.7), channel_id=1, source_target_pairs={{0,2},{1,3},{2,0},{3,1},{4,6},{5,7},{6,4},{7,5},{8,10},{9,11},{10,... | collective-permute-start | bytes 49160 | tf_op jit(solution)/shard_map/ppermute | solution.py:311
  39.8 4.9 %collective-permute-start.6 = (bf16[1,8,2048]{2,1,0:T(8,128)(2,1)S(1)}, bf16[1,8,2048]{2,1,0:T(8,128)(2,1)S(1)}, u32[]{:S(2)}, u32[]{:S(2)}) collective-permute-start(bf16[1,8,2048]{2,1,0:T(8,128)(2,1)S(1)} %pad_maximum_fusion.1), channel_id=1, source_target_pairs={{0,8},{1,9},{2,10},{3,11},{4,12},{5,13},{6,14},{7,15},{8,0},{9,1},... | collective-permute-start | bytes 98312 | tf_op jit(solution)/shard_map/ppermute | solution.py:311
  44.7 1.3 %collective-permute-start.8 = (bf16[2,8,2048]{2,1,0:T(8,128)(2,1)S(1)}, bf16[2,8,2048]{2,1,0:T(8,128)(2,1)S(1)}, u32[]{:S(2)}, u32[]{:S(2)}) collective-permute-start(bf16[2,8,2048]{2,1,0:T(8,128)(2,1)S(1)} %pad_maximum_fusion.mine_ref), channel_id=1, source_target_pairs={{0,1},{1,0},{2,3},{3,2},{4,5},{5,4},{6,7},{7,6},{8,9},{9,8},{10,11... | collective-permute-start | bytes 196616 | tf_op jit(solution)/shard_map/ppermute | solution.py:311
  44.8 4.5 %collective-permute-start.7 = (bf16[2,8,2048]{2,1,0:T(8,128)(2,1)S(1)}, bf16[2,8,2048]{2,1,0:T(8,128)(2,1)S(1)}, u32[]{:S(2)}, u32[]{:S(2)}) collective-permute-start(bf16[2,8,2048]{2,1,0:T(8,128)(2,1)S(1)} %pad_maximum_fusion.mine_ref), channel_id=1, source_target_pairs={{0,4},{1,5},{2,6},{3,7},{4,0},{5,1},{6,2},{7,3},{8,12},{9,13},{10,... | collective-permute-start | bytes 196616 | tf_op jit(solution)/shard_map/ppermute | solution.py:311
  49.3 1.3 %collective-permute-start.9 = (bf16[2,8,2048]{2,1,0:T(8,128)(2,1)S(1)}, bf16[2,8,2048]{2,1,0:T(8,128)(2,1)S(1)}, u32[]{:S(2)}, u32[]{:S(2)}) collective-permute-start(bf16[2,8,2048]{2,1,0:T(8,128)(2,1)S(1)} %shard_map.121.mine_ref), channel_id=1, source_target_pairs={{0,1},{1,0},{2,3},{3,2},{4,5},{5,4},{6,7},{7,6},{8,9},{9,8},{10,11... | collective-permute-start | bytes 196616 | tf_op jit(solution)/shard_map/ppermute | solution.py:311

commit v6 on v5

--- a/solution.py
+++ b/solution.py
@@ -79,15 +79,19 @@
 
 
 def share_kernel(
+    pairs,
     scaled_ref,
+    lengths_ref,
+    rate_ref,
     far_tokens,
     far_slot,
     far_key,
     far_value,
-    after_ref,
     key_share_ref,
     value_share_ref,
     squares_ref,
+    turns_ref,
+    limits_ref,
     tokens_ref,
     slot_ref,
     key_ref,
@@ -97,6 +101,14 @@
     copies = fetch(
         ((far_tokens, tokens_ref), (far_slot, slot_ref), (far_key, key_ref), (far_value, value_ref)), sems
     )
+    own = (lax.axis_index("wide") * pairs) % lengths_ref.shape[0]
+    positions = jnp.concatenate(
+        [jnp.full((1, HEAD_SIZE), lengths_ref[own + i], jnp.int32) for i in range(pairs)], 0
+    )
+    angle = positions.astype(F32) * rate_ref[...]
+    turns_ref[0] = jnp.cos(angle)
+    turns_ref[1] = jnp.sin(angle)
+    limits_ref[...] = positions
     copies[0].wait()
     copies[1].wait()
     rows = tokens_ref.shape[0]
@@ -111,37 +123,27 @@
     value_share_ref[...] = jnp.dot(scaled_ref[...], value_ref[...], preferred_element_type=F32)
 
 
-def products(offsets, first, blocks_ref, weight_ref, total):
-    features = blocks_ref.shape[2]
+def products(offsets, pieces, weight_ref, total):
     place = lax.axis_index("wide")
-    for k, offset in enumerate(offsets):
-        start = pl.multiple_of((place ^ offset) * features, features)
-        total = total + jnp.dot(
-            blocks_ref[first + k], weight_ref[pl.ds(start, features), :], preferred_element_type=F32
-        )
+    for of_piece, blocks_ref in zip(offsets, pieces):
+        features = blocks_ref.shape[2]
+        for k, offset in enumerate(of_piece):
+            start = pl.multiple_of((place ^ offset) * features, features)
+            total = total + jnp.dot(
+                blocks_ref[k], weight_ref[pl.ds(start, features), :], preferred_element_type=F32
+            )
     return total
 
 
-def query_kernel(offsets, first, blocks_ref, weight_ref, total_ref, out_ref):
-    out_ref[...] = products(offsets, first, blocks_ref, weight_ref, total_ref[...])
-
-
-def query_turns_kernel(offsets, pairs, blocks_ref, weight_ref, lengths_ref, rate_ref, out_ref, turns_ref, limits_ref):
-    out_ref[...] = products(offsets, 0, blocks_ref, weight_ref, jnp.zeros(out_ref.shape, F32))
-    own = (lax.axis_index("wide") * pairs) % lengths_ref.shape[0]
-    positions = jnp.concatenate(
-        [jnp.full((1, HEAD_SIZE), lengths_ref[own + i], jnp.int32) for i in range(pairs)], 0
-    )
-    angle = positions.astype(F32) * rate_ref[...]
-    turns_ref[0] = jnp.cos(angle)
-    turns_ref[1] = jnp.sin(angle)
-    limits_ref[...] = positions
-
-
-def message_kernel(
-    offsets, pairs, blocks_ref, weight_ref, total_ref, key_ref, value_ref, squares_ref, message_ref
-):
-    query = products(offsets, 0, blocks_ref, weight_ref, total_ref[...])
+def query_kernel(offsets, weight_ref, *refs):
+    pieces, before, out_ref = refs[: len(offsets)], refs[len(offsets) : -1], refs[-1]
+    total = before[0][...] if before else jnp.zeros(out_ref.shape, F32)
+    out_ref[...] = products(offsets, pieces, weight_ref, total)
+
+
+def message_kernel(offsets, pairs, weight_ref, total_ref, key_ref, value_ref, squares_ref, *refs):
+    message_ref = refs[-1]
+    query = products(offsets, refs[:-1], weight_ref, total_ref[...])
     rows = query.shape[0]
     held = query.shape[1] // HEAD_SIZE
     for target in range(message_ref.shape[0]):
@@ -252,33 +254,30 @@
     out_ref[...] = wide_ref[...].astype(BF16)
 
 
-def project_half(pairs, head_offsets, slot_offsets, slot_ref, pieces, weight_ref, total):
+def project_half(pairs, places, slot_ref, pieces, weight_ref, total):
     rows = slot_ref.shape[1]
     held = pieces[0].shape[1]
     devices_of_head = rows // pairs
     place = lax.axis_index("wide")
-    group_place = place % devices_of_head
-    head_place = place // devices_of_head
     slot_of_row = jnp.transpose(jnp.broadcast_to(slot_ref[...], (rows, rows)))[:, 0:1]
     position = lax.broadcasted_iota(jnp.int32, (rows, held), 1)
-    picks = []
-    for offsets in slot_offsets:
-        device = jnp.zeros_like(position)
-        for k, offset in enumerate(offsets):
-            device = jnp.where(position // pairs == k, group_place ^ offset, device)
-        picks.append((slot_of_row == device * pairs + position % pairs).astype(BF16))
-    ordered = [
-        sum(
-            jnp.dot(pick, piece[z], preferred_element_type=F32) for pick, piece in zip(picks, pieces)
-        ).astype(BF16)
-        for z in range(len(head_offsets))
-    ]
+    ordered, heads = [], []
+    for z, by_piece in enumerate(places):
+        result = 0.0
+        for offsets, piece in zip(by_piece, pieces):
+            device = jnp.zeros_like(position)
+            for k, offset in enumerate(offsets):
+                device = jnp.where(position // pairs == k, (place ^ offset) % devices_of_head, device)
+            pick = (slot_of_row == device * pairs + position % pairs).astype(BF16)
+            result = result + jnp.dot(pick, piece[z], preferred_element_type=F32)
+        ordered.append(result.astype(BF16))
+        heads.append((place ^ by_piece[0][0]) // devices_of_head)
     for g in range(QUERY_GROUP):
         columns = slice(g * HEAD_SIZE, (g + 1) * HEAD_SIZE)
         weights = []
-        for offset in head_offsets:
-            start = (g * KEY_VALUE_HEADS + (head_place ^ offset)) * HEAD_SIZE
-            weights.append(weight_ref[pl.ds(pl.multiple_of(start, HEAD_SIZE), HEAD_SIZE), :])
+        for head in heads:
+            start = pl.multiple_of((g * KEY_VALUE_HEADS + head) * HEAD_SIZE, HEAD_SIZE)
+            weights.append(weight_ref[pl.ds(start, HEAD_SIZE), :])
         total = total + jnp.dot(
             jnp.concatenate([o[:, columns] for o in ordered], axis=1),
             jnp.concatenate(weights, axis=0),
@@ -287,24 +286,20 @@
     return total
 
 
-def first_half_kernel(pairs, head_offsets, slot_offsets, slot_ref, mine_ref, other_ref, weight_ref, out_ref):
+def first_half_kernel(pairs, places, slot_ref, weight_ref, *refs):
+    out_ref = refs[-1]
     out_ref[...] = project_half(
-        pairs,
-        head_offsets,
-        slot_offsets,
-        slot_ref,
-        (mine_ref, other_ref),
-        weight_ref,
-        jnp.zeros(out_ref.shape, F32),
-    )
-
-
-def second_half_kernel(
-    pairs, head_offsets, slot_offsets, slot_ref, mine_ref, other_ref, weight_ref, half_ref, out_ref
-):
-    out_ref[...] = project_half(
-        pairs, head_offsets, slot_offsets, slot_ref, (mine_ref, other_ref), weight_ref, half_ref[...]
-    ).astype(BF16)
+        pairs, places, slot_ref, refs[:-1], weight_ref, jnp.zeros(out_ref.shape, F32)
+    )
+
+
+def second_half_kernel(pairs, places, slot_ref, weight_ref, half_ref, *refs):
+    out_ref = refs[-1]
+    out_ref[...] = project_half(pairs, places, slot_ref, refs[:-1], weight_ref, half_ref[...]).astype(BF16)
+
+
+def passed(array, *after):
+    return call(pass_kernel, jax.ShapeDtypeStruct(array.shape, array.dtype), (array, *after))
 
 
 def swap(array, bit, count):
@@ -351,43 +346,36 @@
     totals = jax.ShapeDtypeStruct((rows, query_columns), F32)
     shares = jax.ShapeDtypeStruct((rows, key_projection.shape[1]), F32)
 
-    def query(offsets, first, array, total):
+    def query(by_piece, *total):
+        blocks = sum(piece.shape[0] for piece in by_piece.values())
         return call(
-            functools.partial(query_kernel, tuple(offsets), first),
+            functools.partial(query_kernel, tuple(tuple(o ^ by for o in offsets) for by in by_piece)),
             totals,
-            (array, w_query, total),
-            near=(0, 1),
-            flops=2 * rows * len(offsets) * features * query_columns,
-            read=2 * len(offsets) * features * query_columns,
+            (w_query, *by_piece.values(), *total),
+            near=range(1 + len(by_piece)),
+            flops=2 * rows * blocks * features * query_columns,
+            read=2 * blocks * features * query_columns,
         )
 
-    core, half = bits[-1], count // 2
-    blocks, offsets, new, after = scaled[None], [0], [0], None
-    for far in bits[:-1]:
-        arrived = swap(blocks, far, count)
-        if len(offsets) == 2:
-            after, turns, limits = call(
-                functools.partial(query_turns_kernel, tuple(offsets), pairs),
+    *outer, far, near, core = bits
+    corners = (far | near | core, near | core, far | core)
+    blocks, offsets, key_share = scaled[None], [0], None
+    for bit in outer:
+        arrived = swap(blocks, bit | core, count)
+        if key_share is None:
+            key_share, value_share, squares, turns, limits = call(
+                functools.partial(share_kernel, pairs),
                 (
-                    totals,
+                    shares,
+                    shares,
+                    jax.ShapeDtypeStruct((rows, HEAD_SIZE), F32),
                     jax.ShapeDtypeStruct((2, pairs, HEAD_SIZE), F32),
                     jax.ShapeDtypeStruct((pairs, HEAD_SIZE), jnp.int32),
                 ),
-                (blocks, w_query, lengths, jnp.asarray(rate)),
-                near=(0, 1),
-                smem=(2,),
-                flops=2 * rows * len(offsets) * features * query_columns,
-                read=2 * len(offsets) * features * query_columns,
-            )
-        elif len(offsets) > 2:
-            after = query(new, len(offsets) - len(new), blocks, after)
-        if len(offsets) == 4:
-            key_share, value_share, squares = call(
-                share_kernel,
-                (shares, shares, jax.ShapeDtypeStruct((rows, HEAD_SIZE), F32)),
-                (scaled, tokens, slot_row, key_projection, value_projection, after),
+                (scaled, lengths, jnp.asarray(rate), tokens, slot_row, key_projection, value_projection),
                 near=(0,),
-                far=(1, 2, 3, 4),
+                far=(3, 4, 5, 6),
+                smem=(1,),
                 scratch=(
                     pltpu.VMEM((rows, features), BF16),
                     pltpu.VMEM((1, rows), jnp.int32),
@@ -398,30 +386,27 @@
                 flops=4 * rows * key_projection.size,
                 read=4 * key_projection.size,
             )
-        new = [o ^ far for o in offsets]
-        if 2 * len(offsets) == half:
-            break
         blocks = call(
             join_kernel,
             jax.ShapeDtypeStruct((2 * len(offsets), rows, features), BF16),
-            (blocks, arrived) if after is None else (blocks, arrived, key_share if len(offsets) == 4 else after),
+            (blocks, arrived, key_share),
         )
-        offsets = offsets + new
-    blocks = call(
-        pass_kernel, jax.ShapeDtypeStruct(blocks.shape, BF16), (blocks, arrived, after, key_share)
-    )
-    first = swap(blocks, core, count)
-    last = swap(arrived, core, count)
-    total = query(new, 0, arrived, after)
-    total = query([o ^ core for o in offsets], 0, first, total)
+        offsets = offsets + [o ^ bit ^ core for o in offsets]
+    pieces = {by: swap(blocks, by, count) for by in corners}
+    total = query({0: blocks, core: swap(blocks, core, count)})
+    pieces = {by: passed(piece, total) for by, piece in pieces.items()}
+    last = {by ^ core: swap(piece, core, count) for by, piece in pieces.items()}
+    total = query(pieces, total)
     sent = held // KEY_VALUE_HEADS if held % KEY_VALUE_HEADS == 0 else held
     message = call(
-        functools.partial(message_kernel, tuple(o ^ core for o in new), pairs),
+        functools.partial(
+            message_kernel, tuple(tuple(o ^ by for o in offsets) for by in last), pairs
+        ),
         jax.ShapeDtypeStruct((count, pairs * (sent + 3), HEAD_SIZE), F32),
-        (last, w_query, total, key_share, value_share, squares),
-        near=(0, 1),
-        flops=2 * last.size * query_columns,
-        read=2 * len(new) * features * query_columns,
+        (w_query, total, key_share, value_share, squares, *last.values()),
+        near=(0, *range(5, 5 + len(last))),
+        flops=6 * blocks.size * query_columns,
+        read=6 * len(offsets) * features * query_columns,
     )
 
     got = lax.all_to_all(message, "wide", 0, 0, tiled=True)
@@ -454,32 +439,38 @@
     )
 
     mine = attended[None]
-    slot_offsets = [0]
-    for far in bits:
-        if core < far < devices_of_head:
-            mine = jnp.concatenate([mine, swap(mine, far, count)], 1)
-            slot_offsets = slot_offsets + [o ^ far for o in slot_offsets]
-    high, low = bits[0] // devices_of_head, bits[1] // devices_of_head
-    mine = jnp.concatenate([mine, swap(mine, bits[0], count)], 0)
-    across = swap(mine, bits[1], count)
-    beside = swap(mine, core, count)
-    slots = (tuple(slot_offsets), tuple(o ^ core for o in slot_offsets))
+    offsets = [0]
+    for bit in bits:
+        if near < bit < devices_of_head:
+            mine = jnp.concatenate([mine, swap(mine, bit | core, count)], 1)
+            offsets = offsets + [o ^ bit ^ core for o in offsets]
+    high, low = bits[0] | core, bits[1]
+    mine = jnp.concatenate([mine, swap(mine, high, count)], 0)
+    corners = (near | core, low | near | core, low | core)
+    pieces = {0: mine} | {by: swap(mine, by, count) for by in corners}
+
+    def with_core(*members):
+        both = [(by, pieces[by]) for by in members]
+        both += [(by ^ core, swap(pieces[by], core, count)) for by in members]
+        places = tuple(
+            tuple(tuple(o ^ head ^ by for o in offsets) for by, _ in both) for head in (0, high)
+        )
+        return places, [piece for _, piece in both]
+
     columns = output_projection.shape[1]
+    places, held_pieces = with_core(0, corners[0])
     half = call(
-        functools.partial(first_half_kernel, pairs, (0, high), slots),
+        functools.partial(first_half_kernel, pairs, places),
         jax.ShapeDtypeStruct((rows, columns), F32),
-        (slot_row, mine, beside, output_projection),
-        near=(3,),
-        flops=rows * output_projection.size,
-        read=output_projection.size,
-    )
-    across = call(pass_kernel, jax.ShapeDtypeStruct(across.shape, BF16), (across, half))
-    both = swap(across, core, count)
+        (slot_row, output_projection, *held_pieces),
+        near=(1,),
+    )
+    places, held_pieces = with_core(*corners[1:])
     return call(
-        functools.partial(second_half_kernel, pairs, (low, low ^ high), slots),
+        functools.partial(second_half_kernel, pairs, places),
         jax.ShapeDtypeStruct((rows, columns), BF16),
-        (slot_row, across, both, output_projection, half),
-        near=(3,),
+        (slot_row, output_projection, half, *held_pieces),
+        near=(1,),
         flops=rows * output_projection.size,
         read=output_projection.size,
     )

time: 52.8 us -> 45.8 us (0.87)
  waiting for transfers between devices: 17.5 us -> 8.16 us
  starting transfers between devices: 8.73 us -> 12.4 us
  blocking collectives: 14.2 us -> 12.9 us
    ppermute x10 -> x16, waiting for transfers between devices: 17.5 us -> 8.16 us  [swap(): return lax.ppermute(array, 'wide', [(i, i ^ bit) for i in range(count)])]
    ppermute x10 -> x16, starting transfers between devices: 8.73 us -> 12.4 us  [swap(): return lax.ppermute(array, 'wide', [(i, i ^ bit) for i in range(count)])]
    all_to_all x1, blocking collectives: 14.2 us -> 12.9 us  [body(): got = lax.all_to_all(message, 'wide', 0, 0, tiled=True)]
    pallas_call x14 -> x12, Pallas kernels: 12 us -> 12 us  [call(): pl.pallas_call(kernel, out_shape=out_shape, in_specs=specs, out_specs=jax...]
  transfers between devices with their start and end apart: 10 -> 16, of which waited for: 9 -> 5; matrix products, arithmetic and copies ran while one was open for 0% -> 0% of each run, Pallas kernels for 11% -> 12%
where the time goes in v6:
time: 45.8 us; the launch traced here: 45.7 us
  blocking collectives  12.9 us (28%)
  starting transfers between devices  12.4 us (27%)
  Pallas kernels  12 us (26%)
  waiting for transfers between devices  8.16 us (18%)
    all_to_all x1, blocking collectives, body(): got = lax.all_to_all(message, 'wide', 0, 0, tiled=True)  12.9 us
    ppermute x16, starting transfers between devices, swap(): return lax.ppermute(array, 'wide', [(i, i ^ bit) for i in range(count)])  12.4 us
    pallas_call x12, Pallas kernels, call(): pl.pallas_call(kernel, out_shape=out_shape, in_specs=specs, out_specs=jax...  12 us
    ppermute x16, waiting for transfers between devices, swap(): return lax.ppermute(array, 'wide', [(i, i ^ bit) for i in range(count)])  8.16 us
  transfers between devices with their start and end apart: 16, of which 5 were waited for; matrix products, arithmetic and copies ran while one was open for 0% of the time, Pallas kernels for 12%

profile of v6, /device:TPU:0, one launch (start us, length us, event | category | flops | bytes accessed | tf_op | source)
XLA Modules:
  0.0 45.7 jit_solution(6436343477146085583)
XLA Ops:
  0.0 1.1 %shard_map.109.scaled_ref = bf16[16,1024]{1,0:T(8,128)(2,1)S(1)} custom-call(bf16[16,1024]{1,0:T(8,128)(2,1)} %far_tokens.3, bf16[1024]{0:T(1024)(128)(2,1)} %far_gain.1, s32[1,16]{1,0:T(1,128)} %bitcast.9, bf16[16384,512]{1,0:T(8,128)(2,1)} %weight_ref.7), custom_call_target="tpu_custom_call" | custom-call | bytes 67108864 | tf_op jit(solution)/shard_map/pallas_call | solution.py:35
  1.1 3.5 %collective-permute-start = (bf16[1,16,1024]{2,1,0:T(8,128)(2,1)S(1)}, bf16[1,16,1024]{2,1,0:T(8,128)(2,1)S(1)}, u32[]{:S(2)}, u32[]{:S(2)}) collective-permute-start(bf16[1,16,1024]{2,1,0:T(8,128)(2,1)S(1)} %bitcast.5), channel_id=1, source_target_pairs={{0,9},{1,8},{2,11},{3,10},{4,13},{5,12},{6,15},{7,14},{8,1},{9,0},... | collective-permute-start | bytes 98312 | tf_op jit(solution)/shard_map/ppermute | solution.py:306
  4.6 0.0 copy-done.5
  4.6 0.0 copy-done.4
  4.6 2.4 %shard_map.110 = (f32[16,512]{1,0:T(8,128)S(1)}, f32[16,512]{1,0:T(8,128)S(1)}, f32[16,128]{1,0:T(8,128)S(1)}, f32[2,4,128]{2,1,0:T(4,128)S(1)}, s32[4,128]{1,0:T(4,128)S(1)}) custom-call(bf16[16,1024]{1,0:T(8,128)(2,1)S(1)} %shard_map.109.scaled_ref, s32[16]{0:T(128)S(1)} %copy-done.4, f32[1,128]{1,0:T(1,128)S(1)} %copy-done.5, ...), custom_call_target="tpu_custom_call" | custom-call | flops 33554432 | bytes 2097152 | tf_op jit(solution)/shard_map/pallas_call | solution.py:35
  7.1 0.0 collective-permute-done.arrived_ref
  7.1 0.7 %collective-permute-start.2 = (bf16[2,16,1024]{2,1,0:T(8,128)(2,1)S(1)}, bf16[2,16,1024]{2,1,0:T(8,128)(2,1)S(1)}, u32[]{:S(2)}, u32[]{:S(2)}) collective-permute-start(bf16[2,16,1024]{2,1,0:T(8,128)(2,1)S(1)} %shard_map.111.refs_0_), channel_id=1, source_target_pairs={{0,1},{1,0},{2,3},{3,2},{4,5},{5,4},{6,7},{7,6},{8,9},{9,8},{10,11... | collective-permute-start | bytes 196616 | tf_op jit(solution)/shard_map/ppermute | solution.py:306
  7.8 2.7 %collective-permute-start.1 = (bf16[2,16,1024]{2,1,0:T(8,128)(2,1)S(1)}, bf16[2,16,1024]{2,1,0:T(8,128)(2,1)S(1)}, u32[]{:S(2)}, u32[]{:S(2)}) collective-permute-start(bf16[2,16,1024]{2,1,0:T(8,128)(2,1)S(1)} %shard_map.111.refs_0_), channel_id=1, source_target_pairs={{0,7},{1,6},{2,5},{3,4},{4,3},{5,2},{6,1},{7,0},{8,15},{9,14},{10,... | collective-permute-start | bytes 196616 | tf_op jit(solution)/shard_map/ppermute | solution.py:306
  10.5 0.3 collective-permute-start.3
  10.8 0.1 collective-permute-start.4
  10.9 0.0 collective-permute-done.2.refs_1_
  10.9 0.0 copy-done
  10.9 0.6 %shard_map.112.refs_0_.refs_3_ = f32[16,512]{1,0:T(8,128)S(1)} custom-call(bf16[16384,512]{1,0:T(8,128)(2,1)S(1)} %copy-done, bf16[2,16,1024]{2,1,0:T(8,128)(2,1)S(1)} %shard_map.111.refs_0_, bf16[2,16,1024]{2,1,0:T(8,128)(2,1)S(1)} %collective-permute-done.2.refs_1_), custom_call_target="tpu_custom_call" | custom-call | flops 67108864 | bytes 4194304 | tf_op jit(solution)/shard_map/pallas_call | solution.py:35
  11.6 1.4 %collective-permute-done.1.array_ref = bf16[2,16,1024]{2,1,0:T(8,128)(2,1)S(1)} collective-permute-done((bf16[2,16,1024]{2,1,0:T(8,128)(2,1)S(1)}, bf16[2,16,1024]{2,1,0:T(8,128)(2,1)S(1)}, u32[]{:S(2)}, u32[]{:S(2)}) %collective-permute-start.1) | collective-permute-done | bytes 65568 | tf_op jit(solution)/shard_map/ppermute | solution.py:306
  13.0 0.0 collective-permute-start.5
  13.0 1.6 %collective-permute-done.3.array_ref = bf16[2,16,1024]{2,1,0:T(8,128)(2,1)S(1)} collective-permute-done((bf16[2,16,1024]{2,1,0:T(8,128)(2,1)S(1)}, bf16[2,16,1024]{2,1,0:T(8,128)(2,1)S(1)}, u32[]{:S(2)}, u32[]{:S(2)}) %collective-permute-start.3) | collective-permute-done | bytes 65568 | tf_op jit(solution)/shard_map/ppermute | solution.py:306
  14.7 0.3 collective-permute-start.6
  14.9 0.0 collective-permute-done.4.array_ref
  15.0 0.0 copy-start.1
  15.0 0.0 copy-start.2
  15.0 0.3 collective-permute-start.7
  15.3 0.9 %shard_map.116.total_ref = f32[16,512]{1,0:T(8,128)S(1)} custom-call(bf16[16384,512]{1,0:T(8,128)(2,1)S(1)} %copy-done, bf16[2,16,1024]{2,1,0:T(8,128)(2,1)S(1)} %shard_map.113.refs_0_, bf16[2,16,1024]{2,1,0:T(8,128)(2,1)S(1)} %shard_map.114.refs_1_, bf16[2,16,1024]{2,1,0:T(8,128)(2,1)S(1)} %shard_map.115.refs_2_, f32[16,512]{1,0:T(8,128)S(1)} %shard_map.112.refs_0_.refs_3_), custom_call_target="tpu_custom_call" | custom-call | flops 100663296 | bytes 6291456 | tf_op jit(solution)/shard_map/pallas_call | solution.py:35
  16.2 0.0 collective-permute-done.5.refs_0_
  16.2 0.0 collective-permute-done.6.refs_1_
  16.2 0.1 collective-permute-done.7.refs_2_
  16.3 0.9 %shard_map.117 = f32[16,16,128]{2,1,0:T(8,128)S(1)} custom-call(bf16[16384,512]{1,0:T(8,128)(2,1)S(1)} %copy-done, f32[16,512]{1,0:T(8,128)S(1)} %shard_map.116.total_ref, f32[16,512]{1,0:T(8,128)S(1)} %get-tuple-element.12.refs_0_.key_ref, f32[16,512]{1,0:T(8,128)S(1)} %get-tuple-element.13.value_ref, f32[16,128]{1,0:T(8,128)S(1)} %get-tuple-element.14.squares_ref, ...), custom_call_target="tpu_custom_call" | custom-call | flops 100663296 | bytes 6291456 | tf_op jit(solution)/shard_map/pallas_call | solution.py:35
  17.2 12.9 %all_to_all.5.query_ref.rest_ref = f32[16,16,128]{2,1,0:T(8,128)S(1)} all-to-all(f32[16,16,128]{2,1,0:T(8,128)S(1)} %shard_map.117), channel_id=1, replica_groups=mesh['groups'=2,'wide'=16] {'wide'}, dimensions={0} | all-to-all | bytes 262144 | tf_op jit(solution)/shard_map/all_to_all | solution.py:412
  30.1 0.0 copy-done.1
  30.1 0.0 copy-done.2
  30.1 2.3 %shard_map.118 = bf16[4,2048]{1,0:T(4,128)(2,1)S(1)} custom-call(s32[4,128]{1,0:T(4,128)S(1)} %get-tuple-element.10.limits_ref, f32[2,4,128]{2,1,0:T(4,128)S(1)} %get-tuple-element.11.turns_ref, f32[16,16,128]{2,1,0:T(8,128)S(1)} %all_to_all.5.query_ref.rest_ref, f32[16,16,128]{2,1,0:T(8,128)S(1)} %all_to_all.5.query_ref.rest_ref, ...), custom_call_target="tpu_custom_call" | custom-call | flops 134217728 | bytes 8388608 | tf_op jit(solution)/shard_map/pallas_call | solution.py:35
  32.4 0.1 collective-permute-start.8
  32.5 4.0 %collective-permute-done.8 = bf16[1,4,2048]{2,1,0:T(4,128)(2,1)S(1)} collective-permute-done((bf16[1,4,2048]{2,1,0:T(4,128)(2,1)S(1)}, bf16[1,4,2048]{2,1,0:T(4,128)(2,1)S(1)}, u32[]{:S(2)}, u32[]{:S(2)}) %collective-permute-start.8) | collective-permute-done | bytes 16416 | tf_op jit(solution)/shard_map/ppermute | solution.py:306
  36.5 0.1 collective-permute-start.9
  36.6 0.6 %collective-permute-start.12 = (bf16[2,4,2048]{2,1,0:T(4,128)(2,1)S(1)}, bf16[2,4,2048]{2,1,0:T(4,128)(2,1)S(1)}, u32[]{:S(2)}, u32[]{:S(2)}) collective-permute-start(bf16[2,4,2048]{2,1,0:T(4,128)(2,1)S(1)} %pad_maximum_fusion.refs_0_), channel_id=1, source_target_pairs={{0,7},{1,6},{2,5},{3,4},{4,3},{5,2},{6,1},{7,0},{8,15},{9,14},{10,... | collective-permute-start | bytes 98312 | tf_op jit(solution)/shard_map/ppermute | solution.py:306
  37.2 1.6 %collective-permute-start.13 = (bf16[2,4,2048]{2,1,0:T(4,128)(2,1)S(1)}, bf16[2,4,2048]{2,1,0:T(4,128)(2,1)S(1)}, u32[]{:S(2)}, u32[]{:S(2)}) collective-permute-start(bf16[2,4,2048]{2,1,0:T(4,128)(2,1)S(1)} %pad_maximum_fusion.refs_0_), channel_id=1, source_target_pairs={{0,5},{1,4},{2,7},{3,6},{4,1},{5,0},{6,3},{7,2},{8,13},{9,12},{10,... | collective-permute-start | bytes 98312 | tf_op jit(solution)/shard_map/ppermute | solution.py:306
  38.8 1.2 %collective-permute-start.10 = (bf16[2,4,2048]{2,1,0:T(4,128)(2,1)S(1)}, bf16[2,4,2048]{2,1,0:T(4,128)(2,1)S(1)}, u32[]{:S(2)}, u32[]{:S(2)}) collective-permute-start(bf16[2,4,2048]{2,1,0:T(4,128)(2,1)S(1)} %pad_maximum_fusion.refs_0_), channel_id=1, source_target_pairs={{0,1},{1,0},{2,3},{3,2},{4,5},{5,4},{6,7},{7,6},{8,9},{9,8},{10,11... | collective-permute-start | bytes 98312 | tf_op jit(solution)/shard_map/ppermute | solution.py:306
  39.9 0.0 collective-permute-done.9.refs_1_
  39.9 0.0 collective-permute-start.11
  39.9 1.0 %collective-permute-done.12.refs_0_ = bf16[2,4,2048]{2,1,0:T(4,128)(2,1)S(1)} collective-permute-done((bf16[2,4,2048]{2,1,0:T(4,128)(2,1)S(1)}, bf16[2,4,2048]{2,1,0:T(4,128)(2,1)S(1)}, u32[]{:S(2)}, u32[]{:S(2)}) %collective-permute-start.12) | collective-permute-done | bytes 32800 | tf_op jit(solution)/shard_map/ppermute | solution.py:306
  40.9 0.0 collective-permute-start.14
  40.9 0.0 collective-permute-done.13.refs_1_
  40.9 0.9 %collective-permute-start.15 = (bf16[2,4,2048]{2,1,0:T(4,128)(2,1)S(1)}, bf16[2,4,2048]{2,1,0:T(4,128)(2,1)S(1)}, u32[]{:S(2)}, u32[]{:S(2)}) collective-permute-start(bf16[2,4,2048]{2,1,0:T(4,128)(2,1)S(1)} %collective-permute-done.13.refs_1_), channel_id=1, source_target_pairs={{0,1},{1,0},{2,3},{3,2},{4,5},{5,4},{6,7},{7,6},{8,9},{9,8},{10,11... | collective-permute-start | bytes 98312 | tf_op jit(solution)/shard_map/ppermute | solution.py:306
  41.9 0.0 collective-permute-done.10.refs_2_
  41.9 0.0 collective-permute-done.11.refs_3_
  41.9 1.6 %shard_map.119.half_ref = f32[16,1024]{1,0:T(8,128)S(1)} custom-call(s32[1,16]{1,0:T(1,128)S(1)} %bitcast.11, bf16[8192,1024]{1,0:T(8,128)(2,1)S(1)} %bitcast.4, bf16[2,4,2048]{2,1,0:T(4,128)(2,1)S(1)} %pad_maximum_fusion.refs_0_, bf16[2,4,2048]{2,1,0:T(4,128)(2,1)S(1)} %collective-permute-done.9.refs_1_, ...), custom_call_target="tpu_custom_call" | custom-call | tf_op jit(solution)/shard_map/pallas_call | solution.py:35
  43.5 0.0 collective-permute-done.14.refs_2_
  43.5 0.0 collective-permute-done.15.refs_3_
  43.5 2.2 %shard_map.120 = bf16[16,1024]{1,0:T(8,128)(2,1)} custom-call(s32[1,16]{1,0:T(1,128)S(1)} %bitcast.12, bf16[8192,1024]{1,0:T(8,128)(2,1)S(1)} %bitcast.4, f32[16,1024]{1,0:T(8,128)S(1)} %shard_map.119.half_ref, bf16[2,4,2048]{2,1,0:T(4,128)(2,1)S(1)} %collective-permute-done.12.refs_0_, bf16[2,4,2048]{2,1,0:T(4,128)(2,1)S(1)} %collective-permute-done.13.refs_1_, ...), custom_call_target="tpu_custom_call" | custom-call | flops 134217728 | bytes 8388608 | tf_op jit(solution)/shard_map/pallas_call | solution.py:35
  (19 shorter events, 0.1 us)
Async XLA Ops:
  0.0 4.6 %copy-start.5 = (f32[1,128]{1,0:T(1,128)S(1)}, f32[1,128]{1,0:T(1,128)}, u32[]{:S(2)}) copy-start(f32[1,128]{1,0:T(1,128)} %constant.2.clone.rate_ref) | copy-start | bytes 1540
  0.0 10.9 %copy-start = (bf16[16384,512]{1,0:T(8,128)(2,1)S(1)}, bf16[16384,512]{1,0:T(8,128)(2,1)}, u32[]{:S(2)}) copy-start(bf16[16384,512]{1,0:T(8,128)(2,1)} %weight_ref.7) | copy-start | bytes 50331652
  0.0 4.6 %copy-start.4 = (s32[16]{0:T(128)S(1)}, s32[16]{0:T(128)}, u32[]{:S(2)}) copy-start(s32[16]{0:T(128)} %lengths_ref.1) | copy-start | bytes 196
  1.1 6.0 %collective-permute-start = (bf16[1,16,1024]{2,1,0:T(8,128)(2,1)S(1)}, bf16[1,16,1024]{2,1,0:T(8,128)(2,1)S(1)}, u32[]{:S(2)}, u32[]{:S(2)}) collective-permute-start(bf16[1,16,1024]{2,1,0:T(8,128)(2,1)S(1)} %bitcast.5), channel_id=1, source_target_pairs={{0,9},{1,8},{2,11},{3,10},{4,13},{5,12},{6,15},{7,14},{8,1},{9,0},... | collective-permute-start | bytes 98312 | tf_op jit(solution)/shard_map/ppermute | solution.py:306
  7.1 3.8 %collective-permute-start.2 = (bf16[2,16,1024]{2,1,0:T(8,128)(2,1)S(1)}, bf16[2,16,1024]{2,1,0:T(8,128)(2,1)S(1)}, u32[]{:S(2)}, u32[]{:S(2)}) collective-permute-start(bf16[2,16,1024]{2,1,0:T(8,128)(2,1)S(1)} %shard_map.111.refs_0_), channel_id=1, source_target_pairs={{0,1},{1,0},{2,3},{3,2},{4,5},{5,4},{6,7},{7,6},{8,9},{9,8},{10,11... | collective-permute-start | bytes 196616 | tf_op jit(solution)/shard_map/ppermute | solution.py:306
  7.8 5.2 %collective-permute-start.1 = (bf16[2,16,1024]{2,1,0:T(8,128)(2,1)S(1)}, bf16[2,16,1024]{2,1,0:T(8,128)(2,1)S(1)}, u32[]{:S(2)}, u32[]{:S(2)}) collective-permute-start(bf16[2,16,1024]{2,1,0:T(8,128)(2,1)S(1)} %shard_map.111.refs_0_), channel_id=1, source_target_pairs={{0,7},{1,6},{2,5},{3,4},{4,3},{5,2},{6,1},{7,0},{8,15},{9,14},{10,... | collective-permute-start | bytes 196616 | tf_op jit(solution)/shard_map/ppermute | solution.py:306
  10.5 4.1 %collective-permute-start.3 = (bf16[2,16,1024]{2,1,0:T(8,128)(2,1)S(1)}, bf16[2,16,1024]{2,1,0:T(8,128)(2,1)S(1)}, u32[]{:S(2)}, u32[]{:S(2)}) collective-permute-start(bf16[2,16,1024]{2,1,0:T(8,128)(2,1)S(1)} %shard_map.111.refs_0_), channel_id=1, source_target_pairs={{0,3},{1,2},{2,1},{3,0},{4,7},{5,6},{6,5},{7,4},{8,11},{9,10},{10,... | collective-permute-start | bytes 196616 | tf_op jit(solution)/shard_map/ppermute | solution.py:306
  10.8 4.1 %collective-permute-start.4 = (bf16[2,16,1024]{2,1,0:T(8,128)(2,1)S(1)}, bf16[2,16,1024]{2,1,0:T(8,128)(2,1)S(1)}, u32[]{:S(2)}, u32[]{:S(2)}) collective-permute-start(bf16[2,16,1024]{2,1,0:T(8,128)(2,1)S(1)} %shard_map.111.refs_0_), channel_id=1, source_target_pairs={{0,5},{1,4},{2,7},{3,6},{4,1},{5,0},{6,3},{7,2},{8,13},{9,12},{10,... | collective-permute-start | bytes 196616 | tf_op jit(solution)/shard_map/ppermute | solution.py:306
  13.0 3.2 %collective-permute-start.5 = (bf16[2,16,1024]{2,1,0:T(8,128)(2,1)S(1)}, bf16[2,16,1024]{2,1,0:T(8,128)(2,1)S(1)}, u32[]{:S(2)}, u32[]{:S(2)}) collective-permute-start(bf16[2,16,1024]{2,1,0:T(8,128)(2,1)S(1)} %shard_map.113.refs_0_), channel_id=1, source_target_pairs={{0,1},{1,0},{2,3},{3,2},{4,5},{5,4},{6,7},{7,6},{8,9},{9,8},{10,11... | collective-permute-start | bytes 196616 | tf_op jit(solution)/shard_map/ppermute | solution.py:306
  14.7 1.5 %collective-permute-start.6 = (bf16[2,16,1024]{2,1,0:T(8,128)(2,1)S(1)}, bf16[2,16,1024]{2,1,0:T(8,128)(2,1)S(1)}, u32[]{:S(2)}, u32[]{:S(2)}) collective-permute-start(bf16[2,16,1024]{2,1,0:T(8,128)(2,1)S(1)} %shard_map.114.refs_1_), channel_id=1, source_target_pairs={{0,1},{1,0},{2,3},{3,2},{4,5},{5,4},{6,7},{7,6},{8,9},{9,8},{10,11... | collective-permute-start | bytes 196616 | tf_op jit(solution)/shard_map/ppermute | solution.py:306
  15.0 15.2 %copy-start.1 = (bf16[4,4096,128]{2,1,0:T(8,128)(2,1)S(1)}, bf16[4,4096,128]{2,1,0:T(8,128)(2,1)}, u32[]{:S(2)}) copy-start(bf16[4,4096,128]{2,1,0:T(8,128)(2,1)} %keys_ref.1) | copy-start | bytes 12582916
  15.0 15.1 %copy-start.2 = (bf16[4,4096,128]{2,1,0:T(8,128)(2,1)S(1)}, bf16[4,4096,128]{2,1,0:T(8,128)(2,1)}, u32[]{:S(2)}) copy-start(bf16[4,4096,128]{2,1,0:T(8,128)(2,1)} %values_ref.1) | copy-start | bytes 12582916
  15.0 1.3 %collective-permute-start.7 = (bf16[2,16,1024]{2,1,0:T(8,128)(2,1)S(1)}, bf16[2,16,1024]{2,1,0:T(8,128)(2,1)S(1)}, u32[]{:S(2)}, u32[]{:S(2)}) collective-permute-start(bf16[2,16,1024]{2,1,0:T(8,128)(2,1)S(1)} %shard_map.115.refs_2_), channel_id=1, source_target_pairs={{0,1},{1,0},{2,3},{3,2},{4,5},{5,4},{6,7},{7,6},{8,9},{9,8},{10,11... | collective-permute-start | bytes 196616 | tf_op jit(solution)/shard_map/ppermute | solution.py:306
  15.3 26.6 %slice-start = ((s8[16777216]{0:T(1024)(128)(4,1)}), s8[4194304]{0:T(1024)(128)(4,1)S(1)}, s32[]{:S(2)}) async-start(s8[16777216]{0:T(1024)(128)(4,1)} %bitcast.3), calls=%async_computation.1 | async-start | bytes 8388608
  15.3 26.6 %slice-start.1 = ((s8[16777216]{0:T(1024)(128)(4,1)}), s8[4194304]{0:T(1024)(128)(4,1)S(1)}, s32[]{:S(2)}) async-start(s8[16777216]{0:T(1024)(128)(4,1)} %bitcast.3), calls=%async_computation.2 | async-start | bytes 8388608
  16.2 25.7 %copy-start.3 = (s32[16]{0:T(128)S(1)}, s32[16]{0:T(128)}, u32[]{:S(2)}) copy-start(s32[16]{0:T(128)} %param.13) | copy-start | bytes 196
  16.3 25.6 %slice-start.2 = ((s8[16777216]{0:T(1024)(128)(4,1)}), s8[4194304]{0:T(1024)(128)(4,1)S(1)}, s32[]{:S(2)}) async-start(s8[16777216]{0:T(1024)(128)(4,1)} %bitcast.3), calls=%async_computation.3 | async-start | bytes 8388608
  16.3 25.6 %slice-start.3 = ((s8[16777216]{0:T(1024)(128)(4,1)}), s8[4194304]{0:T(1024)(128)(4,1)S(1)}, s32[]{:S(2)}) async-start(s8[16777216]{0:T(1024)(128)(4,1)} %bitcast.3), calls=%async_computation.4 | async-start | bytes 8388608
  32.4 4.1 %collective-permute-start.8 = (bf16[1,4,2048]{2,1,0:T(4,128)(2,1)S(1)}, bf16[1,4,2048]{2,1,0:T(4,128)(2,1)S(1)}, u32[]{:S(2)}, u32[]{:S(2)}) collective-permute-start(bf16[1,4,2048]{2,1,0:T(4,128)(2,1)S(1)} %bitcast.7), channel_id=1, source_target_pairs={{0,9},{1,8},{2,11},{3,10},{4,13},{5,12},{6,15},{7,14},{8,1},{9,0},... | collective-permute-start | bytes 49160 | tf_op jit(solution)/shard_map/ppermute | solution.py:306
  36.5 3.4 %collective-permute-start.9 = (bf16[2,4,2048]{2,1,0:T(4,128)(2,1)S(1)}, bf16[2,4,2048]{2,1,0:T(4,128)(2,1)S(1)}, u32[]{:S(2)}, u32[]{:S(2)}) collective-permute-start(bf16[2,4,2048]{2,1,0:T(4,128)(2,1)S(1)} %pad_maximum_fusion.refs_0_), channel_id=1, source_target_pairs={{0,3},{1,2},{2,1},{3,0},{4,7},{5,6},{6,5},{7,4},{8,11},{9,10},{10,... | collective-permute-start | bytes 98312 | tf_op jit(solution)/shard_map/ppermute | solution.py:306
  36.6 4.3 %collective-permute-start.12 = (bf16[2,4,2048]{2,1,0:T(4,128)(2,1)S(1)}, bf16[2,4,2048]{2,1,0:T(4,128)(2,1)S(1)}, u32[]{:S(2)}, u32[]{:S(2)}) collective-permute-start(bf16[2,4,2048]{2,1,0:T(4,128)(2,1)S(1)} %pad_maximum_fusion.refs_0_), channel_id=1, source_target_pairs={{0,7},{1,6},{2,5},{3,4},{4,3},{5,2},{6,1},{7,0},{8,15},{9,14},{10,... | collective-permute-start | bytes 98312 | tf_op jit(solution)/shard_map/ppermute | solution.py:306
  37.2 3.8 %collective-permute-start.13 = (bf16[2,4,2048]{2,1,0:T(4,128)(2,1)S(1)}, bf16[2,4,2048]{2,1,0:T(4,128)(2,1)S(1)}, u32[]{:S(2)}, u32[]{:S(2)}) collective-permute-start(bf16[2,4,2048]{2,1,0:T(4,128)(2,1)S(1)} %pad_maximum_fusion.refs_0_), channel_id=1, source_target_pairs={{0,5},{1,4},{2,7},{3,6},{4,1},{5,0},{6,3},{7,2},{8,13},{9,12},{10,... | collective-permute-start | bytes 98312 | tf_op jit(solution)/shard_map/ppermute | solution.py:306
  38.8 3.1 %collective-permute-start.10 = (bf16[2,4,2048]{2,1,0:T(4,128)(2,1)S(1)}, bf16[2,4,2048]{2,1,0:T(4,128)(2,1)S(1)}, u32[]{:S(2)}, u32[]{:S(2)}) collective-permute-start(bf16[2,4,2048]{2,1,0:T(4,128)(2,1)S(1)} %pad_maximum_fusion.refs_0_), channel_id=1, source_target_pairs={{0,1},{1,0},{2,3},{3,2},{4,5},{5,4},{6,7},{7,6},{8,9},{9,8},{10,11... | collective-permute-start | bytes 98312 | tf_op jit(solution)/shard_map/ppermute | solution.py:306
  39.9 1.9 %collective-permute-start.11 = (bf16[2,4,2048]{2,1,0:T(4,128)(2,1)S(1)}, bf16[2,4,2048]{2,1,0:T(4,128)(2,1)S(1)}, u32[]{:S(2)}, u32[]{:S(2)}) collective-permute-start(bf16[2,4,2048]{2,1,0:T(4,128)(2,1)S(1)} %collective-permute-done.9.refs_1_), channel_id=1, source_target_pairs={{0,1},{1,0},{2,3},{3,2},{4,5},{5,4},{6,7},{7,6},{8,9},{9,8},{10,11... | collective-permute-start | bytes 98312 | tf_op jit(solution)/shard_map/ppermute | solution.py:306
  40.9 2.6 %collective-permute-start.14 = (bf16[2,4,2048]{2,1,0:T(4,128)(2,1)S(1)}, bf16[2,4,2048]{2,1,0:T(4,128)(2,1)S(1)}, u32[]{:S(2)}, u32[]{:S(2)}) collective-permute-start(bf16[2,4,2048]{2,1,0:T(4,128)(2,1)S(1)} %collective-permute-done.12.refs_0_), channel_id=1, source_target_pairs={{0,1},{1,0},{2,3},{3,2},{4,5},{5,4},{6,7},{7,6},{8,9},{9,8},{10,11... | collective-permute-start | bytes 98312 | tf_op jit(solution)/shard_map/ppermute | solution.py:306
  40.9 2.6 %collective-permute-start.15 = (bf16[2,4,2048]{2,1,0:T(4,128)(2,1)S(1)}, bf16[2,4,2048]{2,1,0:T(4,128)(2,1)S(1)}, u32[]{:S(2)}, u32[]{:S(2)}) collective-permute-start(bf16[2,4,2048]{2,1,0:T(4,128)(2,1)S(1)} %collective-permute-done.13.refs_1_), channel_id=1, source_target_pairs={{0,1},{1,0},{2,3},{3,2},{4,5},{5,4},{6,7},{7,6},{8,9},{9,8},{10,11... | collective-permute-start | bytes 98312 | tf_op jit(solution)/shard_map/ppermute | solution.py:306

commit v7 on v6

--- a/solution.py
+++ b/solution.py
@@ -71,11 +71,11 @@
     refs[-1][...] = array_ref[...]
 
 
-def join_kernel(mine_ref, arrived_ref, *refs):
-    joined_ref = refs[-1]
-    count = mine_ref.shape[0]
-    joined_ref[:count] = mine_ref[...]
-    joined_ref[count:] = arrived_ref[...]
+def join_kernel(*refs):
+    at = 0
+    for ref in refs[:-2]:
+        refs[-1][at : at + ref.shape[0]] = ref[...]
+        at += ref.shape[0]
 
 
 def share_kernel(
@@ -125,18 +125,18 @@
 
 def products(offsets, pieces, weight_ref, total):
     place = lax.axis_index("wide")
-    for of_piece, blocks_ref in zip(offsets, pieces):
-        features = blocks_ref.shape[2]
-        for k, offset in enumerate(of_piece):
-            start = pl.multiple_of((place ^ offset) * features, features)
-            total = total + jnp.dot(
-                blocks_ref[k], weight_ref[pl.ds(start, features), :], preferred_element_type=F32
-            )
+    blocks = [(ref, k) for ref in pieces for k in range(ref.shape[0])]
+    for offset, (ref, k) in zip(offsets, blocks):
+        features = ref.shape[2]
+        start = pl.multiple_of((place ^ offset) * features, features)
+        total = total + jnp.dot(
+            ref[k], weight_ref[pl.ds(start, features), :], preferred_element_type=F32
+        )
     return total
 
 
-def query_kernel(offsets, weight_ref, *refs):
-    pieces, before, out_ref = refs[: len(offsets)], refs[len(offsets) : -1], refs[-1]
+def query_kernel(offsets, count, weight_ref, *refs):
+    pieces, before, out_ref = refs[:count], refs[count:-1], refs[-1]
     total = before[0][...] if before else jnp.zeros(out_ref.shape, F32)
     out_ref[...] = products(offsets, pieces, weight_ref, total)
 
@@ -346,19 +346,19 @@
     totals = jax.ShapeDtypeStruct((rows, query_columns), F32)
     shares = jax.ShapeDtypeStruct((rows, key_projection.shape[1]), F32)
 
-    def query(by_piece, *total):
-        blocks = sum(piece.shape[0] for piece in by_piece.values())
+    def query(by, pieces, *total):
+        blocks = sum(piece.shape[0] for piece in pieces)
         return call(
-            functools.partial(query_kernel, tuple(tuple(o ^ by for o in offsets) for by in by_piece)),
+            functools.partial(query_kernel, tuple(o ^ b for b in by for o in offsets), len(pieces)),
             totals,
-            (w_query, *by_piece.values(), *total),
-            near=range(1 + len(by_piece)),
+            (w_query, *pieces, *total),
+            near=range(1 + len(pieces)),
             flops=2 * rows * blocks * features * query_columns,
             read=2 * blocks * features * query_columns,
         )
 
     *outer, far, near, core = bits
-    corners = (far | near | core, near | core, far | core)
+    corners = (far | core, near | core, far | near | core)
     blocks, offsets, key_share = scaled[None], [0], None
     for bit in outer:
         arrived = swap(blocks, bit | core, count)
@@ -393,18 +393,23 @@
         )
         offsets = offsets + [o ^ bit ^ core for o in offsets]
     pieces = {by: swap(blocks, by, count) for by in corners}
-    total = query({0: blocks, core: swap(blocks, core, count)})
-    pieces = {by: passed(piece, total) for by, piece in pieces.items()}
-    last = {by ^ core: swap(piece, core, count) for by, piece in pieces.items()}
-    total = query(pieces, total)
+    total = query((0, core), (blocks, swap(blocks, core, count)))
+    joined = call(
+        join_kernel,
+        jax.ShapeDtypeStruct((3 * len(offsets), rows, features), BF16),
+        (*pieces.values(), total),
+    )
+    last = swap(joined, core, count)
+    total = query(corners, (joined,), total)
+    by_last = tuple(by ^ core for by in corners)
     sent = held // KEY_VALUE_HEADS if held % KEY_VALUE_HEADS == 0 else held
     message = call(
         functools.partial(
-            message_kernel, tuple(tuple(o ^ by for o in offsets) for by in last), pairs
+            message_kernel, tuple(o ^ by for by in by_last for o in offsets), pairs
         ),
         jax.ShapeDtypeStruct((count, pairs * (sent + 3), HEAD_SIZE), F32),
-        (w_query, total, key_share, value_share, squares, *last.values()),
-        near=(0, *range(5, 5 + len(last))),
+        (w_query, total, key_share, value_share, squares, last),
+        near=(0, 5),
         flops=6 * blocks.size * query_columns,
         read=6 * len(offsets) * features * query_columns,
     )

time: 45.8 us -> 45.7 us (level)
    ppermute x16 -> x14, starting transfers between devices: 12.4 us -> 12.5 us  [swap(): return lax.ppermute(array, 'wide', [(i, i ^ bit) for i in range(count)])]
    pallas_call x12 -> x10, Pallas kernels: 12 us -> 12 us  [call(): pl.pallas_call(kernel, out_shape=out_shape, in_specs=specs, out_specs=jax...]
    ppermute x16 -> x14, waiting for transfers between devices: 8.16 us -> 8.16 us  [swap(): return lax.ppermute(array, 'wide', [(i, i ^ bit) for i in range(count)])]
  transfers between devices with their start and end apart: 16 -> 14, of which waited for: 5 -> 7; matrix products, arithmetic and copies ran while one was open for 0% -> 0% of each run, Pallas kernels for 12% -> 12%
where the time goes in v7:
time: 45.7 us; the launch traced here: 45.5 us
  blocking collectives  12.7 us (28%)
  starting transfers between devices  12.5 us (27%)
  Pallas kernels  12 us (26%)
  waiting for transfers between devices  8.16 us (18%)
    all_to_all x1, blocking collectives, body(): got = lax.all_to_all(message, 'wide', 0, 0, tiled=True)  12.7 us
    ppermute x14, starting transfers between devices, swap(): return lax.ppermute(array, 'wide', [(i, i ^ bit) for i in range(count)])  12.5 us
    pallas_call x10, Pallas kernels, call(): pl.pallas_call(kernel, out_shape=out_shape, in_specs=specs, out_specs=jax...  12 us
    ppermute x14, waiting for transfers between devices, swap(): return lax.ppermute(array, 'wide', [(i, i ^ bit) for i in range(count)])  8.16 us
  transfers between devices with their start and end apart: 14, of which 7 were waited for; matrix products, arithmetic and copies ran while one was open for 0% of the time, Pallas kernels for 12%

profile of v7, /device:TPU:0, one launch (start us, length us, event | category | flops | bytes accessed | tf_op | source)
XLA Modules:
  0.0 45.5 jit_solution(13975387194305171353)
XLA Ops:
  0.0 1.1 %shard_map.109.scaled_ref = bf16[16,1024]{1,0:T(8,128)(2,1)S(1)} custom-call(bf16[16,1024]{1,0:T(8,128)(2,1)} %far_tokens.3, bf16[1024]{0:T(1024)(128)(2,1)} %far_gain.1, s32[1,16]{1,0:T(1,128)} %bitcast.9, bf16[16384,512]{1,0:T(8,128)(2,1)} %weight_ref.7), custom_call_target="tpu_custom_call" | custom-call | bytes 67108864 | tf_op jit(solution)/shard_map/pallas_call | solution.py:35
  1.1 3.5 %collective-permute-start = (bf16[1,16,1024]{2,1,0:T(8,128)(2,1)S(1)}, bf16[1,16,1024]{2,1,0:T(8,128)(2,1)S(1)}, u32[]{:S(2)}, u32[]{:S(2)}) collective-permute-start(bf16[1,16,1024]{2,1,0:T(8,128)(2,1)S(1)} %bitcast.5), channel_id=1, source_target_pairs={{0,9},{1,8},{2,11},{3,10},{4,13},{5,12},{6,15},{7,14},{8,1},{9,0},... | collective-permute-start | bytes 98312 | tf_op jit(solution)/shard_map/ppermute | solution.py:306
  4.6 0.0 copy-done.5
  4.6 0.0 copy-done.4
  4.6 2.4 %shard_map.110 = (f32[16,512]{1,0:T(8,128)S(1)}, f32[16,512]{1,0:T(8,128)S(1)}, f32[16,128]{1,0:T(8,128)S(1)}, f32[2,4,128]{2,1,0:T(4,128)S(1)}, s32[4,128]{1,0:T(4,128)S(1)}) custom-call(bf16[16,1024]{1,0:T(8,128)(2,1)S(1)} %shard_map.109.scaled_ref, s32[16]{0:T(128)S(1)} %copy-done.4, f32[1,128]{1,0:T(1,128)S(1)} %copy-done.5, ...), custom_call_target="tpu_custom_call" | custom-call | flops 33554432 | bytes 2097152 | tf_op jit(solution)/shard_map/pallas_call | solution.py:35
  7.1 0.0 collective-permute-done.refs_1_
  7.1 0.7 %collective-permute-start.4 = (bf16[2,16,1024]{2,1,0:T(8,128)(2,1)S(1)}, bf16[2,16,1024]{2,1,0:T(8,128)(2,1)S(1)}, u32[]{:S(2)}, u32[]{:S(2)}) collective-permute-start(bf16[2,16,1024]{2,1,0:T(8,128)(2,1)S(1)} %shard_map.111.refs_0_), channel_id=1, source_target_pairs={{0,1},{1,0},{2,3},{3,2},{4,5},{5,4},{6,7},{7,6},{8,9},{9,8},{10,11... | collective-permute-start | bytes 196616 | tf_op jit(solution)/shard_map/ppermute | solution.py:306
  7.8 2.7 %collective-permute-start.3 = (bf16[2,16,1024]{2,1,0:T(8,128)(2,1)S(1)}, bf16[2,16,1024]{2,1,0:T(8,128)(2,1)S(1)}, u32[]{:S(2)}, u32[]{:S(2)}) collective-permute-start(bf16[2,16,1024]{2,1,0:T(8,128)(2,1)S(1)} %shard_map.111.refs_0_), channel_id=1, source_target_pairs={{0,7},{1,6},{2,5},{3,4},{4,3},{5,2},{6,1},{7,0},{8,15},{9,14},{10,... | collective-permute-start | bytes 196616 | tf_op jit(solution)/shard_map/ppermute | solution.py:306
  10.5 0.3 collective-permute-start.2
  10.8 0.1 collective-permute-start.1
  10.9 0.0 collective-permute-done.4.refs_1_
  10.9 0.0 copy-done
  10.9 0.6 %shard_map.112.refs_3_.refs_1_ = f32[16,512]{1,0:T(8,128)S(1)} custom-call(bf16[16384,512]{1,0:T(8,128)(2,1)S(1)} %copy-done, bf16[2,16,1024]{2,1,0:T(8,128)(2,1)S(1)} %shard_map.111.refs_0_, bf16[2,16,1024]{2,1,0:T(8,128)(2,1)S(1)} %collective-permute-done.4.refs_1_), custom_call_target="tpu_custom_call" | custom-call | flops 67108864 | bytes 4194304 | tf_op jit(solution)/shard_map/pallas_call | solution.py:35
  11.6 1.4 %collective-permute-done.3.refs_2_ = bf16[2,16,1024]{2,1,0:T(8,128)(2,1)S(1)} collective-permute-done((bf16[2,16,1024]{2,1,0:T(8,128)(2,1)S(1)}, bf16[2,16,1024]{2,1,0:T(8,128)(2,1)S(1)}, u32[]{:S(2)}, u32[]{:S(2)}) %collective-permute-start.3) | collective-permute-done | bytes 65568 | tf_op jit(solution)/shard_map/ppermute | solution.py:306
  13.0 1.6 %collective-permute-done.2.refs_1_ = bf16[2,16,1024]{2,1,0:T(8,128)(2,1)S(1)} collective-permute-done((bf16[2,16,1024]{2,1,0:T(8,128)(2,1)S(1)}, bf16[2,16,1024]{2,1,0:T(8,128)(2,1)S(1)}, u32[]{:S(2)}, u32[]{:S(2)}) %collective-permute-start.2) | collective-permute-done | bytes 65568 | tf_op jit(solution)/shard_map/ppermute | solution.py:306
  14.6 0.2 collective-permute-done.1.refs_0_
  14.8 0.0 copy-start.1
  14.9 0.0 copy-start.2
  14.9 0.3 collective-permute-start.5
  15.2 0.9 %shard_map.114.total_ref = f32[16,512]{1,0:T(8,128)S(1)} custom-call(bf16[16384,512]{1,0:T(8,128)(2,1)S(1)} %copy-done, bf16[6,16,1024]{2,1,0:T(8,128)(2,1)S(1)} %shard_map.113.refs_0_, f32[16,512]{1,0:T(8,128)S(1)} %shard_map.112.refs_3_.refs_1_), custom_call_target="tpu_custom_call" | custom-call | flops 100663296 | bytes 6291456 | tf_op jit(solution)/shard_map/pallas_call | solution.py:35
  16.1 0.3 collective-permute-done.5.refs_0_
  16.4 0.9 %shard_map.115 = f32[16,16,128]{2,1,0:T(8,128)S(1)} custom-call(bf16[16384,512]{1,0:T(8,128)(2,1)S(1)} %copy-done, f32[16,512]{1,0:T(8,128)S(1)} %shard_map.114.total_ref, f32[16,512]{1,0:T(8,128)S(1)} %get-tuple-element.12.refs_2_.key_ref, f32[16,512]{1,0:T(8,128)S(1)} %get-tuple-element.13.value_ref, f32[16,128]{1,0:T(8,128)S(1)} %get-tuple-element.14.squares_ref, ...), custom_call_target="tpu_custom_call" | custom-call | flops 100663296 | bytes 6291456 | tf_op jit(solution)/shard_map/pallas_call | solution.py:35
  17.3 12.7 %all_to_all.5.query_ref.rest_ref = f32[16,16,128]{2,1,0:T(8,128)S(1)} all-to-all(f32[16,16,128]{2,1,0:T(8,128)S(1)} %shard_map.115), channel_id=1, replica_groups=mesh['groups'=2,'wide'=16] {'wide'}, dimensions={0} | all-to-all | bytes 262144 | tf_op jit(solution)/shard_map/all_to_all | solution.py:417
  29.9 0.0 copy-done.1
  29.9 0.0 copy-done.2
  29.9 2.3 %shard_map.116 = bf16[4,2048]{1,0:T(4,128)(2,1)S(1)} custom-call(s32[4,128]{1,0:T(4,128)S(1)} %get-tuple-element.10.limits_ref, f32[2,4,128]{2,1,0:T(4,128)S(1)} %get-tuple-element.11.turns_ref, f32[16,16,128]{2,1,0:T(8,128)S(1)} %all_to_all.5.query_ref.rest_ref, f32[16,16,128]{2,1,0:T(8,128)S(1)} %all_to_all.5.query_ref.rest_ref, ...), custom_call_target="tpu_custom_call" | custom-call | flops 134217728 | bytes 8388608 | tf_op jit(solution)/shard_map/pallas_call | solution.py:35
  32.2 0.2 collective-permute-start.6
  32.4 4.0 %collective-permute-done.6 = bf16[1,4,2048]{2,1,0:T(4,128)(2,1)S(1)} collective-permute-done((bf16[1,4,2048]{2,1,0:T(4,128)(2,1)S(1)}, bf16[1,4,2048]{2,1,0:T(4,128)(2,1)S(1)}, u32[]{:S(2)}, u32[]{:S(2)}) %collective-permute-start.6) | collective-permute-done | bytes 16416 | tf_op jit(solution)/shard_map/ppermute | solution.py:306
  36.4 0.1 collective-permute-start.7
  36.5 0.1 collective-permute-start.11
  36.5 2.1 %collective-permute-start.10 = (bf16[2,4,2048]{2,1,0:T(4,128)(2,1)S(1)}, bf16[2,4,2048]{2,1,0:T(4,128)(2,1)S(1)}, u32[]{:S(2)}, u32[]{:S(2)}) collective-permute-start(bf16[2,4,2048]{2,1,0:T(4,128)(2,1)S(1)} %pad_maximum_fusion.refs_0_), channel_id=1, source_target_pairs={{0,7},{1,6},{2,5},{3,4},{4,3},{5,2},{6,1},{7,0},{8,15},{9,14},{10,... | collective-permute-start | bytes 98312 | tf_op jit(solution)/shard_map/ppermute | solution.py:306
  38.6 1.2 %collective-permute-start.8 = (bf16[2,4,2048]{2,1,0:T(4,128)(2,1)S(1)}, bf16[2,4,2048]{2,1,0:T(4,128)(2,1)S(1)}, u32[]{:S(2)}, u32[]{:S(2)}) collective-permute-start(bf16[2,4,2048]{2,1,0:T(4,128)(2,1)S(1)} %pad_maximum_fusion.refs_0_), channel_id=1, source_target_pairs={{0,1},{1,0},{2,3},{3,2},{4,5},{5,4},{6,7},{7,6},{8,9},{9,8},{10,11... | collective-permute-start | bytes 98312 | tf_op jit(solution)/shard_map/ppermute | solution.py:306
  39.8 0.0 collective-permute-done.7.refs_1_
  39.8 0.0 collective-permute-start.9
  39.8 0.1 collective-permute-done.11.refs_1_
  39.9 0.4 collective-permute-start.13
  40.3 0.5 %collective-permute-done.10.refs_0_ = bf16[2,4,2048]{2,1,0:T(4,128)(2,1)S(1)} collective-permute-done((bf16[2,4,2048]{2,1,0:T(4,128)(2,1)S(1)}, bf16[2,4,2048]{2,1,0:T(4,128)(2,1)S(1)}, u32[]{:S(2)}, u32[]{:S(2)}) %collective-permute-start.10) | collective-permute-done | bytes 32800 | tf_op jit(solution)/shard_map/ppermute | solution.py:306
  40.8 0.9 %collective-permute-start.12 = (bf16[2,4,2048]{2,1,0:T(4,128)(2,1)S(1)}, bf16[2,4,2048]{2,1,0:T(4,128)(2,1)S(1)}, u32[]{:S(2)}, u32[]{:S(2)}) collective-permute-start(bf16[2,4,2048]{2,1,0:T(4,128)(2,1)S(1)} %collective-permute-done.10.refs_0_), channel_id=1, source_target_pairs={{0,1},{1,0},{2,3},{3,2},{4,5},{5,4},{6,7},{7,6},{8,9},{9,8},{10,11... | collective-permute-start | bytes 98312 | tf_op jit(solution)/shard_map/ppermute | solution.py:306
  41.7 0.0 collective-permute-done.8.refs_2_
  41.7 0.0 collective-permute-done.9.refs_3_
  41.7 0.0 slice-done
  41.7 0.0 slice-done.1
  41.7 0.0 copy-done.3
  41.7 0.0 slice-done.2
  41.8 1.6 %shard_map.117.half_ref = f32[16,1024]{1,0:T(8,128)S(1)} custom-call(s32[1,16]{1,0:T(1,128)S(1)} %bitcast.11, bf16[8192,1024]{1,0:T(8,128)(2,1)S(1)} %bitcast.4, bf16[2,4,2048]{2,1,0:T(4,128)(2,1)S(1)} %pad_maximum_fusion.refs_0_, bf16[2,4,2048]{2,1,0:T(4,128)(2,1)S(1)} %collective-permute-done.7.refs_1_, ...), custom_call_target="tpu_custom_call" | custom-call | tf_op jit(solution)/shard_map/pallas_call | solution.py:35
  43.3 0.0 collective-permute-done.13.refs_3_
  43.3 0.0 collective-permute-done.12.refs_2_
  43.3 2.2 %shard_map.118 = bf16[16,1024]{1,0:T(8,128)(2,1)} custom-call(s32[1,16]{1,0:T(1,128)S(1)} %bitcast.12, bf16[8192,1024]{1,0:T(8,128)(2,1)S(1)} %bitcast.4, f32[16,1024]{1,0:T(8,128)S(1)} %shard_map.117.half_ref, bf16[2,4,2048]{2,1,0:T(4,128)(2,1)S(1)} %collective-permute-done.10.refs_0_, bf16[2,4,2048]{2,1,0:T(4,128)(2,1)S(1)} %collective-permute-done.11.refs_1_, ...), custom_call_target="tpu_custom_call" | custom-call | flops 134217728 | bytes 8388608 | tf_op jit(solution)/shard_map/pallas_call | solution.py:35
  (13 shorter events, 0.1 us)
Async XLA Ops:
  0.0 4.6 %copy-start.5 = (f32[1,128]{1,0:T(1,128)S(1)}, f32[1,128]{1,0:T(1,128)}, u32[]{:S(2)}) copy-start(f32[1,128]{1,0:T(1,128)} %constant.2.clone.rate_ref) | copy-start | bytes 1540
  0.0 10.9 %copy-start = (bf16[16384,512]{1,0:T(8,128)(2,1)S(1)}, bf16[16384,512]{1,0:T(8,128)(2,1)}, u32[]{:S(2)}) copy-start(bf16[16384,512]{1,0:T(8,128)(2,1)} %weight_ref.7) | copy-start | bytes 50331652
  0.0 4.6 %copy-start.4 = (s32[16]{0:T(128)S(1)}, s32[16]{0:T(128)}, u32[]{:S(2)}) copy-start(s32[16]{0:T(128)} %lengths_ref.1) | copy-start | bytes 196
  1.1 6.0 %collective-permute-start = (bf16[1,16,1024]{2,1,0:T(8,128)(2,1)S(1)}, bf16[1,16,1024]{2,1,0:T(8,128)(2,1)S(1)}, u32[]{:S(2)}, u32[]{:S(2)}) collective-permute-start(bf16[1,16,1024]{2,1,0:T(8,128)(2,1)S(1)} %bitcast.5), channel_id=1, source_target_pairs={{0,9},{1,8},{2,11},{3,10},{4,13},{5,12},{6,15},{7,14},{8,1},{9,0},... | collective-permute-start | bytes 98312 | tf_op jit(solution)/shard_map/ppermute | solution.py:306
  7.1 3.8 %collective-permute-start.4 = (bf16[2,16,1024]{2,1,0:T(8,128)(2,1)S(1)}, bf16[2,16,1024]{2,1,0:T(8,128)(2,1)S(1)}, u32[]{:S(2)}, u32[]{:S(2)}) collective-permute-start(bf16[2,16,1024]{2,1,0:T(8,128)(2,1)S(1)} %shard_map.111.refs_0_), channel_id=1, source_target_pairs={{0,1},{1,0},{2,3},{3,2},{4,5},{5,4},{6,7},{7,6},{8,9},{9,8},{10,11... | collective-permute-start | bytes 196616 | tf_op jit(solution)/shard_map/ppermute | solution.py:306
  7.8 5.2 %collective-permute-start.3 = (bf16[2,16,1024]{2,1,0:T(8,128)(2,1)S(1)}, bf16[2,16,1024]{2,1,0:T(8,128)(2,1)S(1)}, u32[]{:S(2)}, u32[]{:S(2)}) collective-permute-start(bf16[2,16,1024]{2,1,0:T(8,128)(2,1)S(1)} %shard_map.111.refs_0_), channel_id=1, source_target_pairs={{0,7},{1,6},{2,5},{3,4},{4,3},{5,2},{6,1},{7,0},{8,15},{9,14},{10,... | collective-permute-start | bytes 196616 | tf_op jit(solution)/shard_map/ppermute | solution.py:306
  10.5 4.1 %collective-permute-start.2 = (bf16[2,16,1024]{2,1,0:T(8,128)(2,1)S(1)}, bf16[2,16,1024]{2,1,0:T(8,128)(2,1)S(1)}, u32[]{:S(2)}, u32[]{:S(2)}) collective-permute-start(bf16[2,16,1024]{2,1,0:T(8,128)(2,1)S(1)} %shard_map.111.refs_0_), channel_id=1, source_target_pairs={{0,3},{1,2},{2,1},{3,0},{4,7},{5,6},{6,5},{7,4},{8,11},{9,10},{10,... | collective-permute-start | bytes 196616 | tf_op jit(solution)/shard_map/ppermute | solution.py:306
  10.8 4.0 %collective-permute-start.1 = (bf16[2,16,1024]{2,1,0:T(8,128)(2,1)S(1)}, bf16[2,16,1024]{2,1,0:T(8,128)(2,1)S(1)}, u32[]{:S(2)}, u32[]{:S(2)}) collective-permute-start(bf16[2,16,1024]{2,1,0:T(8,128)(2,1)S(1)} %shard_map.111.refs_0_), channel_id=1, source_target_pairs={{0,5},{1,4},{2,7},{3,6},{4,1},{5,0},{6,3},{7,2},{8,13},{9,12},{10,... | collective-permute-start | bytes 196616 | tf_op jit(solution)/shard_map/ppermute | solution.py:306
  14.8 15.1 %copy-start.1 = (bf16[4,4096,128]{2,1,0:T(8,128)(2,1)S(1)}, bf16[4,4096,128]{2,1,0:T(8,128)(2,1)}, u32[]{:S(2)}) copy-start(bf16[4,4096,128]{2,1,0:T(8,128)(2,1)} %keys_ref.1) | copy-start | bytes 12582916
  14.9 15.1 %copy-start.2 = (bf16[4,4096,128]{2,1,0:T(8,128)(2,1)S(1)}, bf16[4,4096,128]{2,1,0:T(8,128)(2,1)}, u32[]{:S(2)}) copy-start(bf16[4,4096,128]{2,1,0:T(8,128)(2,1)} %values_ref.1) | copy-start | bytes 12582916
  14.9 1.5 %collective-permute-start.5 = (bf16[6,16,1024]{2,1,0:T(8,128)(2,1)S(1)}, bf16[6,16,1024]{2,1,0:T(8,128)(2,1)S(1)}, u32[]{:S(2)}, u32[]{:S(2)}) collective-permute-start(bf16[6,16,1024]{2,1,0:T(8,128)(2,1)S(1)} %shard_map.113.refs_0_), channel_id=1, source_target_pairs={{0,1},{1,0},{2,3},{3,2},{4,5},{5,4},{6,7},{7,6},{8,9},{9,8},{10,11... | collective-permute-start | bytes 589832 | tf_op jit(solution)/shard_map/ppermute | solution.py:306
  15.2 26.5 %slice-start = ((s8[16777216]{0:T(1024)(128)(4,1)}), s8[4194304]{0:T(1024)(128)(4,1)S(1)}, s32[]{:S(2)}) async-start(s8[16777216]{0:T(1024)(128)(4,1)} %bitcast.3), calls=%async_computation.1 | async-start | bytes 8388608
  15.2 26.5 %slice-start.1 = ((s8[16777216]{0:T(1024)(128)(4,1)}), s8[4194304]{0:T(1024)(128)(4,1)S(1)}, s32[]{:S(2)}) async-start(s8[16777216]{0:T(1024)(128)(4,1)} %bitcast.3), calls=%async_computation.2 | async-start | bytes 8388608
  16.1 25.6 %copy-start.3 = (s32[16]{0:T(128)S(1)}, s32[16]{0:T(128)}, u32[]{:S(2)}) copy-start(s32[16]{0:T(128)} %param.13) | copy-start | bytes 196
  16.4 25.4 %slice-start.2 = ((s8[16777216]{0:T(1024)(128)(4,1)}), s8[4194304]{0:T(1024)(128)(4,1)S(1)}, s32[]{:S(2)}) async-start(s8[16777216]{0:T(1024)(128)(4,1)} %bitcast.3), calls=%async_computation.3 | async-start | bytes 8388608
  16.4 25.4 %slice-start.3 = ((s8[16777216]{0:T(1024)(128)(4,1)}), s8[4194304]{0:T(1024)(128)(4,1)S(1)}, s32[]{:S(2)}) async-start(s8[16777216]{0:T(1024)(128)(4,1)} %bitcast.3), calls=%async_computation.4 | async-start | bytes 8388608
  32.2 4.1 %collective-permute-start.6 = (bf16[1,4,2048]{2,1,0:T(4,128)(2,1)S(1)}, bf16[1,4,2048]{2,1,0:T(4,128)(2,1)S(1)}, u32[]{:S(2)}, u32[]{:S(2)}) collective-permute-start(bf16[1,4,2048]{2,1,0:T(4,128)(2,1)S(1)} %bitcast.7), channel_id=1, source_target_pairs={{0,9},{1,8},{2,11},{3,10},{4,13},{5,12},{6,15},{7,14},{8,1},{9,0},... | collective-permute-start | bytes 49160 | tf_op jit(solution)/shard_map/ppermute | solution.py:306
  36.4 3.4 %collective-permute-start.7 = (bf16[2,4,2048]{2,1,0:T(4,128)(2,1)S(1)}, bf16[2,4,2048]{2,1,0:T(4,128)(2,1)S(1)}, u32[]{:S(2)}, u32[]{:S(2)}) collective-permute-start(bf16[2,4,2048]{2,1,0:T(4,128)(2,1)S(1)} %pad_maximum_fusion.refs_0_), channel_id=1, source_target_pairs={{0,3},{1,2},{2,1},{3,0},{4,7},{5,6},{6,5},{7,4},{8,11},{9,10},{10,... | collective-permute-start | bytes 98312 | tf_op jit(solution)/shard_map/ppermute | solution.py:306
  36.5 3.4 %collective-permute-start.11 = (bf16[2,4,2048]{2,1,0:T(4,128)(2,1)S(1)}, bf16[2,4,2048]{2,1,0:T(4,128)(2,1)S(1)}, u32[]{:S(2)}, u32[]{:S(2)}) collective-permute-start(bf16[2,4,2048]{2,1,0:T(4,128)(2,1)S(1)} %pad_maximum_fusion.refs_0_), channel_id=1, source_target_pairs={{0,5},{1,4},{2,7},{3,6},{4,1},{5,0},{6,3},{7,2},{8,13},{9,12},{10,... | collective-permute-start | bytes 98312 | tf_op jit(solution)/shard_map/ppermute | solution.py:306
  36.5 4.3 %collective-permute-start.10 = (bf16[2,4,2048]{2,1,0:T(4,128)(2,1)S(1)}, bf16[2,4,2048]{2,1,0:T(4,128)(2,1)S(1)}, u32[]{:S(2)}, u32[]{:S(2)}) collective-permute-start(bf16[2,4,2048]{2,1,0:T(4,128)(2,1)S(1)} %pad_maximum_fusion.refs_0_), channel_id=1, source_target_pairs={{0,7},{1,6},{2,5},{3,4},{4,3},{5,2},{6,1},{7,0},{8,15},{9,14},{10,... | collective-permute-start | bytes 98312 | tf_op jit(solution)/shard_map/ppermute | solution.py:306
  38.6 3.1 %collective-permute-start.8 = (bf16[2,4,2048]{2,1,0:T(4,128)(2,1)S(1)}, bf16[2,4,2048]{2,1,0:T(4,128)(2,1)S(1)}, u32[]{:S(2)}, u32[]{:S(2)}) collective-permute-start(bf16[2,4,2048]{2,1,0:T(4,128)(2,1)S(1)} %pad_maximum_fusion.refs_0_), channel_id=1, source_target_pairs={{0,1},{1,0},{2,3},{3,2},{4,5},{5,4},{6,7},{7,6},{8,9},{9,8},{10,11... | collective-permute-start | bytes 98312 | tf_op jit(solution)/shard_map/ppermute | solution.py:306
  39.8 1.9 %collective-permute-start.9 = (bf16[2,4,2048]{2,1,0:T(4,128)(2,1)S(1)}, bf16[2,4,2048]{2,1,0:T(4,128)(2,1)S(1)}, u32[]{:S(2)}, u32[]{:S(2)}) collective-permute-start(bf16[2,4,2048]{2,1,0:T(4,128)(2,1)S(1)} %collective-permute-done.7.refs_1_), channel_id=1, source_target_pairs={{0,1},{1,0},{2,3},{3,2},{4,5},{5,4},{6,7},{7,6},{8,9},{9,8},{10,11... | collective-permute-start | bytes 98312 | tf_op jit(solution)/shard_map/ppermute | solution.py:306
  39.9 3.5 %collective-permute-start.13 = (bf16[2,4,2048]{2,1,0:T(4,128)(2,1)S(1)}, bf16[2,4,2048]{2,1,0:T(4,128)(2,1)S(1)}, u32[]{:S(2)}, u32[]{:S(2)}) collective-permute-start(bf16[2,4,2048]{2,1,0:T(4,128)(2,1)S(1)} %collective-permute-done.11.refs_1_), channel_id=1, source_target_pairs={{0,1},{1,0},{2,3},{3,2},{4,5},{5,4},{6,7},{7,6},{8,9},{9,8},{10,11... | collective-permute-start | bytes 98312 | tf_op jit(solution)/shard_map/ppermute | solution.py:306
  40.8 2.5 %collective-permute-start.12 = (bf16[2,4,2048]{2,1,0:T(4,128)(2,1)S(1)}, bf16[2,4,2048]{2,1,0:T(4,128)(2,1)S(1)}, u32[]{:S(2)}, u32[]{:S(2)}) collective-permute-start(bf16[2,4,2048]{2,1,0:T(4,128)(2,1)S(1)} %collective-permute-done.10.refs_0_), channel_id=1, source_target_pairs={{0,1},{1,0},{2,3},{3,2},{4,5},{5,4},{6,7},{7,6},{8,9},{9,8},{10,11... | collective-permute-start | bytes 98312 | tf_op jit(solution)/shard_map/ppermute | solution.py:306

commit v8 on v7

--- a/solution.py
+++ b/solution.py
@@ -141,6 +141,15 @@
     out_ref[...] = products(offsets, pieces, weight_ref, total)
 
 
+def turn_kernel(total_ref, keys_ref, turned_ref, same_ref):
+    same_ref[...] = total_ref[...]
+    pairs, length, _ = keys_ref.shape
+    step = math.gcd(length, 512)
+    for i in range(pairs):
+        for start in range(0, length, step):
+            turned_ref[i, :, start : start + step] = jnp.transpose(keys_ref[i, start : start + step, :])
+
+
 def message_kernel(offsets, pairs, weight_ref, total_ref, key_ref, value_ref, squares_ref, *refs):
     message_ref = refs[-1]
     query = products(offsets, refs[:-1], weight_ref, total_ref[...])
@@ -184,7 +193,7 @@
     pairs, width, limits_ref, turns_ref, query_ref, rest_ref, keys_ref, values_ref, out_ref, scores_ref, wide_ref
 ):
     group = query_ref.shape[0]
-    length = keys_ref.shape[1]
+    length = values_ref.shape[1]
     at = rest_ref.shape[1] - 3 * pairs
     summed = jnp.sum(rest_ref[:, at:, :], axis=0)
     score_scale = 1.0 / math.sqrt(HEAD_SIZE)
@@ -218,8 +227,8 @@
         for start in range(0, length, step):
             scores = lax.dot_general(
                 stacked,
-                side_by_side(keys_ref, members, start, step),
-                (((1,), (1,)), ((), ())),
+                jnp.concatenate([keys_ref[i, :, start : start + step] for i in members], axis=0),
+                (((1,), (0,)), ((), ())),
                 preferred_element_type=F32,
             )
             for at in range(0, step, HEAD_SIZE):
@@ -256,20 +265,21 @@
 
 def project_half(pairs, places, slot_ref, pieces, weight_ref, total):
     rows = slot_ref.shape[1]
-    held = pieces[0].shape[1]
+    held = sum(piece.shape[1] for piece in pieces)
     devices_of_head = rows // pairs
     place = lax.axis_index("wide")
     slot_of_row = jnp.transpose(jnp.broadcast_to(slot_ref[...], (rows, rows)))[:, 0:1]
     position = lax.broadcasted_iota(jnp.int32, (rows, held), 1)
     ordered, heads = [], []
     for z, by_piece in enumerate(places):
-        result = 0.0
-        for offsets, piece in zip(by_piece, pieces):
-            device = jnp.zeros_like(position)
-            for k, offset in enumerate(offsets):
-                device = jnp.where(position // pairs == k, (place ^ offset) % devices_of_head, device)
-            pick = (slot_of_row == device * pairs + position % pairs).astype(BF16)
-            result = result + jnp.dot(pick, piece[z], preferred_element_type=F32)
+        device = jnp.zeros_like(position)
+        for k, offset in enumerate(o for offsets in by_piece for o in offsets):
+            device = jnp.where(position // pairs == k, (place ^ offset) % devices_of_head, device)
+        pick = (slot_of_row == device * pairs + position % pairs).astype(BF16)
+        result = jnp.dot(
+            pick, jnp.concatenate([piece[z].astype(F32) for piece in pieces], axis=0).astype(BF16),
+            preferred_element_type=F32
+        )
         ordered.append(result.astype(BF16))
         heads.append((place ^ by_piece[0][0]) // devices_of_head)
     for g in range(QUERY_GROUP):
@@ -394,6 +404,13 @@
         offsets = offsets + [o ^ bit ^ core for o in offsets]
     pieces = {by: swap(blocks, by, count) for by in corners}
     total = query((0, core), (blocks, swap(blocks, core, count)))
+    keys, total = call(
+        turn_kernel,
+        (pltpu.VMEM((pairs, HEAD_SIZE, slot_key_cache.shape[1]), BF16), totals),
+        (total, slot_key_cache),
+        near=(1,),
+        read=2 * slot_key_cache.size,
+    )
     joined = call(
         join_kernel,
         jax.ShapeDtypeStruct((3 * len(offsets), rows, features), BF16),
@@ -430,7 +447,7 @@
     attended = call(
         functools.partial(attend_kernel, pairs, width),
         jax.ShapeDtypeStruct((pairs, QUERY_GROUP * HEAD_SIZE), BF16),
-        (limits, turns, query_rows, got, slot_key_cache, slot_value_cache),
+        (limits, turns, query_rows, got, keys, slot_value_cache),
         near=(4, 5),
         scratch=(
             pltpu.VMEM(

time: 45.7 us -> 45.1 us (0.987)
  waiting for transfers between devices: 8.16 us -> 7.04 us
    ppermute x14, waiting for transfers between devices: 8.16 us -> 7.04 us  [swap(): return lax.ppermute(array, 'wide', [(i, i ^ bit) for i in range(count)])]
    pallas_call x10 -> x11, Pallas kernels: 12 us -> 12.4 us  [call(): pl.pallas_call(kernel, out_shape=out_shape, in_specs=specs, out_specs=jax...]
  transfers between devices with their start and end apart: 14 -> 14, of which waited for: 7 -> 7; matrix products, arithmetic and copies ran while one was open for 0% -> 0% of each run, Pallas kernels for 12% -> 15%
where the time goes in v8:
time: 45.1 us; the launch traced here: 44.9 us
  blocking collectives  12.7 us (28%)
  starting transfers between devices  12.5 us (28%)
  Pallas kernels  12.4 us (27%)
  waiting for transfers between devices  7.04 us (16%)
    all_to_all x1, blocking collectives, body(): got = lax.all_to_all(message, 'wide', 0, 0, tiled=True)  12.7 us
    ppermute x14, starting transfers between devices, swap(): return lax.ppermute(array, 'wide', [(i, i ^ bit) for i in range(count)])  12.5 us
    pallas_call x11, Pallas kernels, call(): pl.pallas_call(kernel, out_shape=out_shape, in_specs=specs, out_specs=jax...  12.4 us
    ppermute x14, waiting for transfers between devices, swap(): return lax.ppermute(array, 'wide', [(i, i ^ bit) for i in range(count)])  7.04 us
  transfers between devices with their start and end apart: 14, of which 7 were waited for; matrix products, arithmetic and copies ran while one was open for 0% of the time, Pallas kernels for 15%

profile of v8, /device:TPU:0, one launch (start us, length us, event | category | flops | bytes accessed | tf_op | source)
XLA Modules:
  0.0 44.9 jit_solution(686783580952775961)
XLA Ops:
  0.0 1.1 %shard_map.109.scaled_ref = bf16[16,1024]{1,0:T(8,128)(2,1)S(1)} custom-call(bf16[16,1024]{1,0:T(8,128)(2,1)} %far_tokens.3, bf16[1024]{0:T(1024)(128)(2,1)} %far_gain.1, s32[1,16]{1,0:T(1,128)} %bitcast.9, bf16[16384,512]{1,0:T(8,128)(2,1)} %weight_ref.7), custom_call_target="tpu_custom_call" | custom-call | bytes 67108864 | tf_op jit(solution)/shard_map/pallas_call | solution.py:35
  1.1 3.5 %collective-permute-start = (bf16[1,16,1024]{2,1,0:T(8,128)(2,1)S(1)}, bf16[1,16,1024]{2,1,0:T(8,128)(2,1)S(1)}, u32[]{:S(2)}, u32[]{:S(2)}) collective-permute-start(bf16[1,16,1024]{2,1,0:T(8,128)(2,1)S(1)} %bitcast.5), channel_id=1, source_target_pairs={{0,9},{1,8},{2,11},{3,10},{4,13},{5,12},{6,15},{7,14},{8,1},{9,0},... | collective-permute-start | bytes 98312 | tf_op jit(solution)/shard_map/ppermute | solution.py:316
  4.6 0.0 copy-done.4
  4.6 0.0 copy-done.5
  4.6 2.4 %shard_map.110 = (f32[16,512]{1,0:T(8,128)S(1)}, f32[16,512]{1,0:T(8,128)S(1)}, f32[16,128]{1,0:T(8,128)S(1)}, f32[2,4,128]{2,1,0:T(4,128)S(1)}, s32[4,128]{1,0:T(4,128)S(1)}) custom-call(bf16[16,1024]{1,0:T(8,128)(2,1)S(1)} %shard_map.109.scaled_ref, s32[16]{0:T(128)S(1)} %copy-done.4, f32[1,128]{1,0:T(1,128)S(1)} %copy-done.5, ...), custom_call_target="tpu_custom_call" | custom-call | flops 33554432 | bytes 2097152 | tf_op jit(solution)/shard_map/pallas_call | solution.py:35
  7.0 0.0 collective-permute-done.refs_1_
  7.1 0.0 copy-start.1
  7.1 0.7 %collective-permute-start.4 = (bf16[2,16,1024]{2,1,0:T(8,128)(2,1)S(1)}, bf16[2,16,1024]{2,1,0:T(8,128)(2,1)S(1)}, u32[]{:S(2)}, u32[]{:S(2)}) collective-permute-start(bf16[2,16,1024]{2,1,0:T(8,128)(2,1)S(1)} %shard_map.111.refs_0_), channel_id=1, source_target_pairs={{0,1},{1,0},{2,3},{3,2},{4,5},{5,4},{6,7},{7,6},{8,9},{9,8},{10,11... | collective-permute-start | bytes 196616 | tf_op jit(solution)/shard_map/ppermute | solution.py:316
  7.8 2.7 %collective-permute-start.3 = (bf16[2,16,1024]{2,1,0:T(8,128)(2,1)S(1)}, bf16[2,16,1024]{2,1,0:T(8,128)(2,1)S(1)}, u32[]{:S(2)}, u32[]{:S(2)}) collective-permute-start(bf16[2,16,1024]{2,1,0:T(8,128)(2,1)S(1)} %shard_map.111.refs_0_), channel_id=1, source_target_pairs={{0,7},{1,6},{2,5},{3,4},{4,3},{5,2},{6,1},{7,0},{8,15},{9,14},{10,... | collective-permute-start | bytes 196616 | tf_op jit(solution)/shard_map/ppermute | solution.py:316
  10.5 0.3 collective-permute-start.2
  10.9 0.1 collective-permute-start.1
  10.9 0.0 collective-permute-done.4.refs_1_
  10.9 0.0 copy-done
  10.9 0.6 %shard_map.112.total_ref = f32[16,512]{1,0:T(8,128)S(1)} custom-call(bf16[16384,512]{1,0:T(8,128)(2,1)S(1)} %copy-done, bf16[2,16,1024]{2,1,0:T(8,128)(2,1)S(1)} %shard_map.111.refs_0_, bf16[2,16,1024]{2,1,0:T(8,128)(2,1)S(1)} %collective-permute-done.4.refs_1_), custom_call_target="tpu_custom_call" | custom-call | flops 67108864 | bytes 4194304 | tf_op jit(solution)/shard_map/pallas_call | solution.py:35
  11.6 0.0 copy-done.1
  11.6 1.1 %shard_map.113 = (bf16[4,128,4096]{2,1,0:T(8,128)(2,1)S(1)}, f32[16,512]{1,0:T(8,128)S(1)}) custom-call(f32[16,512]{1,0:T(8,128)S(1)} %shard_map.112.total_ref, bf16[4,4096,128]{2,1,0:T(8,128)(2,1)S(1)} %copy-done.1), custom_call_target="tpu_custom_call" | custom-call | bytes 4194304 | tf_op jit(solution)/shard_map/pallas_call | solution.py:35
  12.7 0.3 collective-permute-done.3.refs_2_
  13.0 1.6 %collective-permute-done.2.refs_1_ = bf16[2,16,1024]{2,1,0:T(8,128)(2,1)S(1)} collective-permute-done((bf16[2,16,1024]{2,1,0:T(8,128)(2,1)S(1)}, bf16[2,16,1024]{2,1,0:T(8,128)(2,1)S(1)}, u32[]{:S(2)}, u32[]{:S(2)}) %collective-permute-start.2) | collective-permute-done | bytes 65568 | tf_op jit(solution)/shard_map/ppermute | solution.py:316
  14.6 0.2 collective-permute-done.1.refs_0_
  14.9 0.3 collective-permute-start.5
  15.2 0.9 %shard_map.115.total_ref = f32[16,512]{1,0:T(8,128)S(1)} custom-call(bf16[16384,512]{1,0:T(8,128)(2,1)S(1)} %copy-done, bf16[6,16,1024]{2,1,0:T(8,128)(2,1)S(1)} %shard_map.114.refs_0_, f32[16,512]{1,0:T(8,128)S(1)} %get-tuple-element.15.refs_3_.refs_1_), custom_call_target="tpu_custom_call" | custom-call | flops 100663296 | bytes 6291456 | tf_op jit(solution)/shard_map/pallas_call | solution.py:35
  16.1 0.3 collective-permute-done.5.refs_0_
  16.4 0.9 %shard_map.116 = f32[16,16,128]{2,1,0:T(8,128)S(1)} custom-call(bf16[16384,512]{1,0:T(8,128)(2,1)S(1)} %copy-done, f32[16,512]{1,0:T(8,128)S(1)} %shard_map.115.total_ref, f32[16,512]{1,0:T(8,128)S(1)} %get-tuple-element.14.refs_2_.key_ref, f32[16,512]{1,0:T(8,128)S(1)} %get-tuple-element.16.value_ref, f32[16,128]{1,0:T(8,128)S(1)} %get-tuple-element.17.squares_ref, ...), custom_call_target="tpu_custom_call" | custom-call | flops 100663296 | bytes 6291456 | tf_op jit(solution)/shard_map/pallas_call | solution.py:35
  17.3 12.7 %all_to_all.5.query_ref.rest_ref = f32[16,16,128]{2,1,0:T(8,128)S(1)} all-to-all(f32[16,16,128]{2,1,0:T(8,128)S(1)} %shard_map.116), channel_id=1, replica_groups=mesh['groups'=2,'wide'=16] {'wide'}, dimensions={0} | all-to-all | bytes 262144 | tf_op jit(solution)/shard_map/all_to_all | solution.py:434
  30.0 0.0 copy-done.2
  30.0 1.8 %shard_map.117 = bf16[4,2048]{1,0:T(4,128)(2,1)S(1)} custom-call(s32[4,128]{1,0:T(4,128)S(1)} %get-tuple-element.12.limits_ref, f32[2,4,128]{2,1,0:T(4,128)S(1)} %get-tuple-element.13.turns_ref, f32[16,16,128]{2,1,0:T(8,128)S(1)} %all_to_all.5.query_ref.rest_ref, f32[16,16,128]{2,1,0:T(8,128)S(1)} %all_to_all.5.query_ref.rest_ref, ...), custom_call_target="tpu_custom_call" | custom-call | flops 134217728 | bytes 8388608 | tf_op jit(solution)/shard_map/pallas_call | solution.py:35
  31.8 0.1 collective-permute-start.6
  32.0 4.0 %collective-permute-done.6 = bf16[1,4,2048]{2,1,0:T(4,128)(2,1)S(1)} collective-permute-done((bf16[1,4,2048]{2,1,0:T(4,128)(2,1)S(1)}, bf16[1,4,2048]{2,1,0:T(4,128)(2,1)S(1)}, u32[]{:S(2)}, u32[]{:S(2)}) %collective-permute-start.6) | collective-permute-done | bytes 16416 | tf_op jit(solution)/shard_map/ppermute | solution.py:316
  36.0 0.1 collective-permute-start.7
  36.0 0.1 collective-permute-start.11
  36.1 2.1 %collective-permute-start.10 = (bf16[2,4,2048]{2,1,0:T(4,128)(2,1)S(1)}, bf16[2,4,2048]{2,1,0:T(4,128)(2,1)S(1)}, u32[]{:S(2)}, u32[]{:S(2)}) collective-permute-start(bf16[2,4,2048]{2,1,0:T(4,128)(2,1)S(1)} %pad_maximum_fusion.refs_0_), channel_id=1, source_target_pairs={{0,7},{1,6},{2,5},{3,4},{4,3},{5,2},{6,1},{7,0},{8,15},{9,14},{10,... | collective-permute-start | bytes 98312 | tf_op jit(solution)/shard_map/ppermute | solution.py:316
  38.2 1.2 %collective-permute-start.8 = (bf16[2,4,2048]{2,1,0:T(4,128)(2,1)S(1)}, bf16[2,4,2048]{2,1,0:T(4,128)(2,1)S(1)}, u32[]{:S(2)}, u32[]{:S(2)}) collective-permute-start(bf16[2,4,2048]{2,1,0:T(4,128)(2,1)S(1)} %pad_maximum_fusion.refs_0_), channel_id=1, source_target_pairs={{0,1},{1,0},{2,3},{3,2},{4,5},{5,4},{6,7},{7,6},{8,9},{9,8},{10,11... | collective-permute-start | bytes 98312 | tf_op jit(solution)/shard_map/ppermute | solution.py:316
  39.4 0.0 collective-permute-done.7.refs_1_
  39.4 0.0 collective-permute-start.9
  39.4 0.1 collective-permute-done.11.refs_1_
  39.5 0.4 collective-permute-start.13
  39.9 0.5 %collective-permute-done.10.refs_0_ = bf16[2,4,2048]{2,1,0:T(4,128)(2,1)S(1)} collective-permute-done((bf16[2,4,2048]{2,1,0:T(4,128)(2,1)S(1)}, bf16[2,4,2048]{2,1,0:T(4,128)(2,1)S(1)}, u32[]{:S(2)}, u32[]{:S(2)}) %collective-permute-start.10) | collective-permute-done | bytes 32800 | tf_op jit(solution)/shard_map/ppermute | solution.py:316
  40.4 0.9 %collective-permute-start.12 = (bf16[2,4,2048]{2,1,0:T(4,128)(2,1)S(1)}, bf16[2,4,2048]{2,1,0:T(4,128)(2,1)S(1)}, u32[]{:S(2)}, u32[]{:S(2)}) collective-permute-start(bf16[2,4,2048]{2,1,0:T(4,128)(2,1)S(1)} %collective-permute-done.10.refs_0_), channel_id=1, source_target_pairs={{0,1},{1,0},{2,3},{3,2},{4,5},{5,4},{6,7},{7,6},{8,9},{9,8},{10,11... | collective-permute-start | bytes 98312 | tf_op jit(solution)/shard_map/ppermute | solution.py:316
  41.3 0.0 collective-permute-done.8.refs_2_
  41.3 0.0 collective-permute-done.9.refs_3_
  41.3 0.0 slice-done
  41.3 0.0 slice-done.1
  41.3 0.0 slice-done.2
  41.3 0.0 slice-done.3
  41.4 1.4 %shard_map.118.half_ref = f32[16,1024]{1,0:T(8,128)S(1)} custom-call(s32[1,16]{1,0:T(1,128)S(1)} %bitcast.11, bf16[8192,1024]{1,0:T(8,128)(2,1)S(1)} %bitcast.4, bf16[2,4,2048]{2,1,0:T(4,128)(2,1)S(1)} %pad_maximum_fusion.refs_0_, bf16[2,4,2048]{2,1,0:T(4,128)(2,1)S(1)} %collective-permute-done.7.refs_1_, ...), custom_call_target="tpu_custom_call" | custom-call | tf_op jit(solution)/shard_map/pallas_call | solution.py:35
  42.8 0.0 collective-permute-done.13.refs_3_
  42.8 0.0 collective-permute-done.12.refs_2_
  42.8 2.1 %shard_map.119 = bf16[16,1024]{1,0:T(8,128)(2,1)} custom-call(s32[1,16]{1,0:T(1,128)S(1)} %bitcast.12, bf16[8192,1024]{1,0:T(8,128)(2,1)S(1)} %bitcast.4, f32[16,1024]{1,0:T(8,128)S(1)} %shard_map.118.half_ref, bf16[2,4,2048]{2,1,0:T(4,128)(2,1)S(1)} %collective-permute-done.10.refs_0_, bf16[2,4,2048]{2,1,0:T(4,128)(2,1)S(1)} %collective-permute-done.11.refs_1_, ...), custom_call_target="tpu_custom_call" | custom-call | flops 134217728 | bytes 8388608 | tf_op jit(solution)/shard_map/pallas_call | solution.py:35
  (14 shorter events, 0.1 us)
Async XLA Ops:
  0.0 4.6 %copy-start.4 = (s32[16]{0:T(128)S(1)}, s32[16]{0:T(128)}, u32[]{:S(2)}) copy-start(s32[16]{0:T(128)} %lengths_ref.1) | copy-start | bytes 196
  0.0 4.6 %copy-start.5 = (f32[1,128]{1,0:T(1,128)S(1)}, f32[1,128]{1,0:T(1,128)}, u32[]{:S(2)}) copy-start(f32[1,128]{1,0:T(1,128)} %constant.2.clone.rate_ref) | copy-start | bytes 1540
  0.0 10.9 %copy-start = (bf16[16384,512]{1,0:T(8,128)(2,1)S(1)}, bf16[16384,512]{1,0:T(8,128)(2,1)}, u32[]{:S(2)}) copy-start(bf16[16384,512]{1,0:T(8,128)(2,1)} %weight_ref.7) | copy-start | bytes 50331652
  1.1 6.0 %collective-permute-start = (bf16[1,16,1024]{2,1,0:T(8,128)(2,1)S(1)}, bf16[1,16,1024]{2,1,0:T(8,128)(2,1)S(1)}, u32[]{:S(2)}, u32[]{:S(2)}) collective-permute-start(bf16[1,16,1024]{2,1,0:T(8,128)(2,1)S(1)} %bitcast.5), channel_id=1, source_target_pairs={{0,9},{1,8},{2,11},{3,10},{4,13},{5,12},{6,15},{7,14},{8,1},{9,0},... | collective-permute-start | bytes 98312 | tf_op jit(solution)/shard_map/ppermute | solution.py:316
  7.1 4.5 %copy-start.1 = (bf16[4,4096,128]{2,1,0:T(8,128)(2,1)S(1)}, bf16[4,4096,128]{2,1,0:T(8,128)(2,1)}, u32[]{:S(2)}) copy-start(bf16[4,4096,128]{2,1,0:T(8,128)(2,1)} %keys_ref.1) | copy-start | bytes 12582916
  7.1 3.8 %collective-permute-start.4 = (bf16[2,16,1024]{2,1,0:T(8,128)(2,1)S(1)}, bf16[2,16,1024]{2,1,0:T(8,128)(2,1)S(1)}, u32[]{:S(2)}, u32[]{:S(2)}) collective-permute-start(bf16[2,16,1024]{2,1,0:T(8,128)(2,1)S(1)} %shard_map.111.refs_0_), channel_id=1, source_target_pairs={{0,1},{1,0},{2,3},{3,2},{4,5},{5,4},{6,7},{7,6},{8,9},{9,8},{10,11... | collective-permute-start | bytes 196616 | tf_op jit(solution)/shard_map/ppermute | solution.py:316
  7.8 5.2 %collective-permute-start.3 = (bf16[2,16,1024]{2,1,0:T(8,128)(2,1)S(1)}, bf16[2,16,1024]{2,1,0:T(8,128)(2,1)S(1)}, u32[]{:S(2)}, u32[]{:S(2)}) collective-permute-start(bf16[2,16,1024]{2,1,0:T(8,128)(2,1)S(1)} %shard_map.111.refs_0_), channel_id=1, source_target_pairs={{0,7},{1,6},{2,5},{3,4},{4,3},{5,2},{6,1},{7,0},{8,15},{9,14},{10,... | collective-permute-start | bytes 196616 | tf_op jit(solution)/shard_map/ppermute | solution.py:316
  10.5 4.1 %collective-permute-start.2 = (bf16[2,16,1024]{2,1,0:T(8,128)(2,1)S(1)}, bf16[2,16,1024]{2,1,0:T(8,128)(2,1)S(1)}, u32[]{:S(2)}, u32[]{:S(2)}) collective-permute-start(bf16[2,16,1024]{2,1,0:T(8,128)(2,1)S(1)} %shard_map.111.refs_0_), channel_id=1, source_target_pairs={{0,3},{1,2},{2,1},{3,0},{4,7},{5,6},{6,5},{7,4},{8,11},{9,10},{10,... | collective-permute-start | bytes 196616 | tf_op jit(solution)/shard_map/ppermute | solution.py:316
  10.9 4.0 %collective-permute-start.1 = (bf16[2,16,1024]{2,1,0:T(8,128)(2,1)S(1)}, bf16[2,16,1024]{2,1,0:T(8,128)(2,1)S(1)}, u32[]{:S(2)}, u32[]{:S(2)}) collective-permute-start(bf16[2,16,1024]{2,1,0:T(8,128)(2,1)S(1)} %shard_map.111.refs_0_), channel_id=1, source_target_pairs={{0,5},{1,4},{2,7},{3,6},{4,1},{5,0},{6,3},{7,2},{8,13},{9,12},{10,... | collective-permute-start | bytes 196616 | tf_op jit(solution)/shard_map/ppermute | solution.py:316
  14.9 1.5 %collective-permute-start.5 = (bf16[6,16,1024]{2,1,0:T(8,128)(2,1)S(1)}, bf16[6,16,1024]{2,1,0:T(8,128)(2,1)S(1)}, u32[]{:S(2)}, u32[]{:S(2)}) collective-permute-start(bf16[6,16,1024]{2,1,0:T(8,128)(2,1)S(1)} %shard_map.114.refs_0_), channel_id=1, source_target_pairs={{0,1},{1,0},{2,3},{3,2},{4,5},{5,4},{6,7},{7,6},{8,9},{9,8},{10,11... | collective-permute-start | bytes 589832 | tf_op jit(solution)/shard_map/ppermute | solution.py:316
  15.2 26.2 %slice-start = ((s8[16777216]{0:T(1024)(128)(4,1)}), s8[4194304]{0:T(1024)(128)(4,1)S(1)}, s32[]{:S(2)}) async-start(s8[16777216]{0:T(1024)(128)(4,1)} %bitcast.3), calls=%async_computation.1 | async-start | bytes 8388608
  15.2 26.2 %slice-start.1 = ((s8[16777216]{0:T(1024)(128)(4,1)}), s8[4194304]{0:T(1024)(128)(4,1)S(1)}, s32[]{:S(2)}) async-start(s8[16777216]{0:T(1024)(128)(4,1)} %bitcast.3), calls=%async_computation.2 | async-start | bytes 8388608
  16.4 13.6 %copy-start.2 = (bf16[4,4096,128]{2,1,0:T(8,128)(2,1)S(1)}, bf16[4,4096,128]{2,1,0:T(8,128)(2,1)}, u32[]{:S(2)}) copy-start(bf16[4,4096,128]{2,1,0:T(8,128)(2,1)} %values_ref.1) | copy-start | bytes 12582916
  16.4 25.0 %slice-start.2 = ((s8[16777216]{0:T(1024)(128)(4,1)}), s8[4194304]{0:T(1024)(128)(4,1)S(1)}, s32[]{:S(2)}) async-start(s8[16777216]{0:T(1024)(128)(4,1)} %bitcast.3), calls=%async_computation.3 | async-start | bytes 8388608
  16.4 25.0 %slice-start.3 = ((s8[16777216]{0:T(1024)(128)(4,1)}), s8[4194304]{0:T(1024)(128)(4,1)S(1)}, s32[]{:S(2)}) async-start(s8[16777216]{0:T(1024)(128)(4,1)} %bitcast.3), calls=%async_computation.4 | async-start | bytes 8388608
  30.0 11.4 %copy-start.3 = (s32[16]{0:T(128)S(1)}, s32[16]{0:T(128)}, u32[]{:S(2)}) copy-start(s32[16]{0:T(128)} %param.13) | copy-start | bytes 196
  31.8 4.1 %collective-permute-start.6 = (bf16[1,4,2048]{2,1,0:T(4,128)(2,1)S(1)}, bf16[1,4,2048]{2,1,0:T(4,128)(2,1)S(1)}, u32[]{:S(2)}, u32[]{:S(2)}) collective-permute-start(bf16[1,4,2048]{2,1,0:T(4,128)(2,1)S(1)} %bitcast.7), channel_id=1, source_target_pairs={{0,9},{1,8},{2,11},{3,10},{4,13},{5,12},{6,15},{7,14},{8,1},{9,0},... | collective-permute-start | bytes 49160 | tf_op jit(solution)/shard_map/ppermute | solution.py:316
  36.0 3.4 %collective-permute-start.7 = (bf16[2,4,2048]{2,1,0:T(4,128)(2,1)S(1)}, bf16[2,4,2048]{2,1,0:T(4,128)(2,1)S(1)}, u32[]{:S(2)}, u32[]{:S(2)}) collective-permute-start(bf16[2,4,2048]{2,1,0:T(4,128)(2,1)S(1)} %pad_maximum_fusion.refs_0_), channel_id=1, source_target_pairs={{0,3},{1,2},{2,1},{3,0},{4,7},{5,6},{6,5},{7,4},{8,11},{9,10},{10,... | collective-permute-start | bytes 98312 | tf_op jit(solution)/shard_map/ppermute | solution.py:316
  36.0 3.4 %collective-permute-start.11 = (bf16[2,4,2048]{2,1,0:T(4,128)(2,1)S(1)}, bf16[2,4,2048]{2,1,0:T(4,128)(2,1)S(1)}, u32[]{:S(2)}, u32[]{:S(2)}) collective-permute-start(bf16[2,4,2048]{2,1,0:T(4,128)(2,1)S(1)} %pad_maximum_fusion.refs_0_), channel_id=1, source_target_pairs={{0,5},{1,4},{2,7},{3,6},{4,1},{5,0},{6,3},{7,2},{8,13},{9,12},{10,... | collective-permute-start | bytes 98312 | tf_op jit(solution)/shard_map/ppermute | solution.py:316
  36.1 4.3 %collective-permute-start.10 = (bf16[2,4,2048]{2,1,0:T(4,128)(2,1)S(1)}, bf16[2,4,2048]{2,1,0:T(4,128)(2,1)S(1)}, u32[]{:S(2)}, u32[]{:S(2)}) collective-permute-start(bf16[2,4,2048]{2,1,0:T(4,128)(2,1)S(1)} %pad_maximum_fusion.refs_0_), channel_id=1, source_target_pairs={{0,7},{1,6},{2,5},{3,4},{4,3},{5,2},{6,1},{7,0},{8,15},{9,14},{10,... | collective-permute-start | bytes 98312 | tf_op jit(solution)/shard_map/ppermute | solution.py:316
  38.2 3.1 %collective-permute-start.8 = (bf16[2,4,2048]{2,1,0:T(4,128)(2,1)S(1)}, bf16[2,4,2048]{2,1,0:T(4,128)(2,1)S(1)}, u32[]{:S(2)}, u32[]{:S(2)}) collective-permute-start(bf16[2,4,2048]{2,1,0:T(4,128)(2,1)S(1)} %pad_maximum_fusion.refs_0_), channel_id=1, source_target_pairs={{0,1},{1,0},{2,3},{3,2},{4,5},{5,4},{6,7},{7,6},{8,9},{9,8},{10,11... | collective-permute-start | bytes 98312 | tf_op jit(solution)/shard_map/ppermute | solution.py:316
  39.4 1.9 %collective-permute-start.9 = (bf16[2,4,2048]{2,1,0:T(4,128)(2,1)S(1)}, bf16[2,4,2048]{2,1,0:T(4,128)(2,1)S(1)}, u32[]{:S(2)}, u32[]{:S(2)}) collective-permute-start(bf16[2,4,2048]{2,1,0:T(4,128)(2,1)S(1)} %collective-permute-done.7.refs_1_), channel_id=1, source_target_pairs={{0,1},{1,0},{2,3},{3,2},{4,5},{5,4},{6,7},{7,6},{8,9},{9,8},{10,11... | collective-permute-start | bytes 98312 | tf_op jit(solution)/shard_map/ppermute | solution.py:316
  39.5 3.4 %collective-permute-start.13 = (bf16[2,4,2048]{2,1,0:T(4,128)(2,1)S(1)}, bf16[2,4,2048]{2,1,0:T(4,128)(2,1)S(1)}, u32[]{:S(2)}, u32[]{:S(2)}) collective-permute-start(bf16[2,4,2048]{2,1,0:T(4,128)(2,1)S(1)} %collective-permute-done.11.refs_1_), channel_id=1, source_target_pairs={{0,1},{1,0},{2,3},{3,2},{4,5},{5,4},{6,7},{7,6},{8,9},{9,8},{10,11... | collective-permute-start | bytes 98312 | tf_op jit(solution)/shard_map/ppermute | solution.py:316
  40.4 2.4 %collective-permute-start.12 = (bf16[2,4,2048]{2,1,0:T(4,128)(2,1)S(1)}, bf16[2,4,2048]{2,1,0:T(4,128)(2,1)S(1)}, u32[]{:S(2)}, u32[]{:S(2)}) collective-permute-start(bf16[2,4,2048]{2,1,0:T(4,128)(2,1)S(1)} %collective-permute-done.10.refs_0_), channel_id=1, source_target_pairs={{0,1},{1,0},{2,3},{3,2},{4,5},{5,4},{6,7},{7,6},{8,9},{9,8},{10,11... | collective-permute-start | bytes 98312 | tf_op jit(solution)/shard_map/ppermute | solution.py:316

commit v9 on v8

--- a/solution.py
+++ b/solution.py
@@ -150,23 +150,31 @@
             turned_ref[i, :, start : start + step] = jnp.transpose(keys_ref[i, start : start + step, :])
 
 
+def halves(array):
+    high = array.astype(BF16).astype(F32)
+    return [high, array - high]
+
+
 def message_kernel(offsets, pairs, weight_ref, total_ref, key_ref, value_ref, squares_ref, *refs):
     message_ref = refs[-1]
     query = products(offsets, refs[:-1], weight_ref, total_ref[...])
     rows = query.shape[0]
     held = query.shape[1] // HEAD_SIZE
+    lane = lax.broadcasted_iota(jnp.int32, squares_ref.shape, 1) // (HEAD_SIZE // 4)
+    left, squares = squares_ref[...], jnp.zeros(squares_ref.shape, F32)
+    for k in range(3):
+        part = left.astype(BF16).astype(F32)
+        squares = jnp.where(lane == k, part, squares)
+        left = left - part
+    key, value = halves(key_ref[...]), halves(value_ref[...])
     for target in range(message_ref.shape[0]):
         head, first = target * pairs // rows, target * pairs % rows
         slots = slice(first, first + pairs)
         columns = slice(head * HEAD_SIZE, (head + 1) * HEAD_SIZE)
         sent = range(head, held, KEY_VALUE_HEADS) if held % KEY_VALUE_HEADS == 0 else range(held)
-        at = 0
-        for j in sent:
-            message_ref[target, at : at + pairs, :] = query[slots, j * HEAD_SIZE : (j + 1) * HEAD_SIZE]
-            at += pairs
-        message_ref[target, at : at + pairs, :] = key_ref[slots, columns]
-        message_ref[target, at + pairs : at + 2 * pairs, :] = value_ref[slots, columns]
-        message_ref[target, at + 2 * pairs : at + 3 * pairs, :] = squares_ref[slots, :]
+        parts = [query[slots, j * HEAD_SIZE : (j + 1) * HEAD_SIZE] for j in sent]
+        parts += [half[slots, columns] for half in key + value] + [squares[slots, :]]
+        message_ref[target] = jnp.concatenate(parts, axis=0).astype(BF16)
 
 
 def rotated(values, cosines, sines):
@@ -190,12 +198,18 @@
 
 
 def attend_kernel(
-    pairs, width, limits_ref, turns_ref, query_ref, rest_ref, keys_ref, values_ref, out_ref, scores_ref, wide_ref
+    pairs, width, limits_ref, turns_ref, query_ref, rest_ref, keys_ref, values_ref, out_ref, scores_ref, wide_ref, near_ref
 ):
     group = query_ref.shape[0]
     length = values_ref.shape[1]
-    at = rest_ref.shape[1] - 3 * pairs
-    summed = jnp.sum(rest_ref[:, at:, :], axis=0)
+    at = rest_ref.shape[1] - 5 * pairs
+    near_ref[...] = query_ref[...].astype(F32)
+    summed = jnp.sum(rest_ref[...].astype(F32), axis=0)[at:, :]
+    new_keys = summed[:pairs, :] + summed[pairs : 2 * pairs, :]
+    new_values = summed[2 * pairs : 3 * pairs, :] + summed[3 * pairs : 4 * pairs, :]
+    lane = lax.broadcasted_iota(jnp.int32, (pairs, HEAD_SIZE), 1)
+    first_of_part = (lane % (HEAD_SIZE // 4) == 0) & (lane < 3 * (HEAD_SIZE // 4))
+    squares = jnp.sum(jnp.where(first_of_part, summed[4 * pairs :, :], 0.0), axis=1, keepdims=True)
     score_scale = 1.0 / math.sqrt(HEAD_SIZE)
     step = math.gcd(length, 512)
     many = 2 if pairs % 2 == 0 else 1
@@ -204,12 +218,12 @@
         members = range(base, base + many)
         queries, owns, values, limits = [], [], [], []
         for i in members:
-            scale = lax.rsqrt(summed[2 * pairs + i : 2 * pairs + i + 1, :] * (1.0 / width) + EPS)
+            scale = lax.rsqrt(squares[i : i + 1, :] * (1.0 / width) + EPS)
             cosines, sines = turns_ref[0, i : i + 1, :], turns_ref[1, i : i + 1, :]
-            query = rotated(query_ref[:, i, :] * scale, cosines, sines).astype(BF16)
-            key = jnp.broadcast_to(summed[i : i + 1, :] * scale, (8, HEAD_SIZE))
+            query = rotated(near_ref[:, i, :] * scale, cosines, sines).astype(BF16)
+            key = jnp.broadcast_to(new_keys[i : i + 1, :] * scale, (8, HEAD_SIZE))
             key = rotated(key, cosines, sines)[0:1, :].astype(BF16).astype(F32)
-            values.append((summed[pairs + i : pairs + i + 1, :] * scale).astype(BF16).astype(F32))
+            values.append((new_values[i : i + 1, :] * scale).astype(BF16).astype(F32))
             owns.append(jnp.sum(query.astype(F32) * key, axis=1, keepdims=True))
             limits.append(jnp.broadcast_to(limits_ref[i : i + 1, :], (group, HEAD_SIZE)))
             blank = jnp.zeros_like(query)
@@ -424,7 +438,7 @@
         functools.partial(
             message_kernel, tuple(o ^ by for by in by_last for o in offsets), pairs
         ),
-        jax.ShapeDtypeStruct((count, pairs * (sent + 3), HEAD_SIZE), F32),
+        jax.ShapeDtypeStruct((count, pairs * (sent + 5), HEAD_SIZE), BF16),
         (w_query, total, key_share, value_share, squares, last),
         near=(0, 5),
         flops=6 * blocks.size * query_columns,
@@ -454,6 +468,7 @@
                 ((pairs + 1) // 2, min(pairs, 2) * QUERY_GROUP, slot_key_cache.shape[1]), F32
             ),
             pltpu.VMEM((pairs, QUERY_GROUP * HEAD_SIZE), F32),
+            pltpu.VMEM(query_rows.shape, F32),
         ),
         limit=8 * MIB,
         flops=4 * QUERY_GROUP * slot_key_cache.size,

time: 45.1 us -> 44.6 us (0.989)
  blocking collectives: 12.7 us -> 12.2 us
  waiting for transfers between devices: 7.04 us -> 7.5 us
    all_to_all x1, blocking collectives: 12.7 us -> 12.2 us  [body(): got = lax.all_to_all(message, 'wide', 0, 0, tiled=True)]
    ppermute x14, starting transfers between devices: 12.5 us -> 12.1 us  [swap(): return lax.ppermute(array, 'wide', [(i, i ^ bit) for i in range(count)])]
    ppermute x14, waiting for transfers between devices: 7.04 us -> 7.5 us  [swap(): return lax.ppermute(array, 'wide', [(i, i ^ bit) for i in range(count)])]
where the time goes in v9:
time: 44.6 us; the launch traced here: 44.4 us
  Pallas kernels  12.5 us (28%)
  blocking collectives  12.2 us (27%)
  starting transfers between devices  12.1 us (27%)
  waiting for transfers between devices  7.5 us (17%)
    pallas_call x11, Pallas kernels, call(): pl.pallas_call(kernel, out_shape=out_shape, in_specs=specs, out_specs=jax...  12.5 us
    all_to_all x1, blocking collectives, body(): got = lax.all_to_all(message, 'wide', 0, 0, tiled=True)  12.2 us
    ppermute x14, starting transfers between devices, swap(): return lax.ppermute(array, 'wide', [(i, i ^ bit) for i in range(count)])  12.1 us
    ppermute x14, waiting for transfers between devices, swap(): return lax.ppermute(array, 'wide', [(i, i ^ bit) for i in range(count)])  7.5 us
  transfers between devices with their start and end apart: 14, of which 7 were waited for; matrix products, arithmetic and copies ran while one was open for 0% of the time, Pallas kernels for 15%

profile of v9, /device:TPU:0, one launch (start us, length us, event | category | flops | bytes accessed | tf_op | source)
XLA Modules:
  0.0 44.4 jit_solution(14443966507434248524)
XLA Ops:
  0.0 1.1 %shard_map.109.scaled_ref = bf16[16,1024]{1,0:T(8,128)(2,1)S(1)} custom-call(bf16[16,1024]{1,0:T(8,128)(2,1)} %far_tokens.3, bf16[1024]{0:T(1024)(128)(2,1)} %far_gain.1, s32[1,16]{1,0:T(1,128)} %bitcast.9, bf16[16384,512]{1,0:T(8,128)(2,1)} %weight_ref.7), custom_call_target="tpu_custom_call" | custom-call | bytes 67108864 | tf_op jit(solution)/shard_map/pallas_call | solution.py:35
  1.1 3.5 %collective-permute-start = (bf16[1,16,1024]{2,1,0:T(8,128)(2,1)S(1)}, bf16[1,16,1024]{2,1,0:T(8,128)(2,1)S(1)}, u32[]{:S(2)}, u32[]{:S(2)}) collective-permute-start(bf16[1,16,1024]{2,1,0:T(8,128)(2,1)S(1)} %bitcast.5), channel_id=1, source_target_pairs={{0,9},{1,8},{2,11},{3,10},{4,13},{5,12},{6,15},{7,14},{8,1},{9,0},... | collective-permute-start | bytes 98312 | tf_op jit(solution)/shard_map/ppermute | solution.py:330
  4.6 0.0 copy-done.4
  4.6 0.0 copy-done.5
  4.6 2.4 %shard_map.110 = (f32[16,512]{1,0:T(8,128)S(1)}, f32[16,512]{1,0:T(8,128)S(1)}, f32[16,128]{1,0:T(8,128)S(1)}, f32[2,4,128]{2,1,0:T(4,128)S(1)}, s32[4,128]{1,0:T(4,128)S(1)}) custom-call(bf16[16,1024]{1,0:T(8,128)(2,1)S(1)} %shard_map.109.scaled_ref, s32[16]{0:T(128)S(1)} %copy-done.4, f32[1,128]{1,0:T(1,128)S(1)} %copy-done.5, ...), custom_call_target="tpu_custom_call" | custom-call | flops 33554432 | bytes 2097152 | tf_op jit(solution)/shard_map/pallas_call | solution.py:35
  7.0 0.0 collective-permute-done.refs_1_
  7.1 0.0 copy-start.1
  7.1 0.7 %collective-permute-start.4 = (bf16[2,16,1024]{2,1,0:T(8,128)(2,1)S(1)}, bf16[2,16,1024]{2,1,0:T(8,128)(2,1)S(1)}, u32[]{:S(2)}, u32[]{:S(2)}) collective-permute-start(bf16[2,16,1024]{2,1,0:T(8,128)(2,1)S(1)} %shard_map.111.refs_0_), channel_id=1, source_target_pairs={{0,1},{1,0},{2,3},{3,2},{4,5},{5,4},{6,7},{7,6},{8,9},{9,8},{10,11... | collective-permute-start | bytes 196616 | tf_op jit(solution)/shard_map/ppermute | solution.py:330
  7.8 2.7 %collective-permute-start.3 = (bf16[2,16,1024]{2,1,0:T(8,128)(2,1)S(1)}, bf16[2,16,1024]{2,1,0:T(8,128)(2,1)S(1)}, u32[]{:S(2)}, u32[]{:S(2)}) collective-permute-start(bf16[2,16,1024]{2,1,0:T(8,128)(2,1)S(1)} %shard_map.111.refs_0_), channel_id=1, source_target_pairs={{0,7},{1,6},{2,5},{3,4},{4,3},{5,2},{6,1},{7,0},{8,15},{9,14},{10,... | collective-permute-start | bytes 196616 | tf_op jit(solution)/shard_map/ppermute | solution.py:330
  10.5 0.3 collective-permute-start.2
  10.9 0.1 collective-permute-start.1
  10.9 0.0 collective-permute-done.4.refs_1_
  10.9 0.0 copy-done
  10.9 0.6 %shard_map.112.total_ref = f32[16,512]{1,0:T(8,128)S(1)} custom-call(bf16[16384,512]{1,0:T(8,128)(2,1)S(1)} %copy-done, bf16[2,16,1024]{2,1,0:T(8,128)(2,1)S(1)} %shard_map.111.refs_0_, bf16[2,16,1024]{2,1,0:T(8,128)(2,1)S(1)} %collective-permute-done.4.refs_1_), custom_call_target="tpu_custom_call" | custom-call | flops 67108864 | bytes 4194304 | tf_op jit(solution)/shard_map/pallas_call | solution.py:35
  11.6 0.0 copy-done.1
  11.6 1.1 %shard_map.113 = (bf16[4,128,4096]{2,1,0:T(8,128)(2,1)S(1)}, f32[16,512]{1,0:T(8,128)S(1)}) custom-call(f32[16,512]{1,0:T(8,128)S(1)} %shard_map.112.total_ref, bf16[4,4096,128]{2,1,0:T(8,128)(2,1)S(1)} %copy-done.1), custom_call_target="tpu_custom_call" | custom-call | bytes 4194304 | tf_op jit(solution)/shard_map/pallas_call | solution.py:35
  12.7 0.3 collective-permute-done.3.refs_2_
  13.0 1.6 %collective-permute-done.2.refs_1_ = bf16[2,16,1024]{2,1,0:T(8,128)(2,1)S(1)} collective-permute-done((bf16[2,16,1024]{2,1,0:T(8,128)(2,1)S(1)}, bf16[2,16,1024]{2,1,0:T(8,128)(2,1)S(1)}, u32[]{:S(2)}, u32[]{:S(2)}) %collective-permute-start.2) | collective-permute-done | bytes 65568 | tf_op jit(solution)/shard_map/ppermute | solution.py:330
  14.6 0.2 collective-permute-done.1.refs_0_
  14.9 0.3 collective-permute-start.5
  15.2 0.9 %shard_map.115.total_ref = f32[16,512]{1,0:T(8,128)S(1)} custom-call(bf16[16384,512]{1,0:T(8,128)(2,1)S(1)} %copy-done, bf16[6,16,1024]{2,1,0:T(8,128)(2,1)S(1)} %shard_map.114.refs_0_, f32[16,512]{1,0:T(8,128)S(1)} %get-tuple-element.15.refs_3_.refs_1_), custom_call_target="tpu_custom_call" | custom-call | flops 100663296 | bytes 6291456 | tf_op jit(solution)/shard_map/pallas_call | solution.py:35
  16.1 0.3 collective-permute-done.5.refs_0_
  16.4 0.9 %shard_map.116 = bf16[16,24,128]{2,1,0:T(8,128)(2,1)S(1)} custom-call(bf16[16384,512]{1,0:T(8,128)(2,1)S(1)} %copy-done, f32[16,512]{1,0:T(8,128)S(1)} %shard_map.115.total_ref, f32[16,512]{1,0:T(8,128)S(1)} %get-tuple-element.14.refs_2_.key_ref, f32[16,512]{1,0:T(8,128)S(1)} %get-tuple-element.16.value_ref, f32[16,128]{1,0:T(8,128)S(1)} %get-tuple-element.17.squares_ref, ...), custom_call_target="tpu_custom_call" | custom-call | flops 100663296 | bytes 6291456 | tf_op jit(solution)/shard_map/pallas_call | solution.py:35
  17.3 12.2 %all_to_all.5.query_ref.rest_ref = bf16[16,24,128]{2,1,0:T(8,128)(2,1)S(1)} all-to-all(bf16[16,24,128]{2,1,0:T(8,128)(2,1)S(1)} %shard_map.116), channel_id=1, replica_groups=mesh['groups'=2,'wide'=16] {'wide'}, dimensions={0} | all-to-all | bytes 196608 | tf_op jit(solution)/shard_map/all_to_all | solution.py:448
  29.5 0.0 copy-done.2
  29.5 1.9 %shard_map.117 = bf16[4,2048]{1,0:T(4,128)(2,1)S(1)} custom-call(s32[4,128]{1,0:T(4,128)S(1)} %get-tuple-element.12.limits_ref, f32[2,4,128]{2,1,0:T(4,128)S(1)} %get-tuple-element.13.turns_ref, bf16[16,24,128]{2,1,0:T(8,128)(2,1)S(1)} %all_to_all.5.query_ref.rest_ref, bf16[16,24,128]{2,1,0:T(8,128)(2,1)S(1)} %all_to_all.5.query_ref.rest_ref, ...), custom_call_target="tpu_custom_call" | custom-call | flops 134217728 | bytes 8388608 | tf_op jit(solution)/shard_map/pallas_call | solution.py:35
  31.4 0.1 collective-permute-start.6
  31.4 4.0 %collective-permute-done.6 = bf16[1,4,2048]{2,1,0:T(4,128)(2,1)S(1)} collective-permute-done((bf16[1,4,2048]{2,1,0:T(4,128)(2,1)S(1)}, bf16[1,4,2048]{2,1,0:T(4,128)(2,1)S(1)}, u32[]{:S(2)}, u32[]{:S(2)}) %collective-permute-start.6) | collective-permute-done | bytes 16416 | tf_op jit(solution)/shard_map/ppermute | solution.py:330
  35.5 0.1 collective-permute-start.7
  35.6 0.3 collective-permute-start.11
  35.9 2.0 %collective-permute-start.10 = (bf16[2,4,2048]{2,1,0:T(4,128)(2,1)S(1)}, bf16[2,4,2048]{2,1,0:T(4,128)(2,1)S(1)}, u32[]{:S(2)}, u32[]{:S(2)}) collective-permute-start(bf16[2,4,2048]{2,1,0:T(4,128)(2,1)S(1)} %pad_maximum_fusion.refs_0_), channel_id=1, source_target_pairs={{0,7},{1,6},{2,5},{3,4},{4,3},{5,2},{6,1},{7,0},{8,15},{9,14},{10,... | collective-permute-start | bytes 98312 | tf_op jit(solution)/shard_map/ppermute | solution.py:330
  37.8 1.1 %collective-permute-start.8 = (bf16[2,4,2048]{2,1,0:T(4,128)(2,1)S(1)}, bf16[2,4,2048]{2,1,0:T(4,128)(2,1)S(1)}, u32[]{:S(2)}, u32[]{:S(2)}) collective-permute-start(bf16[2,4,2048]{2,1,0:T(4,128)(2,1)S(1)} %pad_maximum_fusion.refs_0_), channel_id=1, source_target_pairs={{0,1},{1,0},{2,3},{3,2},{4,5},{5,4},{6,7},{7,6},{8,9},{9,8},{10,11... | collective-permute-start | bytes 98312 | tf_op jit(solution)/shard_map/ppermute | solution.py:330
  38.9 0.0 collective-permute-done.7.refs_1_
  38.9 0.0 collective-permute-start.9
  38.9 0.4 collective-permute-done.11.refs_1_
  39.3 0.1 collective-permute-start.13
  39.4 0.6 %collective-permute-done.10.refs_0_ = bf16[2,4,2048]{2,1,0:T(4,128)(2,1)S(1)} collective-permute-done((bf16[2,4,2048]{2,1,0:T(4,128)(2,1)S(1)}, bf16[2,4,2048]{2,1,0:T(4,128)(2,1)S(1)}, u32[]{:S(2)}, u32[]{:S(2)}) %collective-permute-start.10) | collective-permute-done | bytes 32800 | tf_op jit(solution)/shard_map/ppermute | solution.py:330
  40.1 0.8 %collective-permute-start.12 = (bf16[2,4,2048]{2,1,0:T(4,128)(2,1)S(1)}, bf16[2,4,2048]{2,1,0:T(4,128)(2,1)S(1)}, u32[]{:S(2)}, u32[]{:S(2)}) collective-permute-start(bf16[2,4,2048]{2,1,0:T(4,128)(2,1)S(1)} %collective-permute-done.10.refs_0_), channel_id=1, source_target_pairs={{0,1},{1,0},{2,3},{3,2},{4,5},{5,4},{6,7},{7,6},{8,9},{9,8},{10,11... | collective-permute-start | bytes 98312 | tf_op jit(solution)/shard_map/ppermute | solution.py:330
  40.9 0.0 collective-permute-done.8.refs_2_
  40.9 0.0 collective-permute-done.9.refs_3_
  40.9 0.0 slice-done
  40.9 0.0 slice-done.1
  40.9 0.0 slice-done.2
  40.9 0.0 slice-done.3
  40.9 1.4 %shard_map.118.half_ref = f32[16,1024]{1,0:T(8,128)S(1)} custom-call(s32[1,16]{1,0:T(1,128)S(1)} %bitcast.11, bf16[8192,1024]{1,0:T(8,128)(2,1)S(1)} %bitcast.4, bf16[2,4,2048]{2,1,0:T(4,128)(2,1)S(1)} %pad_maximum_fusion.refs_0_, bf16[2,4,2048]{2,1,0:T(4,128)(2,1)S(1)} %collective-permute-done.7.refs_1_, ...), custom_call_target="tpu_custom_call" | custom-call | tf_op jit(solution)/shard_map/pallas_call | solution.py:35
  42.4 0.0 collective-permute-done.13.refs_3_
  42.4 0.0 collective-permute-done.12.refs_2_
  42.4 2.1 %shard_map.119 = bf16[16,1024]{1,0:T(8,128)(2,1)} custom-call(s32[1,16]{1,0:T(1,128)S(1)} %bitcast.12, bf16[8192,1024]{1,0:T(8,128)(2,1)S(1)} %bitcast.4, f32[16,1024]{1,0:T(8,128)S(1)} %shard_map.118.half_ref, bf16[2,4,2048]{2,1,0:T(4,128)(2,1)S(1)} %collective-permute-done.10.refs_0_, bf16[2,4,2048]{2,1,0:T(4,128)(2,1)S(1)} %collective-permute-done.11.refs_1_, ...), custom_call_target="tpu_custom_call" | custom-call | flops 134217728 | bytes 8388608 | tf_op jit(solution)/shard_map/pallas_call | solution.py:35
  (14 shorter events, 0.1 us)
Async XLA Ops:
  0.0 4.6 %copy-start.4 = (s32[16]{0:T(128)S(1)}, s32[16]{0:T(128)}, u32[]{:S(2)}) copy-start(s32[16]{0:T(128)} %lengths_ref.1) | copy-start | bytes 196
  0.0 4.6 %copy-start.5 = (f32[1,128]{1,0:T(1,128)S(1)}, f32[1,128]{1,0:T(1,128)}, u32[]{:S(2)}) copy-start(f32[1,128]{1,0:T(1,128)} %constant.2.clone.rate_ref) | copy-start | bytes 1540
  0.0 10.9 %copy-start = (bf16[16384,512]{1,0:T(8,128)(2,1)S(1)}, bf16[16384,512]{1,0:T(8,128)(2,1)}, u32[]{:S(2)}) copy-start(bf16[16384,512]{1,0:T(8,128)(2,1)} %weight_ref.7) | copy-start | bytes 50331652
  1.1 6.0 %collective-permute-start = (bf16[1,16,1024]{2,1,0:T(8,128)(2,1)S(1)}, bf16[1,16,1024]{2,1,0:T(8,128)(2,1)S(1)}, u32[]{:S(2)}, u32[]{:S(2)}) collective-permute-start(bf16[1,16,1024]{2,1,0:T(8,128)(2,1)S(1)} %bitcast.5), channel_id=1, source_target_pairs={{0,9},{1,8},{2,11},{3,10},{4,13},{5,12},{6,15},{7,14},{8,1},{9,0},... | collective-permute-start | bytes 98312 | tf_op jit(solution)/shard_map/ppermute | solution.py:330
  7.1 4.5 %copy-start.1 = (bf16[4,4096,128]{2,1,0:T(8,128)(2,1)S(1)}, bf16[4,4096,128]{2,1,0:T(8,128)(2,1)}, u32[]{:S(2)}) copy-start(bf16[4,4096,128]{2,1,0:T(8,128)(2,1)} %keys_ref.1) | copy-start | bytes 12582916
  7.1 3.8 %collective-permute-start.4 = (bf16[2,16,1024]{2,1,0:T(8,128)(2,1)S(1)}, bf16[2,16,1024]{2,1,0:T(8,128)(2,1)S(1)}, u32[]{:S(2)}, u32[]{:S(2)}) collective-permute-start(bf16[2,16,1024]{2,1,0:T(8,128)(2,1)S(1)} %shard_map.111.refs_0_), channel_id=1, source_target_pairs={{0,1},{1,0},{2,3},{3,2},{4,5},{5,4},{6,7},{7,6},{8,9},{9,8},{10,11... | collective-permute-start | bytes 196616 | tf_op jit(solution)/shard_map/ppermute | solution.py:330
  7.8 5.2 %collective-permute-start.3 = (bf16[2,16,1024]{2,1,0:T(8,128)(2,1)S(1)}, bf16[2,16,1024]{2,1,0:T(8,128)(2,1)S(1)}, u32[]{:S(2)}, u32[]{:S(2)}) collective-permute-start(bf16[2,16,1024]{2,1,0:T(8,128)(2,1)S(1)} %shard_map.111.refs_0_), channel_id=1, source_target_pairs={{0,7},{1,6},{2,5},{3,4},{4,3},{5,2},{6,1},{7,0},{8,15},{9,14},{10,... | collective-permute-start | bytes 196616 | tf_op jit(solution)/shard_map/ppermute | solution.py:330
  10.5 4.1 %collective-permute-start.2 = (bf16[2,16,1024]{2,1,0:T(8,128)(2,1)S(1)}, bf16[2,16,1024]{2,1,0:T(8,128)(2,1)S(1)}, u32[]{:S(2)}, u32[]{:S(2)}) collective-permute-start(bf16[2,16,1024]{2,1,0:T(8,128)(2,1)S(1)} %shard_map.111.refs_0_), channel_id=1, source_target_pairs={{0,3},{1,2},{2,1},{3,0},{4,7},{5,6},{6,5},{7,4},{8,11},{9,10},{10,... | collective-permute-start | bytes 196616 | tf_op jit(solution)/shard_map/ppermute | solution.py:330
  10.9 4.0 %collective-permute-start.1 = (bf16[2,16,1024]{2,1,0:T(8,128)(2,1)S(1)}, bf16[2,16,1024]{2,1,0:T(8,128)(2,1)S(1)}, u32[]{:S(2)}, u32[]{:S(2)}) collective-permute-start(bf16[2,16,1024]{2,1,0:T(8,128)(2,1)S(1)} %shard_map.111.refs_0_), channel_id=1, source_target_pairs={{0,5},{1,4},{2,7},{3,6},{4,1},{5,0},{6,3},{7,2},{8,13},{9,12},{10,... | collective-permute-start | bytes 196616 | tf_op jit(solution)/shard_map/ppermute | solution.py:330
  14.9 1.5 %collective-permute-start.5 = (bf16[6,16,1024]{2,1,0:T(8,128)(2,1)S(1)}, bf16[6,16,1024]{2,1,0:T(8,128)(2,1)S(1)}, u32[]{:S(2)}, u32[]{:S(2)}) collective-permute-start(bf16[6,16,1024]{2,1,0:T(8,128)(2,1)S(1)} %shard_map.114.refs_0_), channel_id=1, source_target_pairs={{0,1},{1,0},{2,3},{3,2},{4,5},{5,4},{6,7},{7,6},{8,9},{9,8},{10,11... | collective-permute-start | bytes 589832 | tf_op jit(solution)/shard_map/ppermute | solution.py:330
  15.2 25.7 %slice-start = ((s8[16777216]{0:T(1024)(128)(4,1)}), s8[4194304]{0:T(1024)(128)(4,1)S(1)}, s32[]{:S(2)}) async-start(s8[16777216]{0:T(1024)(128)(4,1)} %bitcast.3), calls=%async_computation.1 | async-start | bytes 8388608
  15.2 25.7 %slice-start.1 = ((s8[16777216]{0:T(1024)(128)(4,1)}), s8[4194304]{0:T(1024)(128)(4,1)S(1)}, s32[]{:S(2)}) async-start(s8[16777216]{0:T(1024)(128)(4,1)} %bitcast.3), calls=%async_computation.2 | async-start | bytes 8388608
  16.4 13.1 %copy-start.2 = (bf16[4,4096,128]{2,1,0:T(8,128)(2,1)S(1)}, bf16[4,4096,128]{2,1,0:T(8,128)(2,1)}, u32[]{:S(2)}) copy-start(bf16[4,4096,128]{2,1,0:T(8,128)(2,1)} %values_ref.1) | copy-start | bytes 12582916
  16.4 24.5 %slice-start.2 = ((s8[16777216]{0:T(1024)(128)(4,1)}), s8[4194304]{0:T(1024)(128)(4,1)S(1)}, s32[]{:S(2)}) async-start(s8[16777216]{0:T(1024)(128)(4,1)} %bitcast.3), calls=%async_computation.3 | async-start | bytes 8388608
  16.4 24.5 %slice-start.3 = ((s8[16777216]{0:T(1024)(128)(4,1)}), s8[4194304]{0:T(1024)(128)(4,1)S(1)}, s32[]{:S(2)}) async-start(s8[16777216]{0:T(1024)(128)(4,1)} %bitcast.3), calls=%async_computation.4 | async-start | bytes 8388608
  29.5 11.4 %copy-start.3 = (s32[16]{0:T(128)S(1)}, s32[16]{0:T(128)}, u32[]{:S(2)}) copy-start(s32[16]{0:T(128)} %param.13) | copy-start | bytes 196
  31.4 4.1 %collective-permute-start.6 = (bf16[1,4,2048]{2,1,0:T(4,128)(2,1)S(1)}, bf16[1,4,2048]{2,1,0:T(4,128)(2,1)S(1)}, u32[]{:S(2)}, u32[]{:S(2)}) collective-permute-start(bf16[1,4,2048]{2,1,0:T(4,128)(2,1)S(1)} %bitcast.7), channel_id=1, source_target_pairs={{0,9},{1,8},{2,11},{3,10},{4,13},{5,12},{6,15},{7,14},{8,1},{9,0},... | collective-permute-start | bytes 49160 | tf_op jit(solution)/shard_map/ppermute | solution.py:330
  35.5 3.4 %collective-permute-start.7 = (bf16[2,4,2048]{2,1,0:T(4,128)(2,1)S(1)}, bf16[2,4,2048]{2,1,0:T(4,128)(2,1)S(1)}, u32[]{:S(2)}, u32[]{:S(2)}) collective-permute-start(bf16[2,4,2048]{2,1,0:T(4,128)(2,1)S(1)} %pad_maximum_fusion.refs_0_), channel_id=1, source_target_pairs={{0,3},{1,2},{2,1},{3,0},{4,7},{5,6},{6,5},{7,4},{8,11},{9,10},{10,... | collective-permute-start | bytes 98312 | tf_op jit(solution)/shard_map/ppermute | solution.py:330
  35.6 3.7 %collective-permute-start.11 = (bf16[2,4,2048]{2,1,0:T(4,128)(2,1)S(1)}, bf16[2,4,2048]{2,1,0:T(4,128)(2,1)S(1)}, u32[]{:S(2)}, u32[]{:S(2)}) collective-permute-start(bf16[2,4,2048]{2,1,0:T(4,128)(2,1)S(1)} %pad_maximum_fusion.refs_0_), channel_id=1, source_target_pairs={{0,5},{1,4},{2,7},{3,6},{4,1},{5,0},{6,3},{7,2},{8,13},{9,12},{10,... | collective-permute-start | bytes 98312 | tf_op jit(solution)/shard_map/ppermute | solution.py:330
  35.9 4.2 %collective-permute-start.10 = (bf16[2,4,2048]{2,1,0:T(4,128)(2,1)S(1)}, bf16[2,4,2048]{2,1,0:T(4,128)(2,1)S(1)}, u32[]{:S(2)}, u32[]{:S(2)}) collective-permute-start(bf16[2,4,2048]{2,1,0:T(4,128)(2,1)S(1)} %pad_maximum_fusion.refs_0_), channel_id=1, source_target_pairs={{0,7},{1,6},{2,5},{3,4},{4,3},{5,2},{6,1},{7,0},{8,15},{9,14},{10,... | collective-permute-start | bytes 98312 | tf_op jit(solution)/shard_map/ppermute | solution.py:330
  37.8 3.0 %collective-permute-start.8 = (bf16[2,4,2048]{2,1,0:T(4,128)(2,1)S(1)}, bf16[2,4,2048]{2,1,0:T(4,128)(2,1)S(1)}, u32[]{:S(2)}, u32[]{:S(2)}) collective-permute-start(bf16[2,4,2048]{2,1,0:T(4,128)(2,1)S(1)} %pad_maximum_fusion.refs_0_), channel_id=1, source_target_pairs={{0,1},{1,0},{2,3},{3,2},{4,5},{5,4},{6,7},{7,6},{8,9},{9,8},{10,11... | collective-permute-start | bytes 98312 | tf_op jit(solution)/shard_map/ppermute | solution.py:330
  38.9 1.9 %collective-permute-start.9 = (bf16[2,4,2048]{2,1,0:T(4,128)(2,1)S(1)}, bf16[2,4,2048]{2,1,0:T(4,128)(2,1)S(1)}, u32[]{:S(2)}, u32[]{:S(2)}) collective-permute-start(bf16[2,4,2048]{2,1,0:T(4,128)(2,1)S(1)} %collective-permute-done.7.refs_1_), channel_id=1, source_target_pairs={{0,1},{1,0},{2,3},{3,2},{4,5},{5,4},{6,7},{7,6},{8,9},{9,8},{10,11... | collective-permute-start | bytes 98312 | tf_op jit(solution)/shard_map/ppermute | solution.py:330
  39.3 3.1 %collective-permute-start.13 = (bf16[2,4,2048]{2,1,0:T(4,128)(2,1)S(1)}, bf16[2,4,2048]{2,1,0:T(4,128)(2,1)S(1)}, u32[]{:S(2)}, u32[]{:S(2)}) collective-permute-start(bf16[2,4,2048]{2,1,0:T(4,128)(2,1)S(1)} %collective-permute-done.11.refs_1_), channel_id=1, source_target_pairs={{0,1},{1,0},{2,3},{3,2},{4,5},{5,4},{6,7},{7,6},{8,9},{9,8},{10,11... | collective-permute-start | bytes 98312 | tf_op jit(solution)/shard_map/ppermute | solution.py:330
  40.1 2.3 %collective-permute-start.12 = (bf16[2,4,2048]{2,1,0:T(4,128)(2,1)S(1)}, bf16[2,4,2048]{2,1,0:T(4,128)(2,1)S(1)}, u32[]{:S(2)}, u32[]{:S(2)}) collective-permute-start(bf16[2,4,2048]{2,1,0:T(4,128)(2,1)S(1)} %collective-permute-done.10.refs_0_), channel_id=1, source_target_pairs={{0,1},{1,0},{2,3},{3,2},{4,5},{5,4},{6,7},{7,6},{8,9},{9,8},{10,11... | collective-permute-start | bytes 98312 | tf_op jit(solution)/shard_map/ppermute | solution.py:330
